TPU v7x, 128 devices: a whole 4x4x4 slice. The times are simulated.
128 devices in a mesh: dp: 8 (over z_hi, y), tp: 16 (over z_lo, x, core).
Axes of the slice: x: 4, y: 4, z: 4 (z_hi: 2, z_lo: 2; z = z_hi * 2 + z_lo), core: 2. Of those that a mesh axis runs over, the one named last changes fastest.
Arguments:
- request_latent_cache: bfloat16 [2048, 192, 576], P(('dp', 'tp')), may hold values from -6 to 6
- lengths: int32 [2048], P(('dp', 'tp')), may hold values from 64 to 192, as said below
- queries: bfloat16 [2048, 2, 128, 576], P(('dp', 'tp')), may hold values from -6 to 6
- incoming_keys: bfloat16 [2048, 2, 576], P(('dp', 'tp')), may hold values from -6 to 6
- hidden_in: bfloat16 [2048, 2, 3584], P(('dp', 'tp')), may hold values from -4 to 4
- value_up_weight: bfloat16 [128, 512, 128], P('tp'), may hold values from -0.25 to 0.25
- w_out: bfloat16 [16384, 3584], P('tp'), may hold values from -0.375 to 0.375
- norm_gain: float32 [3584], replicated, may hold values from 0.25 to 1.75
- w_gate: bfloat16 [3584, 10240], P(None, 'tp'), may hold values from -0.09375 to 0.09375
- w_up: bfloat16 [3584, 10240], P(None, 'tp'), may hold values from -0.09375 to 0.09375
- w_down: bfloat16 [10240, 3584], P('tp'), may hold values from -0.15625 to 0.15625
- partner: int32 [8, 16], P(None, 'tp'), may hold values from 0 to 7, as said below
- moved_request: int32 [128], P(('dp', 'tp')), may hold values from 0 to 15
- moved_pages: int32 [128], P(('dp', 'tp')), may hold values from 1 to 2, as said below
Outputs:
- layer_out: bfloat16 [2048, 2, 3584], P(('dp', 'tp'))
- moved_cache: bfloat16 [256, 64, 576], P(('dp', 'tp'))
Inputs may be any that keep to these rules, and one draw needn't show every extreme that they name: `lengths`: some request holds 192 rows in every draw. For each tp index t, partner[d, t] = d XOR c[t] for one c[t] of 1 to 7, so partner[partner[d, t], t] = d. `moved_pages`: device 0 hands over 2 pages in every draw.
All inputs are finite; a program needn't handle non-finite values.
Results may differ from a plain program's by a relative error of at most 0.025.
Values may be sent and summed in bfloat16 or wider, within the bound.
No kernel may reach another device: no remote copies, remote signals or barrier semaphores. Data moves between devices by JAX's collectives and lax.ppermute only.
A program may use at most 128 MiB of HBM per device.

v0:
```python
import jax
import jax.numpy as jnp
from jax import lax
from jax.sharding import PartitionSpec as P

LATENT_WIDTH = 512
PAGE = 64
MIG_MAX = 2


score_scale = 192.0 ** (-0.5)
masked_score = -1e30
norm_eps = 1e-06


def attend_latent(block_cache, lens, query_rows, fresh_keys):
    capacity = block_cache.shape[1]
    steps_here = fresh_keys.shape[1]
    key_matrix = jnp.concatenate([block_cache, fresh_keys], axis=1)
    scores = (
        jnp.einsum("bshc,btc->bsht", query_rows, key_matrix, preferred_element_type=jnp.float32)
        * score_scale
    )
    positions = jnp.arange(capacity + steps_here, dtype=jnp.int32)
    step_ids = jnp.arange(steps_here, dtype=jnp.int32)
    visible = jnp.where(
        positions[None, None, :] < capacity,
        positions[None, None, :] < lens[:, None, None],
        positions[None, None, :] - capacity <= step_ids[None, :, None],
    )
    scores = jnp.where(visible[:, :, None, :], scores, masked_score)
    peak = jnp.max(scores, axis=-1, keepdims=True)
    weight_table = jnp.exp(scores - peak)
    probabilities = (weight_table / jnp.sum(weight_table, axis=-1, keepdims=True)).astype(
        jnp.bfloat16
    )
    latent_rows = jnp.einsum(
        "uaef,ufv->uaev",
        probabilities,
        key_matrix[..., :LATENT_WIDTH],
        preferred_element_type=jnp.float32,
    )
    return latent_rows.astype(jnp.bfloat16)


def norm_rows(residual, norm_gain):
    scale_rows = lax.rsqrt(jnp.mean(residual * residual, axis=-1, keepdims=True) + norm_eps)
    return (residual * scale_rows * norm_gain).astype(jnp.bfloat16)


def local(
    request_latent_cache,
    lengths,
    queries,
    incoming_keys,
    hidden_in,
    value_up_weight,
    w_out,
    norm_gain,
    w_gate,
    w_up,
    w_down,
    partner,
    moved_request,
    moved_pages,
):
    req_here, steps_here, width = hidden_in.shape
    row_list = req_here * steps_here
    every_head = queries.shape[2]
    latent_output = attend_latent(request_latent_cache, lengths, queries, incoming_keys).reshape(
        row_list, every_head, LATENT_WIDTH
    )
    exchanged = lax.all_to_all(latent_output, "tp", split_axis=1, concat_axis=0, tiled=True)
    values = jnp.einsum(
        "nhc,hcv->nhv", exchanged, value_up_weight, preferred_element_type=jnp.float32
    ).astype(jnp.bfloat16)
    values = values.reshape(values.shape[0], -1)
    own_input = hidden_in.reshape(row_list, width).astype(jnp.float32)
    picked = values
    residual = own_input + lax.psum_scatter(
        jnp.dot(picked, w_out, preferred_element_type=jnp.float32).astype(jnp.bfloat16),
        "tp",
        scatter_dimension=0,
        tiled=True,
    ).astype(jnp.float32)
    piece = lax.all_gather(norm_rows(residual, norm_gain), "tp", axis=0, tiled=True)
    gate = jnp.dot(piece, w_gate, preferred_element_type=jnp.float32)
    up_part = jnp.dot(piece, w_up, preferred_element_type=jnp.float32)
    hidden = (jax.nn.silu(gate) * up_part).astype(jnp.bfloat16)
    picked = hidden
    layer_out = (
        residual
        + lax.psum_scatter(
            jnp.dot(picked, w_down, preferred_element_type=jnp.float32).astype(jnp.bfloat16),
            "tp",
            scatter_dimension=0,
            tiled=True,
        ).astype(jnp.float32)
    ).astype(jnp.bfloat16)
    chosen = lax.dynamic_index_in_dim(request_latent_cache, moved_request[0], 0, keepdims=False)
    block = chosen[: MIG_MAX * PAGE].reshape(MIG_MAX, PAGE, chosen.shape[-1])
    keep = jnp.arange(MIG_MAX, dtype=jnp.int32) < moved_pages[0]
    block = jnp.where(keep[:, None, None], block, jnp.zeros_like(block))
    dp_index = lax.axis_index("dp")
    matched = partner[dp_index, 0]
    everyone = lax.all_gather(block[None], "dp", axis=0, tiled=True)
    block = lax.dynamic_index_in_dim(everyone, matched, 0, keepdims=False)
    return (layer_out.reshape(req_here, steps_here, width), block)


def solution(mesh):
    in_specs = (
        P(("dp", "tp"), None, None),
        P(("dp", "tp")),
        P(("dp", "tp"), None, None, None),
        P(("dp", "tp"), None, None),
        P(("dp", "tp"), None, None),
        P("tp", None, None),
        P("tp", None),
        P(),
        P(None, "tp"),
        P(None, "tp"),
        P("tp", None),
        P(None, "tp"),
        P(("dp", "tp")),
        P(("dp", "tp")),
    )
    out_specs = (P(("dp", "tp"), None, None), P(("dp", "tp"), None, None))
    return jax.shard_map(local, mesh=mesh, in_specs=in_specs, out_specs=out_specs, check_vma=False)
```

profile of v0, /device:TPU:0, one launch (start us, length us, event | category | flops | bytes accessed | tf_op | source)
XLA Modules:
  0.0 316.4 jit_solution(7679821054975244223)
XLA Ops:
  7.2 0.0 copy-start
  7.2 0.0 reduce-scatter.3.cloned.1.call-start
  7.2 0.0 copy-start.7
  7.3 0.0 copy-start.5
  7.3 0.0 copy-start.2
  7.3 2.6 constant_dynamic-update-slice_fusion.1
  9.9 0.0 copy-done.7
  9.9 0.1 iota_compare_fusion
  10.0 0.1 constant_dynamic-update-slice_fusion
  10.1 0.8 copy-done.2
  10.9 1.5 fusion.1
  12.5 5.0 %fusion.14 = (f32[16,2,128]{2,1,0:T(2,128)S(1)}, f32[16,2,128,194]{2,3,1,0:T(8,128)S(1)}) fusion(f32[16,194,2,128]{3,1,2,0:T(8,128)S(1)} %fusion.1, pred[16,2,194]{2,1,0:T(4,128)(4,1)S(1)} %broadcast_select_fusion.1), kind=kOutput, calls=%fused_computation.39 | output fusion | flops 4767937 | bytes 6379584 | tf_op jit(solution)/shard_map/sub | solution.py:33
  17.5 1.4 fusion.4
  18.9 2.3 copy.18
  21.2 0.0 slice-start
  21.2 56.1 %all_to_all.18 = bf16[32,128,512]{2,0,1:T(8,128)(2,1)S(1)} all-to-all(bf16[32,128,512]{2,0,1:T(8,128)(2,1)S(1)} %copy.18), channel_id=1, replica_groups=mesh['dp'=8,'tp'=16] {'tp'}, dimensions={1} | all-to-all | bytes 8388608 | tf_op jit(solution)/shard_map/all_to_all | solution.py:73
  77.3 0.6 copy.19
  77.9 0.0 copy-done
  77.9 1.5 convolution_convert_fusion.2
  79.4 0.0 slice-done
  79.4 0.0 slice-done.1
  79.4 5.5 %convolution_convert_fusion.1 = bf16[512,3584]{1,0:T(8,128)(2,1)} fusion(bf16[512,1024]{0,1:T(8,128)(2,1)S(1)} %bitcast.54, bf16[1024,3584]{1,0:T(8,128)(2,1)S(1)} %bitcast.57), kind=kOutput, calls=%fused_computation.2 | convolution fusion | flops 3759931392 | bytes 12058624 | tf_op jit(solution)/shard_map/dot_general | solution.py:81
  85.0 0.0 reduce-scatter.3.cloned.1.call-update
  85.0 0.0 all-gather.3.cloned.1.call-start
  85.1 0.9 copy-done.4
  85.9 0.1 reshape.106
  86.0 64.6 %reduce-scatter.3.cloned.1.call-done = bf16[32,3584]{1,0:T(8,128)(2,1)} async-done(((bf16[512,3584]{1,0:T(8,128)(2,1)}), bf16[32,3584]{1,0:T(8,128)(2,1)}) %reduce-scatter.3.cloned.1.call-update) | async-done | bytes 229392 | tf_op jit(solution)/shard_map/reduce_scatter | solution.py:80
  150.6 1.1 multiply_reduce_fusion
  151.7 0.0 copy-done.6
  151.7 1.7 multiply_convert_fusion
  153.4 0.0 all-gather.3.cloned.1.call-update
  153.4 0.0 all-gather.5.cloned.1.call-start
  154.8 0.9 constant_dynamic-slice_fusion.1
  155.7 0.8 broadcast_select_fusion
  156.5 0.0 all-gather.5.cloned.1.call-update
  156.5 0.2 reduce-scatter.5.cloned.1.call-start
  156.8 32.1 %all-gather.3.cloned.1.call-done = bf16[512,3584]{1,0:T(8,128)(2,1)} async-done(((bf16[32,3584]{1,0:T(8,128)(2,1)}), bf16[512,3584]{1,0:T(8,128)(2,1)}) %all-gather.3.cloned.1.call-update) | async-done | bytes 3670032 | tf_op jit(solution)/shard_map/all_gather | solution.py:86
  188.9 6.4 %fusion.15 = f32[512,640]{1,0:T(8,128)S(1)} fusion(bf16[512,3584]{1,0:T(8,128)(2,1)} %all-gather.3.cloned.1.call-done, bf16[3584,640]{1,0:T(8,128)(2,1)} %param.22), kind=kOutput, calls=%fused_computation.40 | convolution fusion | flops 2348810240 | bytes 9568256 | tf_op jit(solution)/shard_map/dot_general | solution.py:87
  195.3 0.0 copy-start.1
  195.3 13.8 %convolution_convert_fusion = bf16[512,3584]{1,0:T(8,128)(2,1)} fusion(bf16[640,3584]{1,0:T(8,128)(2,1)} %param.24, bf16[512,3584]{1,0:T(8,128)(2,1)} %all-gather.3.cloned.1.call-done, bf16[3584,640]{1,0:T(8,128)(2,1)} %param.23, f32[512,640]{1,0:T(8,128)S(1)} %fusion.15), kind=kOutput, calls=%fused_computation.1 | convolution fusion | flops 4701421568 | bytes 17825792 | tf_op jit(solution)/shard_map/dot_general | solution.py:94
  209.2 0.0 reduce-scatter.5.cloned.1.call-update
  209.2 0.6 copy-done.8
  209.8 0.6 constant_dynamic-slice_fusion
  212.3 29.0 %all-gather.5.cloned.1.call-done = bf16[8,2,64,576]{3,2,1,0:T(8,128)(2,1)} async-done(((bf16[1,2,64,576]{3,2,1,0:T(8,128)(2,1)}), bf16[8,2,64,576]{3,2,1,0:T(8,128)(2,1)}) %all-gather.5.cloned.1.call-update) | async-done | bytes 1179664 | tf_op jit(solution)/shard_map/all_gather | solution.py:106
  241.4 1.6 dynamic-slice_bitcast_fusion
  243.0 65.1 %reduce-scatter.5.cloned.1.call-done = bf16[32,3584]{1,0:T(8,128)(2,1)} async-done(((bf16[512,3584]{1,0:T(8,128)(2,1)}), bf16[32,3584]{1,0:T(8,128)(2,1)}) %reduce-scatter.5.cloned.1.call-update) | async-done | bytes 229392 | tf_op jit(solution)/shard_map/reduce_scatter | solution.py:93
  308.0 1.0 add_convert_fusion
  309.0 0.8 reshape.104
  (15 shorter events, 0.1 us)
Async XLA Ops:
  7.2 70.7 %copy-start = (bf16[8,512,128]{2,1,0:T(8,128)(2,1)S(1)}, bf16[8,512,128]{2,1,0:T(8,128)(2,1)}, u32[]{:S(2)}) copy-start(bf16[8,512,128]{2,1,0:T(8,128)(2,1)} %param.19) | copy-start | bytes 3145732
  7.2 143.4 %reduce-scatter.3.cloned.1.call-start = ((), (), s32[]{:S(2)}) async-start(), calls=%async_computation.3 | async-start | bytes 3899392 | tf_op jit(solution)/shard_map/reduce_scatter | solution.py:80
  7.2 2.7 copy-start.7
  7.3 2.7 copy-start.5
  7.3 3.6 %copy-start.2 = (bf16[16,2,128,576]{2,3,1,0:T(8,128)(2,1)S(1)}, bf16[16,2,128,576]{2,3,1,0:T(8,128)(2,1)}, u32[]{:S(2)}) copy-start(bf16[16,2,128,576]{2,3,1,0:T(8,128)(2,1)} %param.16) | copy-start | bytes 14155780
  21.2 58.2 %slice-start = ((s8[7340032]{0:T(1024)(128)(4,1)}), s8[4194304]{0:T(1024)(128)(4,1)S(1)}, s32[]{:S(2)}) async-start(s8[7340032]{0:T(1024)(128)(4,1)} %bitcast.56), calls=%async_computation.7 | async-start | bytes 8388608
  77.3 2.1 slice-start.1
  85.0 0.9 copy-start.4
  85.0 66.7 %copy-start.6 = (f32[3584]{0:T(1024)S(1)}, f32[3584]{0:T(1024)}, u32[]{:S(2)}) copy-start(f32[3584]{0:T(1024)} %param.21) | copy-start | bytes 43012
  85.0 103.9 %all-gather.3.cloned.1.call-start = ((), (), s32[]{:S(2)}) async-start(), calls=%async_computation.4 | async-start | bytes 3899392 | tf_op jit(solution)/shard_map/all_gather | solution.py:86
  153.4 87.9 %all-gather.5.cloned.1.call-start = ((), (), s32[]{:S(2)}) async-start(), calls=%async_computation.6 | async-start | bytes 1474560 | tf_op jit(solution)/shard_map/all_gather | solution.py:106
  156.5 151.5 %reduce-scatter.5.cloned.1.call-start = ((), (), s32[]{:S(2)}) async-start(), calls=%async_computation.5 | async-start | bytes 3899392 | tf_op jit(solution)/shard_map/reduce_scatter | solution.py:93
  195.3 114.5 %copy-start.1 = (bf16[8,512,128]{2,1,0:T(8,128)(2,1)S(1)}, bf16[8,512,128]{2,1,0:T(8,128)(2,1)}, u32[]{:S(2)}) copy-start(bf16[8,512,128]{2,1,0:T(8,128)(2,1)} %param.19) | copy-start | bytes 3145732
  209.2 0.7 copy-start.8
  209.2 98.9 %copy-start.3 = (bf16[32,3584]{1,0:T(8,128)(2,1)S(1)}, bf16[32,3584]{1,0:T(8,128)(2,1)}, u32[]{:S(2)}) copy-start(bf16[32,3584]{1,0:T(8,128)(2,1)} %reduce-scatter.3.cloned.1.call-done) | copy-start | bytes 688132
Sparse Core Ops, SparseCore 0:
  85.1 65.3 reduce-scatter.2
  153.6 35.2 all-gather.2
  191.8 49.5 all-gather.4
  243.6 64.3 reduce-scatter.4
where the time goes:
time: 317 us; the launch traced here: 316 us
  waiting for transfers between devices  191 us (60%)
  blocking collectives  56.1 us (18%)
  matrix products  30.2 us (10%)
  between operations  17.2 us (5%)
  local copies, waits for them, and re-layouts  11.9 us (4%)
  other arithmetic  9.73 us (3%)
    reduce_scatter x1, waiting for transfers between devices, local(): lax.psum_scatter(jnp.dot(picked, w_down, preferred_element_type=jnp.float...  65.1 us
    reduce_scatter x1, waiting for transfers between devices, local(): lax.psum_scatter(jnp.dot(picked, w_out, preferred_element_type=jnp.float3...  64.6 us
    all_to_all x1, blocking collectives, local(): lax.all_to_all(latent_output, 'tp', split_axis=1, concat_axis=0, tiled=True)  56.1 us
    all_gather x1, waiting for transfers between devices, local(): lax.all_gather(norm_rows(residual, norm_gain), 'tp', axis=0, tiled=True)  32.1 us
    all_gather x1, waiting for transfers between devices, local(): everyone = lax.all_gather(block[None], 'dp', axis=0, tiled=True)  29 us
    dot_general x1, matrix products, local(): jnp.dot(picked, w_down, preferred_element_type=jnp.float32)  13.8 us
    dot_general x1, matrix products, local(): gate = jnp.dot(piece, w_gate, preferred_element_type=jnp.float32)  6.42 us
  transfers between devices with their start and end apart: 4, of which 4 were waited for; matrix products, arithmetic and copies ran while one was open for 8% of the time, Pallas kernels for 0%

commit v1 on v0

v1 whole, which is shorter than its diff:
```python
import functools

import jax
import jax.numpy as jnp
from jax import lax
from jax.experimental import pallas as pl
from jax.experimental.pallas import tpu as pltpu
from jax.sharding import PartitionSpec as P

LATENT_WIDTH = 512
PAGE = 64
MIG_MAX = 2
N_X = 4
N_Z = 4
N_Y = 4
GRID = ("dp", "tp")
T_PAD = 208
GROUP = 4

score_scale = 192.0 ** (-0.5)
masked_score = -1e30
norm_eps = 1e-06


def place(index):
    d, t = index // 16, index % 16
    return (d // 4) * 2 + t // 8, d % 4, (t // 2) % 4, t % 2


def index_of(z, y, x, c):
    z, y, x = z % N_Z, y % N_Y, x % N_X
    return ((z // 2) * 4 + y) * 16 + (z % 2) * 8 + x * 2 + c


def shift(value, dx=0, dz=0):
    pairs = []
    for i in range(128):
        z, y, x, c = place(i)
        pairs.append((i, index_of(z + dz, y, x + dx, c)))
    return lax.ppermute(value, GRID, pairs)


def swap_cores(value):
    return lax.ppermute(value, "tp", [(t, t ^ 1) for t in range(16)])


def attend_kernel(where_ref, lens_ref, q_ref, cache_ref, fresh_ref, *rest, first_request):
    *outs, keys, rows = rest
    i = pl.program_id(0)
    reqs, steps, width, heads = q_ref.shape
    capacity = cache_ref.shape[1]
    total = keys.shape[1]

    @pl.when(i == 0)
    def _():
        keys[...] = jnp.zeros_like(keys)

    position = lax.broadcasted_iota(jnp.int32, (total, steps * heads), 0)
    column = lax.broadcasted_iota(jnp.int32, (total, steps * heads), 1)
    fresh_ok = (position >= capacity) & (position - capacity <= column // heads)
    z, x, c = where_ref[0], where_ref[1], where_ref[2]
    group = keys.shape[0]
    for first in range(0, reqs, group):
        scores, probs = [], []
        for g in range(group):
            r = first + g
            keys[g, 0:capacity, :] = cache_ref[r]
            keys[g, capacity : capacity + steps, :] = fresh_ref[r]
            q = jnp.concatenate([q_ref[r, s] for s in range(steps)], axis=1)
            scores.append(jnp.dot(keys[g], q, preferred_element_type=jnp.float32))
        for g in range(group):
            visible = (position < lens_ref[first_request + i * reqs + first + g]) | fresh_ok
            masked = jnp.where(visible, scores[g] * score_scale, masked_score)
            peak = jnp.max(masked, axis=0, keepdims=True)
            weight = jnp.exp(masked - peak)
            inverse = 1.0 / jnp.sum(weight, axis=0, keepdims=True)
            probs.append((weight * inverse).astype(jnp.bfloat16))
        for g in range(group):
            latent = lax.dot_general(
                probs[g],
                keys[g, :, :LATENT_WIDTH],
                (((0,), (0,)), ((), ())),
                preferred_element_type=jnp.float32,
            )
            rows[g] = latent
        for g in range(group):
            at = (i * reqs + first + g) * steps
            for side in range(2):
                zz = z if side == 0 else 1 - z
                for rel in range(N_X):
                    out = outs[side * N_X + rel]
                    chip = zz * 64 + lax.rem(x + rel, N_X) * 16
                    for s in range(steps):
                        picked = [
                            rows[g, pl.ds(pl.multiple_of(s * heads + chip + core * 8, 8), 8), :]
                            for core in (c, 1 - c)
                        ]
                        out[at + s] = jnp.concatenate(picked, axis=0).astype(jnp.bfloat16)


def attend(where, lengths, queries, cache, fresh, first, count):
    reqs, steps, width, heads = queries.shape
    capacity = cache.shape[1]
    part = 4
    n = count * steps
    base = first // part
    return pl.pallas_call(
        functools.partial(attend_kernel, first_request=first),
        grid_spec=pltpu.PrefetchScalarGridSpec(
            num_scalar_prefetch=2,
            grid=(count // part,),
            in_specs=[
                pl.BlockSpec((part, steps, width, heads), lambda i, w, l: (base + i, 0, 0, 0)),
                pl.BlockSpec((part, capacity, width), lambda i, w, l: (base + i, 0, 0)),
                pl.BlockSpec((part, steps, width), lambda i, w, l: (base + i, 0, 0)),
            ],
            out_specs=[pl.BlockSpec((n, 16, LATENT_WIDTH), lambda i, w, l: (0, 0, 0))] * (2 * N_X),
            scratch_shapes=[
                pltpu.VMEM((GROUP, T_PAD, width), jnp.bfloat16),
                pltpu.VMEM((GROUP, steps * heads, LATENT_WIDTH), jnp.float32),
            ],
        ),
        out_shape=[jax.ShapeDtypeStruct((n, 16, LATENT_WIDTH), jnp.bfloat16)] * (2 * N_X),
        compiler_params=pltpu.CompilerParams(vmem_limit_bytes=60 * 1024 * 1024),
        cost_estimate=pl.CostEstimate(
            flops=2 * n * heads * 256 * (width + LATENT_WIDTH),
            bytes_accessed=count * 800_000,
            transcendentals=n * heads * 256,
        ),
        name="attend",
    )(where, lengths, queries, cache, fresh)


def vmem_out(shape, dtype=jnp.bfloat16):
    return pltpu.VMEM(shape, dtype)


HBM_SPEC = pl.BlockSpec(memory_space=pltpu.HBM)
VMEM_SPEC = pl.BlockSpec(memory_space=pltpu.VMEM)


def run_copies(copies):
    for copy in copies:
        copy.start()
    for copy in copies:
        copy.wait()


def hold_projection_kernel(up_own, up_other, out_own, out_other, up_ref, out_ref, sems):
    half = out_own.shape[0]
    pairs = [
        (up_own, up_ref.at[0:8]),
        (up_other, up_ref.at[8:16]),
        (out_own, out_ref.at[0:half]),
        (out_other, out_ref.at[half : 2 * half]),
    ]
    run_copies([pltpu.make_async_copy(a, b, sems.at[i]) for i, (a, b) in enumerate(pairs)])


def hold_projection(up_own, up_other, out_own, out_other):
    return pl.pallas_call(
        hold_projection_kernel,
        in_specs=[HBM_SPEC] * 4,
        out_specs=[VMEM_SPEC] * 2,
        out_shape=[
            vmem_out((16,) + up_own.shape[1:]),
            vmem_out((2 * out_own.shape[0], out_own.shape[1])),
        ],
        scratch_shapes=[pltpu.SemaphoreType.DMA((4,))],
        cost_estimate=pl.CostEstimate(flops=0, bytes_accessed=17_000_000, transcendentals=0),
        compiler_params=pltpu.CompilerParams(vmem_limit_bytes=16 * 1024 * 1024),
        name="hold_projection",
    )(up_own, up_other, out_own, out_other)


def hold_feed_kernel(g0, g1, u0, u1, d0, d1, own_ref, other_ref, down_ref, sems):
    units = g0.shape[1]
    pairs = []
    for side, (g, u, d) in enumerate(((g0, u0, d0), (g1, u1, d1))):
        mix = (own_ref, other_ref)[side]
        for j in range(units // 128):
            cols = slice(j * 128, (j + 1) * 128)
            pairs.append((g.at[:, cols], mix.at[j, :, 0:128]))
            pairs.append((u.at[:, cols], mix.at[j, :, 128:256]))
        pairs.append((d, down_ref.at[side * units : (side + 1) * units]))
    run_copies([pltpu.make_async_copy(a, b, sems.at[i]) for i, (a, b) in enumerate(pairs)])


def hold_feed(g0, g1, u0, u1, d0, d1):
    width, units = g0.shape
    tiles = units // 128
    return pl.pallas_call(
        hold_feed_kernel,
        in_specs=[HBM_SPEC] * 6,
        out_specs=[VMEM_SPEC] * 3,
        out_shape=[vmem_out((tiles, width, 256))] * 2 + [vmem_out((2 * units, width))],
        scratch_shapes=[pltpu.SemaphoreType.DMA((4 * tiles + 2,))],
        cost_estimate=pl.CostEstimate(flops=0, bytes_accessed=27_500_000, transcendentals=0),
        compiler_params=pltpu.CompilerParams(vmem_limit_bytes=16 * 1024 * 1024),
        name="hold_feed",
    )(g0, g1, u0, u1, d0, d1)


def values_kernel(*refs, blocks):
    lat, up_ref, out_ref, turned = refs[:blocks], refs[blocks], refs[blocks + 1], refs[blocks + 2]
    heads, depth, wide = up_ref.shape
    n = lat[0].shape[0]
    for i, ref in enumerate(lat):

        @pl.loop(0, n)
        def _(r):
            row = ref[r].astype(jnp.float32)
            at = pl.multiple_of(i * n * heads + r * heads, heads)
            for lane in range(depth // 128):
                turned[lane, pl.ds(at, heads), :] = row[:, lane * 128 : (lane + 1) * 128]

    for h in range(heads):
        rows = jnp.concatenate(
            [turned[lane, pl.ds(h, blocks * n, stride=heads), :] for lane in range(depth // 128)],
            axis=1,
        ).astype(jnp.bfloat16)
        part = jnp.dot(rows, up_ref[h], preferred_element_type=jnp.float32)
        out_ref[:, h * wide : (h + 1) * wide] = part.astype(jnp.bfloat16)


def values_of(blocks, up):
    n, heads, depth = blocks[0].shape
    rows = n * len(blocks)
    wide = up.shape[2]
    return pl.pallas_call(
        functools.partial(values_kernel, blocks=len(blocks)),
        in_specs=[VMEM_SPEC] * (len(blocks) + 1),
        out_specs=VMEM_SPEC,
        out_shape=jax.ShapeDtypeStruct((rows, heads * wide), jnp.bfloat16),
        scratch_shapes=[pltpu.VMEM((depth // 128, rows * heads, 128), jnp.float32)],
        compiler_params=pltpu.CompilerParams(vmem_limit_bytes=16 * 1024 * 1024),
        cost_estimate=pl.CostEstimate(
            flops=2 * rows * heads * depth * wide, bytes_accessed=4_000_000, transcendentals=0
        ),
        name="values",
    )(*blocks, up)


def write_rows(part, outs, cols):
    at = 0
    for out in outs:
        size = out.shape[0]
        out[:, cols] = part[at : at + size].astype(out.dtype)
        at += size


def project_kernel(*refs, parts):
    count = len(parts)
    given, w_ref, outs, values = refs[:count], refs[count], refs[count + 1 : -1], refs[-1]
    at = 0
    for ref, (first, size) in zip(given, parts):
        values[at : at + size, :] = ref[first : first + size, :]
        at += size
    tile = 512

    @pl.loop(0, w_ref.shape[1] // tile)
    def _(j):
        cols = pl.ds(pl.multiple_of(j * tile, tile), tile)
        write_rows(
            jnp.dot(values[...], w_ref[:, cols], preferred_element_type=jnp.float32), outs, cols
        )


def project(values, out, shapes):
    parts = [(first, size) for _, first, size in values]
    rows = sum(size for _, size in parts)
    depth, width = out.shape
    return pl.pallas_call(
        functools.partial(project_kernel, parts=parts),
        in_specs=[VMEM_SPEC] * (len(values) + 1),
        out_specs=[VMEM_SPEC] * len(shapes),
        out_shape=[jax.ShapeDtypeStruct((r, width), d) for r, d in shapes],
        scratch_shapes=[pltpu.VMEM((rows, depth), jnp.bfloat16)],
        compiler_params=pltpu.CompilerParams(vmem_limit_bytes=16 * 1024 * 1024),
        cost_estimate=pl.CostEstimate(
            flops=2 * rows * depth * width, bytes_accessed=17_000_000, transcendentals=0
        ),
        name="project",
    )(*[v for v, _, _ in values], out)


def feed_kernel(*refs, blocks):
    given, mixes, down_ref = refs[:blocks], refs[blocks : blocks + 2], refs[blocks + 2]
    *outs, rows, hidden = refs[blocks + 3 :]
    at = 0
    for b in given:
        rows[at : at + b.shape[0], :] = b[...]
        at += b.shape[0]
    tiles = mixes[0].shape[0]
    for side, mix in enumerate(mixes):

        @pl.loop(0, tiles)
        def _(j):
            both = jnp.dot(rows[...], mix[j], preferred_element_type=jnp.float32)
            gate, up_part = both[:, :128], both[:, 128:]
            value = gate / (1.0 + jnp.exp(-gate)) * up_part
            at = pl.multiple_of((side * tiles + j) * 128, 128)
            hidden[:, pl.ds(at, 128)] = value.astype(jnp.bfloat16)

    tile = 512

    @pl.loop(0, down_ref.shape[1] // tile)
    def _(j):
        cols = pl.ds(pl.multiple_of(j * tile, tile), tile)
        write_rows(
            jnp.dot(hidden[...], down_ref[:, cols], preferred_element_type=jnp.float32), outs, cols
        )


def feed(blocks, held, shapes):
    rows = sum(b.shape[0] for b in blocks)
    units, width = held[2].shape
    return pl.pallas_call(
        functools.partial(feed_kernel, blocks=len(blocks)),
        in_specs=[VMEM_SPEC] * (len(blocks) + 3),
        out_specs=[VMEM_SPEC] * len(shapes),
        out_shape=[jax.ShapeDtypeStruct((r, width), d) for r, d in shapes],
        scratch_shapes=[
            pltpu.VMEM((rows, width), jnp.bfloat16),
            pltpu.VMEM((rows, units), jnp.bfloat16),
        ],
        compiler_params=pltpu.CompilerParams(vmem_limit_bytes=16 * 1024 * 1024),
        cost_estimate=pl.CostEstimate(
            flops=6 * rows * width * units, bytes_accessed=28_000_000, transcendentals=rows * units
        ),
        name="feed",
    )(*blocks, *held)


def after(value, *others):
    return lax.optimization_barrier((value,) + others)[0]


SMALL = pltpu.CompilerParams(vmem_limit_bytes=16 * 1024 * 1024)


def glue(kernel, name, args, shapes):
    return pl.pallas_call(
        kernel,
        in_specs=[VMEM_SPEC] * len(args),
        out_specs=[VMEM_SPEC] * len(shapes),
        out_shape=[jax.ShapeDtypeStruct(s, d) for s, d in shapes],
        compiler_params=SMALL,
        cost_estimate=pl.CostEstimate(flops=10_000, bytes_accessed=2_000_000, transcendentals=0),
        name=name,
    )(*args)


def flatten_kernel(hidden_ref, out_ref):
    steps = hidden_ref.shape[1]
    for r in range(hidden_ref.shape[0]):
        out_ref[r * steps : (r + 1) * steps, :] = hidden_ref[r].astype(jnp.float32)


def column_loop(width, body):
    tile = 512

    @pl.loop(0, width // tile)
    def _(j):
        body(pl.ds(pl.multiple_of(j * tile, tile), tile))


def fold_kernel(near_ref, back_ref, out_ref):
    def body(cols):
        total = near_ref[:, cols] + back_ref[:, cols].astype(jnp.float32)
        out_ref[:, cols] = total.astype(jnp.bfloat16)

    column_loop(near_ref.shape[1], body)


def fold(near, back):
    (out,) = glue(fold_kernel, "fold", (near, back), [(near.shape, jnp.bfloat16)])
    return out


def norm_kernel(hidden_ref, gain_ref, own_ref, *refs):
    *received, residual_ref, normed_ref, squares = refs
    width = own_ref.shape[1]
    squares[...] = jnp.zeros_like(squares)

    def add(cols):
        total = hidden_ref[:, cols] + own_ref[:, cols]
        for ref in received:
            total = total + ref[:, cols].astype(jnp.float32)
        residual_ref[:, cols] = total
        square = total * total
        for at in range(0, square.shape[1], 128):
            squares[...] += square[:, at : at + 128]

    column_loop(width, add)
    mean = jnp.sum(squares[...], axis=1, keepdims=True) / width
    scale = lax.rsqrt(mean + norm_eps)

    def write(cols):
        normed_ref[:, cols] = (residual_ref[:, cols] * scale * gain_ref[:, cols]).astype(jnp.bfloat16)

    column_loop(width, write)


def norm(own, received, hidden, gain):
    n, width = own.shape
    return pl.pallas_call(
        norm_kernel,
        in_specs=[VMEM_SPEC] * (3 + len(received)),
        out_specs=[VMEM_SPEC] * 2,
        out_shape=[
            jax.ShapeDtypeStruct((n, width), jnp.float32),
            jax.ShapeDtypeStruct((n, width), jnp.bfloat16),
        ],
        scratch_shapes=[pltpu.VMEM((n, 128), jnp.float32)],
        compiler_params=SMALL,
        cost_estimate=pl.CostEstimate(flops=10_000, bytes_accessed=2_000_000, transcendentals=0),
        name="norm",
    )(hidden, gain, own, *received)


def finish_kernel(residual_ref, own_ref, *refs):
    *received, out_ref = refs

    def body(cols):
        total = residual_ref[:, cols] + own_ref[:, cols]
        for ref in received:
            total = total + ref[:, cols].astype(jnp.float32)
        out_ref[:, cols] = total.astype(jnp.bfloat16)

    column_loop(own_ref.shape[1], body)


def page_kernel(ids_ref, partner_ref, request_ref, count_ref, cache_ref, block_ref, offset_ref):
    dp = ids_ref[3]
    offset_ref[0] = jnp.bitwise_xor(partner_ref[dp], dp)
    for k in range(MIG_MAX):
        rows = cache_ref[0, k * PAGE : (k + 1) * PAGE, :]
        block_ref[k] = jnp.where(k < count_ref[0], rows, jnp.zeros_like(rows))


def page_block(ids, partner, moved_request, moved_pages, cache):
    width = cache.shape[2]
    return pl.pallas_call(
        page_kernel,
        grid_spec=pltpu.PrefetchScalarGridSpec(
            num_scalar_prefetch=4,
            grid=(1,),
            in_specs=[pl.BlockSpec((1,) + cache.shape[1:], lambda i, ids, p, r, c: (r[0], 0, 0))],
            out_specs=[
                pl.BlockSpec((MIG_MAX, PAGE, width), lambda i, ids, p, r, c: (0, 0, 0)),
                pl.BlockSpec(memory_space=pltpu.SMEM),
            ],
        ),
        out_shape=[
            jax.ShapeDtypeStruct((MIG_MAX, PAGE, width), cache.dtype),
            jax.ShapeDtypeStruct((1,), jnp.int32),
        ],
        compiler_params=SMALL,
        cost_estimate=pl.CostEstimate(flops=1_000, bytes_accessed=400_000, transcendentals=0),
        name="pages",
    )(ids, partner.reshape(-1), moved_request, moved_pages, cache)


def pick_kernel(offset_ref, mine_ref, other_ref, out_ref, *, bit):
    trade = lax.rem(offset_ref[0] // (1 << bit), 2) == 1

    @pl.when(trade)
    def _():
        out_ref[...] = other_ref[...]

    @pl.when(jnp.logical_not(trade))
    def _():
        out_ref[...] = mine_ref[...]


def page_step(block, offset, bit):
    other = lax.ppermute(block, "dp", [(d, d ^ (1 << bit)) for d in range(8)])
    return pl.pallas_call(
        functools.partial(pick_kernel, bit=bit),
        in_specs=[pl.BlockSpec(memory_space=pltpu.SMEM), VMEM_SPEC, VMEM_SPEC],
        out_specs=VMEM_SPEC,
        out_shape=jax.ShapeDtypeStruct(block.shape, block.dtype),
        compiler_params=SMALL,
        cost_estimate=pl.CostEstimate(flops=1_000, bytes_accessed=400_000, transcendentals=0),
        name="pick",
    )(offset, block, other)


def local(
    request_latent_cache,
    lengths,
    queries,
    incoming_keys,
    hidden_in,
    value_up_weight,
    w_out,
    norm_gain,
    w_gate,
    w_up,
    w_down,
    partner,
    moved_request,
    moved_pages,
):
    req_here, steps_here, width = hidden_in.shape
    n = req_here * steps_here
    t = lax.axis_index("tp")
    where = jnp.stack([t // 8, (t // 2) % N_X, t % 2, lax.axis_index("dp")])
    up_other, out_other, gate_other = swap_cores(value_up_weight), swap_cores(w_out), swap_cores(w_gate)
    turned = jnp.swapaxes(queries, 2, 3)
    own0, own1, own2, own3, go0, go1, go2, go3 = attend(
        where, lengths, turned, request_latent_cache, incoming_keys, 0, req_here
    )
    near_shapes = [(n, jnp.float32), (n, jnp.float32), (n, jnp.bfloat16), (n, jnp.float32)]
    far_shapes = [(n, jnp.bfloat16)] * N_X

    go1, go3, own2 = after(go1, up_other), after(go3, up_other), after(own2, up_other)
    far_in1, far_in3 = shift(go1, dz=1), shift(go3, dz=-1)
    near2 = shift(own2, dx=2)
    first = (near2, far_in1, far_in3, out_other, gate_other)
    far1 = shift(after(far_in1, *first), dx=1)
    far3 = shift(after(far_in3, *first), dx=3)
    far_in2, far_in0 = shift(after(go2, *first), dz=-1), shift(after(go0, *first), dz=1)
    far2 = shift(far_in2, dx=2)
    near1 = shift(after(own1, far_in0, far_in2), dx=1)
    near3 = shift(after(own3, far_in0, far_in2), dx=3)
    up2, out2 = hold_projection(value_up_weight, up_other, w_out, out_other)
    second = (far_in0, far_in2, far1, far3)
    fup_other = swap_cores(after(w_up, *second))
    down_other = swap_cores(after(w_down, *second))
    block, offset = page_block(
        after(where, *first), partner, moved_request, moved_pages, request_latent_cache
    )
    (hidden32,) = glue(
        flatten_kernel, "flatten", (after(hidden_in, *first),), [((n, width), jnp.float32)]
    )
    gain = norm_gain.reshape(1, width)
    values_a = values_of([after(own0, near2), near2], up2)
    values_b = values_of([far_in0, far1], up2)
    values_c = values_of([far2, far3], up2)
    far = project(
        [(values_b, 0, 2 * n), (values_c, 0, 2 * n)], out2, far_shapes
    )
    back1, back3 = shift(far[1], dz=-1), shift(far[3], dz=1)
    aside, back0 = shift(far[2], dx=-2), shift(far[0], dz=-1)
    values_d = values_of([after(near1, far[0]), near3], up2)
    near = project(
        [(values_a, 0, n), (values_d, 0, n), (values_a, n, n), (values_d, n, n)], out2, near_shapes
    )
    home2 = shift(near[2], dx=-2)
    back2 = shift(aside, dz=1)
    fold1, fold3 = fold(near[1], back1), fold(near[3], back3)
    home1, home3 = shift(fold1, dx=-1), shift(fold3, dx=-3)
    held = hold_feed(after(w_gate, fold1, fold3), gate_other, w_up, fup_other, w_down, down_other)
    residual, normed = norm(
        near[0], [back0, back2, after(home1, held[0]), home2, home3], hidden32, gain
    )

    row1, row3 = shift(normed, dx=1), shift(normed, dx=3)
    over, under = shift(normed, dz=1), shift(normed, dz=-1)
    row2 = shift(normed, dx=2)
    far_row1, far_row3 = shift(row1, dz=1), shift(row3, dz=-1)
    far_row2 = shift(under, dx=2)
    block = page_step(after(block, normed), offset, 0)
    near = feed([normed, row1, row2, row3], held, near_shapes)
    home2 = shift(near[2], dx=-2)
    far = feed([after(over, near[0]), far_row1, far_row2, far_row3], held, far_shapes)
    back1, back3 = shift(far[1], dz=-1), shift(far[3], dz=1)
    aside, back0 = shift(far[2], dx=-2), shift(far[0], dz=-1)
    block = page_step(after(block, far[0]), offset, 1)
    fold1, fold3 = fold(near[1], back1), fold(near[3], back3)
    home1, home3 = shift(fold1, dx=-1), shift(fold3, dx=-3)
    back2 = shift(aside, dz=1)
    block = page_step(after(block, fold1), offset, 2)
    (out,) = glue(
        finish_kernel, "finish", (residual, near[0], back0, back2, home1, home2, home3),
        [((n, width), jnp.bfloat16)],
    )
    return out.reshape(req_here, steps_here, width), block


def solution(mesh):
    in_specs = (
        P(("dp", "tp"), None, None),
        P(("dp", "tp")),
        P(("dp", "tp"), None, None, None),
        P(("dp", "tp"), None, None),
        P(("dp", "tp"), None, None),
        P("tp", None, None),
        P("tp", None),
        P(),
        P(None, "tp"),
        P(None, "tp"),
        P("tp", None),
        P(None, "tp"),
        P(("dp", "tp")),
        P(("dp", "tp")),
    )
    out_specs = (P(("dp", "tp"), None, None), P(("dp", "tp"), None, None))
    return jax.shard_map(local, mesh=mesh, in_specs=in_specs, out_specs=out_specs, check_vma=False)
```

time: 317 us -> 165 us (0.52)
  waiting for transfers between devices: 191 us -> 47.2 us
  blocking collectives: 56.1 us -> 0 us
  starting transfers between devices: 0.35 us -> 53.7 us
  Pallas kernels: 0 us -> 52.1 us
  matrix products: 30.2 us -> 0 us
  between operations: 17.2 us -> 2.31 us
  other arithmetic: 9.73 us -> 0.64 us
    reduce_scatter x2 -> x0, waiting for transfers between devices: 130 us -> none  [the longest x1 65.1 us: local(): lax.psum_scatter(jnp.dot(picked, w_down, preferred_element_type=jnp.float...]
    all_gather x2 -> x0, waiting for transfers between devices: 61.2 us -> none  [the longest x1 32.1 us: local(): lax.all_gather(norm_rows(residual, norm_gain), 'tp', axis=0, tiled=True)]
    all_to_all x1 -> x0, blocking collectives: 56.1 us -> none  [local(): lax.all_to_all(latent_output, 'tp', split_axis=1, concat_axis=0, tiled=True)]
    ppermute x0 -> x42, starting transfers between devices: none -> 53.7 us  [the longest x34 47.6 us: shift(): return lax.ppermute(value, GRID, pairs)]
    pallas_call x0 -> x22, Pallas kernels: none -> 52.1 us  [the longest x2 13.5 us: feed(): pl.pallas_call(functools.partial(feed_kernel, blocks=len(blocks)), in_spe...]
    ppermute x0 -> x42, waiting for transfers between devices: none -> 47.2 us  [the longest x34 44.6 us: shift(): return lax.ppermute(value, GRID, pairs)]
    dot_general x6 -> x0, matrix products: 30.2 us -> none  [the longest x1 13.8 us: local(): jnp.dot(picked, w_down, preferred_element_type=jnp.float32)]
    sub x2 -> x0, other arithmetic: 4.99 us -> none  [the longest x1 4.99 us: attend_latent(): weight_table = jnp.exp(scores - peak)]
  transfers between devices with their start and end apart: 4 -> 42, of which waited for: 4 -> 15; matrix products, arithmetic and copies ran while one was open for 8% -> 0% of each run, Pallas kernels for 0% -> 31%
where the time goes in v1:
time: 165 us
  starting transfers between devices  53.7 us (33%)
  Pallas kernels  52.1 us (32%)
  waiting for transfers between devices  47.2 us (29%)
  local copies, waits for them, and re-layouts  8.76 us (5%)
  between operations  2.31 us (1%)
    ppermute x34, starting transfers between devices, shift(): return lax.ppermute(value, GRID, pairs)  47.6 us
    ppermute x34, waiting for transfers between devices, shift(): return lax.ppermute(value, GRID, pairs)  44.6 us
    pallas_call x2, Pallas kernels, feed(): pl.pallas_call(functools.partial(feed_kernel, blocks=len(blocks)), in_spe...  13.5 us
    pallas_call x1, Pallas kernels, attend(): pl.pallas_call(functools.partial(attend_kernel, first_request=first), gri...  9.07 us
    pallas_call x1, Pallas kernels, hold_feed(): pl.pallas_call(hold_feed_kernel, in_specs=[HBM_SPEC] * 6, out_specs=[VMEM...  8.48 us
    unnamed x22, local copies, waits for them, and re-layouts  7.97 us
    pallas_call x2, Pallas kernels, project(): pl.pallas_call(functools.partial(project_kernel, parts=parts), in_specs=[...  6.4 us
    pallas_call x4, Pallas kernels, values_of(): pl.pallas_call(functools.partial(values_kernel, blocks=len(blocks)), in_s...  6.11 us
  transfers between devices with their start and end apart: 42, of which 15 were waited for; matrix products, arithmetic and copies ran while one was open for 0% of the time, Pallas kernels for 31%

profile of v1, /device:TPU:0, one launch (start us, length us, event | category | flops | bytes accessed | tf_op | source)
XLA Modules:
  0.0 164.8 jit_solution(15457266991098740535)
XLA Ops:
  2.0 9.1 %attend.1 = (bf16[32,16,512]{2,1,0:T(8,128)(2,1)}, bf16[32,16,512]{2,1,0:T(8,128)(2,1)}, bf16[32,16,512]{2,1,0:T(8,128)(2,1)}, bf16[32,16,512]{2,1,0:T(8,128)(2,...) custom-call(s32[4]{0:T(128)} %pad_add_fusion.where_ref.ids_ref, ...), custom_call_target="tpu_custom_call" | custom-call | flops 2281701376 | bytes 12800000 | tf_op jit(solution)/shard_map/attend/pallas_call | solution.py:107
  11.0 4.1 %collective-permute-start.3 = (bf16[32,16,512]{2,1,0:T(8,128)(2,1)}, bf16[32,16,512]{2,1,0:T(8,128)(2,1)S(1)}, u32[]{:S(2)}, u32[]{:S(2)}) collective-permute-start(bf16[32,16,512]{2,1,0:T(8,128)(2,1)} %get-tuple-element.61), channel_id=1, source_target_pairs={{0,72},{1,73},{2,74},{3,75},{4,76},{5,77},{6,78},{7,79},{8,0},{9,1... | collective-permute-start | bytes 1572872 | tf_op jit(solution)/shard_map/ppermute | solution.py:40
  15.2 3.0 %collective-permute-start.1 = (bf16[32,16,512]{2,1,0:T(8,128)(2,1)}, bf16[32,16,512]{2,1,0:T(8,128)(2,1)S(1)}, u32[]{:S(2)}, u32[]{:S(2)}) collective-permute-start(bf16[32,16,512]{2,1,0:T(8,128)(2,1)} %get-tuple-element.57), channel_id=1, source_target_pairs={{0,4},{1,5},{2,6},{3,7},{4,0},{5,1},{6,2},{7,3},{8,12},{9,13},{10,... | collective-permute-start | bytes 1572872 | tf_op jit(solution)/shard_map/ppermute | solution.py:40
  18.2 9.1 %collective-permute-done.3 = bf16[32,16,512]{2,1,0:T(8,128)(2,1)S(1)} collective-permute-done((bf16[32,16,512]{2,1,0:T(8,128)(2,1)}, bf16[32,16,512]{2,1,0:T(8,128)(2,1)S(1)}, u32[]{:S(2)}, u32[]{:S(2)}) %collective-permute-start.3) | collective-permute-done | bytes 524320 | tf_op jit(solution)/shard_map/ppermute | solution.py:40
  27.3 3.3 %collective-permute-done.2 = bf16[32,16,512]{2,1,0:T(8,128)(2,1)S(1)} collective-permute-done((bf16[32,16,512]{2,1,0:T(8,128)(2,1)}, bf16[32,16,512]{2,1,0:T(8,128)(2,1)S(1)}, u32[]{:S(2)}, u32[]{:S(2)}) %collective-permute-start.2) | collective-permute-done | bytes 524320 | tf_op jit(solution)/shard_map/ppermute | solution.py:40
  30.9 3.2 %collective-permute-start.7 = (bf16[32,16,512]{2,1,0:T(8,128)(2,1)}, bf16[32,16,512]{2,1,0:T(8,128)(2,1)S(1)}, u32[]{:S(2)}, u32[]{:S(2)}) collective-permute-start(bf16[32,16,512]{2,1,0:T(8,128)(2,1)} %get-tuple-element.70), channel_id=1, source_target_pairs={{0,72},{1,73},{2,74},{3,75},{4,76},{5,77},{6,78},{7,79},{8,0},{9,1... | collective-permute-start | bytes 1572872 | tf_op jit(solution)/shard_map/ppermute | solution.py:40
  34.1 1.5 collective-permute-start.9
  35.6 1.8 %collective-permute-start.11 = (bf16[32,16,512]{2,1,0:T(8,128)(2,1)S(1)}, bf16[32,16,512]{2,1,0:T(8,128)(2,1)S(1)}, u32[]{:S(2)}, u32[]{:S(2)}) collective-permute-start(bf16[32,16,512]{2,1,0:T(8,128)(2,1)S(1)} %collective-permute-done.3), channel_id=1, source_target_pairs={{0,6},{1,7},{2,0},{3,1},{4,2},{5,3},{6,4},{7,5},{8,14},{9,15},{10,... | collective-permute-start | bytes 1572872 | tf_op jit(solution)/shard_map/ppermute | solution.py:40
  37.4 8.1 %collective-permute-done.6.refs_0_ = bf16[32,16,512]{2,1,0:T(8,128)(2,1)S(1)} collective-permute-done((bf16[32,16,512]{2,1,0:T(8,128)(2,1)}, bf16[32,16,512]{2,1,0:T(8,128)(2,1)S(1)}, u32[]{:S(2)}, u32[]{:S(2)}) %collective-permute-start.6) | collective-permute-done | bytes 524320 | tf_op jit(solution)/shard_map/ppermute | solution.py:40
  45.5 2.5 %collective-permute-done.9.refs_1_ = bf16[32,16,512]{2,1,0:T(8,128)(2,1)S(1)} collective-permute-done((bf16[32,16,512]{2,1,0:T(8,128)(2,1)S(1)}, bf16[32,16,512]{2,1,0:T(8,128)(2,1)S(1)}, u32[]{:S(2)}, u32[]{:S(2)}) %collective-permute-start.9) | collective-permute-done | bytes 524320 | tf_op jit(solution)/shard_map/ppermute | solution.py:40
  48.4 2.7 %collective-permute-start.10 = (bf16[32,16,512]{2,1,0:T(8,128)(2,1)S(1)}, bf16[32,16,512]{2,1,0:T(8,128)(2,1)S(1)}, u32[]{:S(2)}, u32[]{:S(2)}) collective-permute-start(bf16[32,16,512]{2,1,0:T(8,128)(2,1)S(1)} %collective-permute-done.7), channel_id=1, source_target_pairs={{0,4},{1,5},{2,6},{3,7},{4,0},{5,1},{6,2},{7,3},{8,12},{9,13},{10,... | collective-permute-start | bytes 1572872 | tf_op jit(solution)/shard_map/ppermute | solution.py:40
  51.2 1.1 collective-permute-start.8
  52.3 2.2 %collective-permute-start.12 = (bf16[32,16,512]{2,1,0:T(8,128)(2,1)}, bf16[32,16,512]{2,1,0:T(8,128)(2,1)S(1)}, u32[]{:S(2)}, u32[]{:S(2)}) collective-permute-start(bf16[32,16,512]{2,1,0:T(8,128)(2,1)} %get-tuple-element.78), channel_id=1, source_target_pairs={{0,6},{1,7},{2,0},{3,1},{4,2},{5,3},{6,4},{7,5},{8,14},{9,15},{10,... | collective-permute-start | bytes 1572872 | tf_op jit(solution)/shard_map/ppermute | solution.py:40
  54.4 3.1 %copy-done.1 = bf16[1024,3584]{1,0:T(8,128)(2,1)S(1)} copy-done((bf16[1024,3584]{1,0:T(8,128)(2,1)S(1)}, bf16[1024,3584]{1,0:T(8,128)(2,1)}, u32[]{:S(2)}) %copy-start.1) | copy-done | bytes 7340056
  57.5 3.7 %hold_projection.1 = (bf16[16,512,128]{2,1,0:T(8,128)(2,1)S(1)}, bf16[2048,3584]{1,0:T(8,128)(2,1)S(1)}) custom-call(bf16[8,512,128]{2,1,0:T(8,128)(2,1)S(1)} %copy-done.3, bf16[8,512,128]{2,1,0:T(8,128)(2,1)S(1)} %collective-permute-done.up_other, bf16[1024,3584]{1,0:T(8,128)(2,1)S(1)} %copy-done.1, bf16[1024,3584]{1,0:T(8,128)(2,1)} %collective-permute-done.4.out_other), custom_call_target="tpu_custom_call" | custom-call | bytes 17000000 | tf_op jit(solution)/shard_map/hold_projection/pallas_call | solution.py:161
  61.2 1.5 values.5.refs_0_
  62.8 2.0 %collective-permute-done.10.refs_0_ = bf16[32,16,512]{2,1,0:T(8,128)(2,1)S(1)} collective-permute-done((bf16[32,16,512]{2,1,0:T(8,128)(2,1)S(1)}, bf16[32,16,512]{2,1,0:T(8,128)(2,1)S(1)}, u32[]{:S(2)}, u32[]{:S(2)}) %collective-permute-start.10) | collective-permute-done | bytes 524320 | tf_op jit(solution)/shard_map/ppermute | solution.py:40
  64.8 1.5 values.6.refs_1_
  66.3 3.2 %project.2 = (bf16[32,3584]{1,0:T(8,128)(2,1)S(1)}, bf16[32,3584]{1,0:T(8,128)(2,1)S(1)}, bf16[32,3584]{1,0:T(8,128)(2,1)S(1)}, bf16[32,3584]{1,0:T(8,128)(2,1)S(1)}) custom-call(bf16[64,2048]{1,0:T(8,128)(2,1)S(1)} %values.5.refs_0_, bf16[64,2048]{1,0:T(8,128)(2,1)S(1)} %values.6.refs_1_, bf16[2048,3584]{1,0:T(8,128)(2,1)S(1)} %get-tuple-element.74.refs_2_.refs_4_), custom_call_target="tpu_custom_call" | custom-call | flops 1879048192 | bytes 17000000 | tf_op jit(solution)/shard_map/project/pallas_call | solution.py:273
  69.5 1.5 collective-permute-start.16
  71.0 4.0 %collective-permute-done.8.refs_0_ = bf16[32,16,512]{2,1,0:T(8,128)(2,1)S(1)} collective-permute-done((bf16[32,16,512]{2,1,0:T(8,128)(2,1)}, bf16[32,16,512]{2,1,0:T(8,128)(2,1)S(1)}, u32[]{:S(2)}, u32[]{:S(2)}) %collective-permute-start.8) | collective-permute-done | bytes 524320 | tf_op jit(solution)/shard_map/ppermute | solution.py:40
  75.3 2.2 %collective-permute-start.14 = (bf16[32,3584]{1,0:T(8,128)(2,1)S(1)}, bf16[32,3584]{1,0:T(8,128)(2,1)S(1)}, u32[]{:S(2)}, u32[]{:S(2)}) collective-permute-start(bf16[32,3584]{1,0:T(8,128)(2,1)S(1)} %get-tuple-element.80), channel_id=1, source_target_pairs={{0,4},{1,5},{2,6},{3,7},{4,0},{5,1},{6,2},{7,3},{8,12},{9,13},{10,... | collective-permute-start | bytes 688136 | tf_op jit(solution)/shard_map/ppermute | solution.py:40
  77.6 1.5 values.4.refs_0_.refs_2_
  79.1 1.5 values.7.refs_1_.refs_3_
  80.7 3.2 %project.3 = (f32[32,3584]{1,0:T(8,128)S(1)}, f32[32,3584]{1,0:T(8,128)S(1)}, bf16[32,3584]{1,0:T(8,128)(2,1)S(1)}, f32[32,3584]{1,0:T(8,128)S(1)}) custom-call(bf16[64,2048]{1,0:T(8,128)(2,1)S(1)} %values.4.refs_0_.refs_2_, bf16[64,2048]{1,0:T(8,128)(2,1)S(1)} %values.7.refs_1_.refs_3_, bf16[64,2048]{1,0:T(8,128)(2,1)S(1)} %values.4.refs_0_.refs_2_, ...), custom_call_target="tpu_custom_call" | custom-call | flops 1879048192 | bytes 17000000 | tf_op jit(solution)/shard_map/project/pallas_call | solution.py:273
  83.9 3.3 %collective-permute-start.13 = (bf16[32,3584]{1,0:T(8,128)(2,1)S(1)}, bf16[32,3584]{1,0:T(8,128)(2,1)S(1)}, u32[]{:S(2)}, u32[]{:S(2)}) collective-permute-start(bf16[32,3584]{1,0:T(8,128)(2,1)S(1)} %get-tuple-element.75), channel_id=1, source_target_pairs={{0,72},{1,73},{2,74},{3,75},{4,76},{5,77},{6,78},{7,79},{8,0},{9,1... | collective-permute-start | bytes 688136 | tf_op jit(solution)/shard_map/ppermute | solution.py:40
  87.3 1.5 collective-permute-start.17
  90.0 1.1 copy-done.8
  91.2 1.4 copy-done.9
  92.7 2.3 %copy-done.2 = bf16[3584,640]{1,0:T(8,128)(2,1)S(1)} copy-done((bf16[3584,640]{1,0:T(8,128)(2,1)S(1)}, bf16[3584,640]{1,0:T(8,128)(2,1)}, u32[]{:S(2)}) %copy-start.2) | copy-done | bytes 4587544
  95.0 8.5 %hold_feed.1 = (bf16[5,3584,256]{2,1,0:T(8,128)(2,1)S(1)}, bf16[5,3584,256]{2,1,0:T(8,128)(2,1)S(1)}, bf16[1280,3584]{1,0:T(8,128)(2,1)S(1)}) custom-call(bf16[3584,640]{1,0:T(8,128)(2,1)S(1)} %copy-done.2, bf16[3584,640]{1,0:T(8,128)(2,1)} %collective-permute-done.5.g1, bf16[3584,640]{1,0:T(8,128)(2,1)} %u0.1, bf16[3584,640]{1,0:T(8,128)(2,1)} %copy-done.8, ...), custom_call_target="tpu_custom_call" | custom-call | bytes 27500000 | tf_op jit(solution)/shard_map/hold_feed/pallas_call | solution.py:192
  104.0 1.9 %collective-permute-start.28 = (bf16[32,3584]{1,0:T(8,128)(2,1)S(1)}, bf16[32,3584]{1,0:T(8,128)(2,1)S(1)}, u32[]{:S(2)}, u32[]{:S(2)}) collective-permute-start(bf16[32,3584]{1,0:T(8,128)(2,1)S(1)} %get-tuple-element.92.refs_0_), channel_id=1, source_target_pairs={{0,72},{1,73},{2,74},{3,75},{4,76},{5,77},{6,78},{7,79},{8,0},{9,1... | collective-permute-start | bytes 688136 | tf_op jit(solution)/shard_map/ppermute | solution.py:40
  105.9 3.2 %collective-permute-start.25 = (bf16[32,3584]{1,0:T(8,128)(2,1)S(1)}, bf16[32,3584]{1,0:T(8,128)(2,1)S(1)}, u32[]{:S(2)}, u32[]{:S(2)}) collective-permute-start(bf16[32,3584]{1,0:T(8,128)(2,1)S(1)} %get-tuple-element.92.refs_0_), channel_id=1, source_target_pairs={{0,6},{1,7},{2,0},{3,1},{4,2},{5,3},{6,4},{7,5},{8,14},{9,15},{10,... | collective-permute-start | bytes 688136 | tf_op jit(solution)/shard_map/ppermute | solution.py:40
  109.3 1.4 collective-permute-start.23
  113.4 1.6 collective-permute-start.39
  115.0 4.5 %collective-permute-done.25.refs_3_ = bf16[32,3584]{1,0:T(8,128)(2,1)S(1)} collective-permute-done((bf16[32,3584]{1,0:T(8,128)(2,1)S(1)}, bf16[32,3584]{1,0:T(8,128)(2,1)S(1)}, u32[]{:S(2)}, u32[]{:S(2)}) %collective-permute-start.25) | collective-permute-done | bytes 229408 | tf_op jit(solution)/shard_map/ppermute | solution.py:40
  120.0 2.9 %collective-permute-done.23.refs_1_ = bf16[32,3584]{1,0:T(8,128)(2,1)S(1)} collective-permute-done((bf16[32,3584]{1,0:T(8,128)(2,1)S(1)}, bf16[32,3584]{1,0:T(8,128)(2,1)S(1)}, u32[]{:S(2)}, u32[]{:S(2)}) %collective-permute-start.23) | collective-permute-done | bytes 229408 | tf_op jit(solution)/shard_map/ppermute | solution.py:40
  123.3 6.8 %feed.2 = (f32[32,3584]{1,0:T(8,128)S(1)}, f32[32,3584]{1,0:T(8,128)S(1)}, bf16[32,3584]{1,0:T(8,128)(2,1)S(1)}, f32[32,3584]{1,0:T(8,128)S(1)}) custom-call(bf16[32,3584]{1,0:T(8,128)(2,1)S(1)} %get-tuple-element.92.refs_0_, bf16[32,3584]{1,0:T(8,128)(2,1)S(1)} %collective-permute-done.23.refs_1_, bf16[32,3584]{1,0:T(8,128)(2,1)S(1)} %collective-permute-done.24.refs_2_, ...), custom_call_target="tpu_custom_call" | custom-call | flops 3523215360 | bytes 28000000 | tf_op jit(solution)/shard_map/feed/pallas_call | solution.py:318
  130.1 6.8 %feed.3 = (bf16[32,3584]{1,0:T(8,128)(2,1)S(1)}, bf16[32,3584]{1,0:T(8,128)(2,1)S(1)}, bf16[32,3584]{1,0:T(8,128)(2,1)S(1)}, bf16[32,3584]{1,0:T(8,128)(2,1)S(1)}) custom-call(bf16[32,3584]{1,0:T(8,128)(2,1)S(1)} %collective-permute-done.26.refs_0_, bf16[32,3584]{1,0:T(8,128)(2,1)S(1)} %collective-permute-done.27.refs_1_, ...), custom_call_target="tpu_custom_call" | custom-call | flops 3523215360 | bytes 28000000 | tf_op jit(solution)/shard_map/feed/pallas_call | solution.py:318
  136.8 2.9 %collective-permute-start.34 = (bf16[32,3584]{1,0:T(8,128)(2,1)S(1)}, bf16[32,3584]{1,0:T(8,128)(2,1)S(1)}, u32[]{:S(2)}, u32[]{:S(2)}) collective-permute-start(bf16[32,3584]{1,0:T(8,128)(2,1)S(1)} %get-tuple-element.100), channel_id=1, source_target_pairs={{0,72},{1,73},{2,74},{3,75},{4,76},{5,77},{6,78},{7,79},{8,0},{9,1... | collective-permute-start | bytes 688136 | tf_op jit(solution)/shard_map/ppermute | solution.py:40
  140.4 3.3 %collective-permute-start.40 = (bf16[2,64,576]{2,1,0:T(8,128)(2,1)S(1)}, bf16[2,64,576]{2,1,0:T(8,128)(2,1)S(1)}, u32[]{:S(2)}, u32[]{:S(2)}) collective-permute-start(bf16[2,64,576]{2,1,0:T(8,128)(2,1)S(1)} %pick.3.mine_ref), channel_id=1, source_target_pairs={{0,32},{16,48},{32,0},{48,16},{64,96},{80,112},{96,64},{112,80},{1... | collective-permute-start | bytes 442376 | tf_op jit(solution)/shard_map/ppermute | solution.py:478
  144.7 2.6 %collective-permute-done.40.other_ref = bf16[2,64,576]{2,1,0:T(8,128)(2,1)S(1)} collective-permute-done((bf16[2,64,576]{2,1,0:T(8,128)(2,1)S(1)}, bf16[2,64,576]{2,1,0:T(8,128)(2,1)S(1)}, u32[]{:S(2)}, u32[]{:S(2)}) %collective-permute-start.40) | collective-permute-done | bytes 147488 | tf_op jit(solution)/shard_map/ppermute | solution.py:478
  148.2 1.4 collective-permute-start.36
  149.6 2.2 %collective-permute-start.31 = (bf16[32,3584]{1,0:T(8,128)(2,1)S(1)}, bf16[32,3584]{1,0:T(8,128)(2,1)S(1)}, u32[]{:S(2)}, u32[]{:S(2)}) collective-permute-start(bf16[32,3584]{1,0:T(8,128)(2,1)S(1)} %get-tuple-element.97), channel_id=1, source_target_pairs={{0,72},{1,73},{2,74},{3,75},{4,76},{5,77},{6,78},{7,79},{8,0},{9,1... | collective-permute-start | bytes 688136 | tf_op jit(solution)/shard_map/ppermute | solution.py:40
  151.8 1.6 collective-permute-done.32
  153.4 2.0 %collective-permute-start.35 = (bf16[32,3584]{1,0:T(8,128)(2,1)S(1)}, bf16[32,3584]{1,0:T(8,128)(2,1)S(1)}, u32[]{:S(2)}, u32[]{:S(2)}) collective-permute-start(bf16[32,3584]{1,0:T(8,128)(2,1)S(1)} %fold.6), channel_id=1, source_target_pairs={{0,6},{1,7},{2,0},{3,1},{4,2},{5,3},{6,4},{7,5},{8,14},{9,15},{10,... | collective-permute-start | bytes 688136 | tf_op jit(solution)/shard_map/ppermute | solution.py:40
  157.3 1.3 pick.5
  158.7 4.9 %collective-permute-done.33.refs_1_ = bf16[32,3584]{1,0:T(8,128)(2,1)S(1)} collective-permute-done((bf16[32,3584]{1,0:T(8,128)(2,1)S(1)}, bf16[32,3584]{1,0:T(8,128)(2,1)S(1)}, u32[]{:S(2)}, u32[]{:S(2)}) %collective-permute-start.33) | collective-permute-done | bytes 229408 | tf_op jit(solution)/shard_map/ppermute | solution.py:40
  (83 shorter events, 12.4 us)
Async XLA Ops:
  0.6 53.8 %copy-start.3 = (bf16[8,512,128]{2,1,0:T(8,128)(2,1)S(1)}, bf16[8,512,128]{2,1,0:T(8,128)(2,1)}, u32[]{:S(2)}) copy-start(bf16[8,512,128]{2,1,0:T(8,128)(2,1)} %up_own.1) | copy-start | bytes 3145732
  0.6 30.2 %collective-permute-start.4 = (bf16[1024,3584]{1,0:T(8,128)(2,1)}, bf16[1024,3584]{1,0:T(8,128)(2,1)}, u32[]{:S(2)}, u32[]{:S(2)}) collective-permute-start(bf16[1024,3584]{1,0:T(8,128)(2,1)} %out_own.1), channel_id=1, source_target_pairs={{0,1},{1,0},{2,3},{3,2},{4,5},{5,4},{6,7},{7,6},{8,9},{9,8},{10,11... | collective-permute-start | bytes 22020104 | tf_op jit(solution)/shard_map/ppermute | solution.py:44
  0.7 30.1 %collective-permute-start.5 = (bf16[3584,640]{1,0:T(8,128)(2,1)}, bf16[3584,640]{1,0:T(8,128)(2,1)}, u32[]{:S(2)}, u32[]{:S(2)}) collective-permute-start(bf16[3584,640]{1,0:T(8,128)(2,1)} %g0), channel_id=1, source_target_pairs={{0,1},{1,0},{2,3},{3,2},{4,5},{5,4},{6,7},{7,6},{8,9},{9,8},{10,11... | collective-permute-start | bytes 13762568 | tf_op jit(solution)/shard_map/ppermute | solution.py:44
  1.2 9.8 %collective-permute-start = (bf16[8,512,128]{2,1,0:T(8,128)(2,1)}, bf16[8,512,128]{2,1,0:T(8,128)(2,1)S(1)}, u32[]{:S(2)}, u32[]{:S(2)}) collective-permute-start(bf16[8,512,128]{2,1,0:T(8,128)(2,1)} %up_own.1), channel_id=1, source_target_pairs={{0,1},{1,0},{2,3},{3,2},{4,5},{5,4},{6,7},{7,6},{8,9},{9,8},{10,11... | collective-permute-start | bytes 3145736 | tf_op jit(solution)/shard_map/ppermute | solution.py:44
  11.0 16.2 %collective-permute-start.3 = (bf16[32,16,512]{2,1,0:T(8,128)(2,1)}, bf16[32,16,512]{2,1,0:T(8,128)(2,1)S(1)}, u32[]{:S(2)}, u32[]{:S(2)}) collective-permute-start(bf16[32,16,512]{2,1,0:T(8,128)(2,1)} %get-tuple-element.61), channel_id=1, source_target_pairs={{0,72},{1,73},{2,74},{3,75},{4,76},{5,77},{6,78},{7,79},{8,0},{9,1... | collective-permute-start | bytes 1572872 | tf_op jit(solution)/shard_map/ppermute | solution.py:40
  15.2 15.4 %collective-permute-start.2 = (bf16[32,16,512]{2,1,0:T(8,128)(2,1)}, bf16[32,16,512]{2,1,0:T(8,128)(2,1)S(1)}, u32[]{:S(2)}, u32[]{:S(2)}) collective-permute-start(bf16[32,16,512]{2,1,0:T(8,128)(2,1)} %get-tuple-element.59), channel_id=1, source_target_pairs={{0,8},{1,9},{2,10},{3,11},{4,12},{5,13},{6,14},{7,15},{8,64},{9,65... | collective-permute-start | bytes 1572872 | tf_op jit(solution)/shard_map/ppermute | solution.py:40
  15.2 15.7 %collective-permute-start.1 = (bf16[32,16,512]{2,1,0:T(8,128)(2,1)}, bf16[32,16,512]{2,1,0:T(8,128)(2,1)S(1)}, u32[]{:S(2)}, u32[]{:S(2)}) collective-permute-start(bf16[32,16,512]{2,1,0:T(8,128)(2,1)} %get-tuple-element.57), channel_id=1, source_target_pairs={{0,4},{1,5},{2,6},{3,7},{4,0},{5,1},{6,2},{7,3},{8,12},{9,13},{10,... | collective-permute-start | bytes 1572872 | tf_op jit(solution)/shard_map/ppermute | solution.py:40
  30.9 14.6 %collective-permute-start.6 = (bf16[32,16,512]{2,1,0:T(8,128)(2,1)}, bf16[32,16,512]{2,1,0:T(8,128)(2,1)S(1)}, u32[]{:S(2)}, u32[]{:S(2)}) collective-permute-start(bf16[32,16,512]{2,1,0:T(8,128)(2,1)} %get-tuple-element.68), channel_id=1, source_target_pairs={{0,8},{1,9},{2,10},{3,11},{4,12},{5,13},{6,14},{7,15},{8,64},{9,65... | collective-permute-start | bytes 1572872 | tf_op jit(solution)/shard_map/ppermute | solution.py:40
  30.9 14.6 %collective-permute-start.7 = (bf16[32,16,512]{2,1,0:T(8,128)(2,1)}, bf16[32,16,512]{2,1,0:T(8,128)(2,1)S(1)}, u32[]{:S(2)}, u32[]{:S(2)}) collective-permute-start(bf16[32,16,512]{2,1,0:T(8,128)(2,1)} %get-tuple-element.70), channel_id=1, source_target_pairs={{0,72},{1,73},{2,74},{3,75},{4,76},{5,77},{6,78},{7,79},{8,0},{9,1... | collective-permute-start | bytes 1572872 | tf_op jit(solution)/shard_map/ppermute | solution.py:40
  34.1 13.8 %collective-permute-start.9 = (bf16[32,16,512]{2,1,0:T(8,128)(2,1)S(1)}, bf16[32,16,512]{2,1,0:T(8,128)(2,1)S(1)}, u32[]{:S(2)}, u32[]{:S(2)}) collective-permute-start(bf16[32,16,512]{2,1,0:T(8,128)(2,1)S(1)} %collective-permute-done.2), channel_id=1, source_target_pairs={{0,2},{1,3},{2,4},{3,5},{4,6},{5,7},{6,0},{7,1},{8,10},{9,11},{10,... | collective-permute-start | bytes 1572872 | tf_op jit(solution)/shard_map/ppermute | solution.py:40
  35.6 12.3 %collective-permute-start.11 = (bf16[32,16,512]{2,1,0:T(8,128)(2,1)S(1)}, bf16[32,16,512]{2,1,0:T(8,128)(2,1)S(1)}, u32[]{:S(2)}, u32[]{:S(2)}) collective-permute-start(bf16[32,16,512]{2,1,0:T(8,128)(2,1)S(1)} %collective-permute-done.3), channel_id=1, source_target_pairs={{0,6},{1,7},{2,0},{3,1},{4,2},{5,3},{6,4},{7,5},{8,14},{9,15},{10,... | collective-permute-start | bytes 1572872 | tf_op jit(solution)/shard_map/ppermute | solution.py:40
  47.9 41.1 %collective-permute-start.19 = (bf16[3584,640]{1,0:T(8,128)(2,1)}, bf16[3584,640]{1,0:T(8,128)(2,1)S(1)}, u32[]{:S(2)}, u32[]{:S(2)}) collective-permute-start(bf16[3584,640]{1,0:T(8,128)(2,1)} %u0.1), channel_id=1, source_target_pairs={{0,1},{1,0},{2,3},{3,2},{4,5},{5,4},{6,7},{7,6},{8,9},{9,8},{10,11... | collective-permute-start | bytes 13762568 | tf_op jit(solution)/shard_map/ppermute | solution.py:44
  47.9 41.7 %collective-permute-start.20 = (bf16[640,3584]{1,0:T(8,128)(2,1)}, bf16[640,3584]{1,0:T(8,128)(2,1)S(1)}, u32[]{:S(2)}, u32[]{:S(2)}) collective-permute-start(bf16[640,3584]{1,0:T(8,128)(2,1)} %d0.1), channel_id=1, source_target_pairs={{0,1},{1,0},{2,3},{3,2},{4,5},{5,4},{6,7},{7,6},{8,9},{9,8},{10,11... | collective-permute-start | bytes 13762568 | tf_op jit(solution)/shard_map/ppermute | solution.py:44
  48.4 16.3 %collective-permute-start.10 = (bf16[32,16,512]{2,1,0:T(8,128)(2,1)S(1)}, bf16[32,16,512]{2,1,0:T(8,128)(2,1)S(1)}, u32[]{:S(2)}, u32[]{:S(2)}) collective-permute-start(bf16[32,16,512]{2,1,0:T(8,128)(2,1)S(1)} %collective-permute-done.7), channel_id=1, source_target_pairs={{0,4},{1,5},{2,6},{3,7},{4,0},{5,1},{6,2},{7,3},{8,12},{9,13},{10,... | collective-permute-start | bytes 1572872 | tf_op jit(solution)/shard_map/ppermute | solution.py:40
  51.2 23.8 %collective-permute-start.8 = (bf16[32,16,512]{2,1,0:T(8,128)(2,1)}, bf16[32,16,512]{2,1,0:T(8,128)(2,1)S(1)}, u32[]{:S(2)}, u32[]{:S(2)}) collective-permute-start(bf16[32,16,512]{2,1,0:T(8,128)(2,1)} %get-tuple-element.71), channel_id=1, source_target_pairs={{0,2},{1,3},{2,4},{3,5},{4,6},{5,7},{6,0},{7,1},{8,10},{9,11},{10,... | collective-permute-start | bytes 1572872 | tf_op jit(solution)/shard_map/ppermute | solution.py:40
  52.3 23.1 %collective-permute-start.12 = (bf16[32,16,512]{2,1,0:T(8,128)(2,1)}, bf16[32,16,512]{2,1,0:T(8,128)(2,1)S(1)}, u32[]{:S(2)}, u32[]{:S(2)}) collective-permute-start(bf16[32,16,512]{2,1,0:T(8,128)(2,1)} %get-tuple-element.78), channel_id=1, source_target_pairs={{0,6},{1,7},{2,0},{3,1},{4,2},{5,3},{6,4},{7,5},{8,14},{9,15},{10,... | collective-permute-start | bytes 1572872 | tf_op jit(solution)/shard_map/ppermute | solution.py:40
  66.3 11.3 %copy-start.4 = (bf16[32,16,512]{2,1,0:T(8,128)(2,1)S(1)}, bf16[32,16,512]{2,1,0:T(8,128)(2,1)}, u32[]{:S(2)}) copy-start(bf16[32,16,512]{2,1,0:T(8,128)(2,1)} %get-tuple-element.64.refs_0_) | copy-start | bytes 1572868
  69.5 14.3 %collective-permute-start.16 = (bf16[32,3584]{1,0:T(8,128)(2,1)S(1)}, bf16[32,3584]{1,0:T(8,128)(2,1)S(1)}, u32[]{:S(2)}, u32[]{:S(2)}) collective-permute-start(bf16[32,3584]{1,0:T(8,128)(2,1)S(1)} %get-tuple-element.82), channel_id=1, source_target_pairs={{0,72},{1,73},{2,74},{3,75},{4,76},{5,77},{6,78},{7,79},{8,0},{9,1... | collective-permute-start | bytes 688136 | tf_op jit(solution)/shard_map/ppermute | solution.py:40
  75.0 12.2 %collective-permute-start.18 = (bf16[32,3584]{1,0:T(8,128)(2,1)S(1)}, bf16[32,3584]{1,0:T(8,128)(2,1)S(1)}, u32[]{:S(2)}, u32[]{:S(2)}) collective-permute-start(bf16[32,3584]{1,0:T(8,128)(2,1)S(1)} %get-tuple-element.84), channel_id=1, source_target_pairs={{0,8},{1,9},{2,10},{3,11},{4,12},{5,13},{6,14},{7,15},{8,64},{9,65... | collective-permute-start | bytes 688136 | tf_op jit(solution)/shard_map/ppermute | solution.py:40
  75.3 13.5 %collective-permute-start.14 = (bf16[32,3584]{1,0:T(8,128)(2,1)S(1)}, bf16[32,3584]{1,0:T(8,128)(2,1)S(1)}, u32[]{:S(2)}, u32[]{:S(2)}) collective-permute-start(bf16[32,3584]{1,0:T(8,128)(2,1)S(1)} %get-tuple-element.80), channel_id=1, source_target_pairs={{0,4},{1,5},{2,6},{3,7},{4,0},{5,1},{6,2},{7,3},{8,12},{9,13},{10,... | collective-permute-start | bytes 688136 | tf_op jit(solution)/shard_map/ppermute | solution.py:40
  80.7 11.9 %copy-start.5 = (bf16[16,2,3584]{2,1,0:T(2,128)(2,1)S(1)}, bf16[16,2,3584]{2,1,0:T(2,128)(2,1)}, u32[]{:S(2)}) copy-start(bf16[16,2,3584]{2,1,0:T(2,128)(2,1)} %hidden_ref) | copy-start | bytes 688132
  83.9 19.7 %collective-permute-start.13 = (bf16[32,3584]{1,0:T(8,128)(2,1)S(1)}, bf16[32,3584]{1,0:T(8,128)(2,1)S(1)}, u32[]{:S(2)}, u32[]{:S(2)}) collective-permute-start(bf16[32,3584]{1,0:T(8,128)(2,1)S(1)} %get-tuple-element.75), channel_id=1, source_target_pairs={{0,72},{1,73},{2,74},{3,75},{4,76},{5,77},{6,78},{7,79},{8,0},{9,1... | collective-permute-start | bytes 688136 | tf_op jit(solution)/shard_map/ppermute | solution.py:40
  87.3 16.3 %collective-permute-start.17 = (bf16[32,3584]{1,0:T(8,128)(2,1)S(1)}, bf16[32,3584]{1,0:T(8,128)(2,1)S(1)}, u32[]{:S(2)}, u32[]{:S(2)}) collective-permute-start(bf16[32,3584]{1,0:T(8,128)(2,1)S(1)} %fold.4), channel_id=1, source_target_pairs={{0,6},{1,7},{2,0},{3,1},{4,2},{5,3},{6,4},{7,5},{8,14},{9,15},{10,... | collective-permute-start | bytes 688136 | tf_op jit(solution)/shard_map/ppermute | solution.py:40
  88.8 14.7 %collective-permute-start.21 = (bf16[32,3584]{1,0:T(8,128)(2,1)S(1)}, bf16[32,3584]{1,0:T(8,128)(2,1)S(1)}, u32[]{:S(2)}, u32[]{:S(2)}) collective-permute-start(bf16[32,3584]{1,0:T(8,128)(2,1)S(1)} %get-tuple-element.90), channel_id=1, source_target_pairs={{0,4},{1,5},{2,6},{3,7},{4,0},{5,1},{6,2},{7,3},{8,12},{9,13},{10,... | collective-permute-start | bytes 688136 | tf_op jit(solution)/shard_map/ppermute | solution.py:40
  89.0 14.5 %collective-permute-start.15 = (bf16[32,3584]{1,0:T(8,128)(2,1)S(1)}, bf16[32,3584]{1,0:T(8,128)(2,1)S(1)}, u32[]{:S(2)}, u32[]{:S(2)}) collective-permute-start(bf16[32,3584]{1,0:T(8,128)(2,1)S(1)} %collective-permute-done.14), channel_id=1, source_target_pairs={{0,8},{1,9},{2,10},{3,11},{4,12},{5,13},{6,14},{7,15},{8,64},{9,65... | collective-permute-start | bytes 688136 | tf_op jit(solution)/shard_map/ppermute | solution.py:40
  89.6 13.9 %collective-permute-start.22 = (bf16[32,3584]{1,0:T(8,128)(2,1)S(1)}, bf16[32,3584]{1,0:T(8,128)(2,1)S(1)}, u32[]{:S(2)}, u32[]{:S(2)}) collective-permute-start(bf16[32,3584]{1,0:T(8,128)(2,1)S(1)} %fold.5), channel_id=1, source_target_pairs={{0,2},{1,3},{2,4},{3,5},{4,6},{5,7},{6,0},{7,1},{8,10},{9,11},{10,... | collective-permute-start | bytes 688136 | tf_op jit(solution)/shard_map/ppermute | solution.py:40
  95.0 17.0 %copy-start = (bf16[16,192,576]{2,1,0:T(8,128)(2,1)S(1)}, bf16[16,192,576]{2,1,0:T(8,128)(2,1)}, u32[]{:S(2)}) copy-start(bf16[16,192,576]{2,1,0:T(8,128)(2,1)} %cache_ref.3) | copy-start | bytes 10616836
  95.0 17.1 %copy-start.6 = (s32[4]{0:T(128)S(1)}, s32[4]{0:T(128)}, u32[]{:S(2)}) copy-start(s32[4]{0:T(128)} %pad_add_fusion.where_ref.ids_ref) | copy-start | bytes 52
  95.0 17.1 %copy-start.7 = (s32[8,1]{0,1:T(1,128)S(1)}, s32[8,1]{0,1:T(1,128)}, u32[]{:S(2)}) copy-start(s32[8,1]{0,1:T(1,128)} %param.25) | copy-start | bytes 100
  104.0 9.4 %collective-permute-start.28 = (bf16[32,3584]{1,0:T(8,128)(2,1)S(1)}, bf16[32,3584]{1,0:T(8,128)(2,1)S(1)}, u32[]{:S(2)}, u32[]{:S(2)}) collective-permute-start(bf16[32,3584]{1,0:T(8,128)(2,1)S(1)} %get-tuple-element.92.refs_0_), channel_id=1, source_target_pairs={{0,72},{1,73},{2,74},{3,75},{4,76},{5,77},{6,78},{7,79},{8,0},{9,1... | collective-permute-start | bytes 688136 | tf_op jit(solution)/shard_map/ppermute | solution.py:40
  105.9 13.5 %collective-permute-start.25 = (bf16[32,3584]{1,0:T(8,128)(2,1)S(1)}, bf16[32,3584]{1,0:T(8,128)(2,1)S(1)}, u32[]{:S(2)}, u32[]{:S(2)}) collective-permute-start(bf16[32,3584]{1,0:T(8,128)(2,1)S(1)} %get-tuple-element.92.refs_0_), channel_id=1, source_target_pairs={{0,6},{1,7},{2,0},{3,1},{4,2},{5,3},{6,4},{7,5},{8,14},{9,15},{10,... | collective-permute-start | bytes 688136 | tf_op jit(solution)/shard_map/ppermute | solution.py:40
  109.1 10.3 %collective-permute-start.24 = (bf16[32,3584]{1,0:T(8,128)(2,1)S(1)}, bf16[32,3584]{1,0:T(8,128)(2,1)S(1)}, u32[]{:S(2)}, u32[]{:S(2)}) collective-permute-start(bf16[32,3584]{1,0:T(8,128)(2,1)S(1)} %get-tuple-element.92.refs_0_), channel_id=1, source_target_pairs={{0,4},{1,5},{2,6},{3,7},{4,0},{5,1},{6,2},{7,3},{8,12},{9,13},{10,... | collective-permute-start | bytes 688136 | tf_op jit(solution)/shard_map/ppermute | solution.py:40
  109.3 13.5 %collective-permute-start.23 = (bf16[32,3584]{1,0:T(8,128)(2,1)S(1)}, bf16[32,3584]{1,0:T(8,128)(2,1)S(1)}, u32[]{:S(2)}, u32[]{:S(2)}) collective-permute-start(bf16[32,3584]{1,0:T(8,128)(2,1)S(1)} %get-tuple-element.92.refs_0_), channel_id=1, source_target_pairs={{0,2},{1,3},{2,4},{3,5},{4,6},{5,7},{6,0},{7,1},{8,10},{9,11},{10,... | collective-permute-start | bytes 688136 | tf_op jit(solution)/shard_map/ppermute | solution.py:40
  113.2 16.9 %collective-permute-start.26 = (bf16[32,3584]{1,0:T(8,128)(2,1)S(1)}, bf16[32,3584]{1,0:T(8,128)(2,1)S(1)}, u32[]{:S(2)}, u32[]{:S(2)}) collective-permute-start(bf16[32,3584]{1,0:T(8,128)(2,1)S(1)} %get-tuple-element.92.refs_0_), channel_id=1, source_target_pairs={{0,8},{1,9},{2,10},{3,11},{4,12},{5,13},{6,14},{7,15},{8,64},{9,65... | collective-permute-start | bytes 688136 | tf_op jit(solution)/shard_map/ppermute | solution.py:40
  113.4 26.3 %collective-permute-start.39 = (bf16[2,64,576]{2,1,0:T(8,128)(2,1)S(1)}, bf16[2,64,576]{2,1,0:T(8,128)(2,1)S(1)}, u32[]{:S(2)}, u32[]{:S(2)}) collective-permute-start(bf16[2,64,576]{2,1,0:T(8,128)(2,1)S(1)} %get-tuple-element.107.mine_ref), channel_id=1, source_target_pairs={{0,16},{16,0},{32,48},{48,32},{64,80},{80,64},{96,112},{112,96},{1... | collective-permute-start | bytes 442376 | tf_op jit(solution)/shard_map/ppermute | solution.py:478
  119.5 10.6 %collective-permute-start.29 = (bf16[32,3584]{1,0:T(8,128)(2,1)S(1)}, bf16[32,3584]{1,0:T(8,128)(2,1)S(1)}, u32[]{:S(2)}, u32[]{:S(2)}) collective-permute-start(bf16[32,3584]{1,0:T(8,128)(2,1)S(1)} %collective-permute-done.28), channel_id=1, source_target_pairs={{0,4},{1,5},{2,6},{3,7},{4,0},{5,1},{6,2},{7,3},{8,12},{9,13},{10,... | collective-permute-start | bytes 688136 | tf_op jit(solution)/shard_map/ppermute | solution.py:40
  119.5 10.6 %collective-permute-start.30 = (bf16[32,3584]{1,0:T(8,128)(2,1)S(1)}, bf16[32,3584]{1,0:T(8,128)(2,1)S(1)}, u32[]{:S(2)}, u32[]{:S(2)}) collective-permute-start(bf16[32,3584]{1,0:T(8,128)(2,1)S(1)} %collective-permute-done.25.refs_3_), channel_id=1, source_target_pairs={{0,72},{1,73},{2,74},{3,75},{4,76},{5,77},{6,78},{7,79},{8,0},{9,1... | collective-permute-start | bytes 688136 | tf_op jit(solution)/shard_map/ppermute | solution.py:40
  122.8 7.2 %collective-permute-start.27 = (bf16[32,3584]{1,0:T(8,128)(2,1)S(1)}, bf16[32,3584]{1,0:T(8,128)(2,1)S(1)}, u32[]{:S(2)}, u32[]{:S(2)}) collective-permute-start(bf16[32,3584]{1,0:T(8,128)(2,1)S(1)} %collective-permute-done.23.refs_1_), channel_id=1, source_target_pairs={{0,8},{1,9},{2,10},{3,11},{4,12},{5,13},{6,14},{7,15},{8,64},{9,65... | collective-permute-start | bytes 688136 | tf_op jit(solution)/shard_map/ppermute | solution.py:40
  136.8 11.1 %collective-permute-start.34 = (bf16[32,3584]{1,0:T(8,128)(2,1)S(1)}, bf16[32,3584]{1,0:T(8,128)(2,1)S(1)}, u32[]{:S(2)}, u32[]{:S(2)}) collective-permute-start(bf16[32,3584]{1,0:T(8,128)(2,1)S(1)} %get-tuple-element.100), channel_id=1, source_target_pairs={{0,72},{1,73},{2,74},{3,75},{4,76},{5,77},{6,78},{7,79},{8,0},{9,1... | collective-permute-start | bytes 688136 | tf_op jit(solution)/shard_map/ppermute | solution.py:40
  140.4 6.9 %collective-permute-start.40 = (bf16[2,64,576]{2,1,0:T(8,128)(2,1)S(1)}, bf16[2,64,576]{2,1,0:T(8,128)(2,1)S(1)}, u32[]{:S(2)}, u32[]{:S(2)}) collective-permute-start(bf16[2,64,576]{2,1,0:T(8,128)(2,1)S(1)} %pick.3.mine_ref), channel_id=1, source_target_pairs={{0,32},{16,48},{32,0},{48,16},{64,96},{80,112},{96,64},{112,80},{1... | collective-permute-start | bytes 442376 | tf_op jit(solution)/shard_map/ppermute | solution.py:478
  143.7 9.7 %collective-permute-start.32 = (bf16[32,3584]{1,0:T(8,128)(2,1)S(1)}, bf16[32,3584]{1,0:T(8,128)(2,1)S(1)}, u32[]{:S(2)}, u32[]{:S(2)}) collective-permute-start(bf16[32,3584]{1,0:T(8,128)(2,1)S(1)} %get-tuple-element.98), channel_id=1, source_target_pairs={{0,4},{1,5},{2,6},{3,7},{4,0},{5,1},{6,2},{7,3},{8,12},{9,13},{10,... | collective-permute-start | bytes 688136 | tf_op jit(solution)/shard_map/ppermute | solution.py:40
  144.3 12.1 %collective-permute-start.37 = (bf16[32,3584]{1,0:T(8,128)(2,1)S(1)}, bf16[32,3584]{1,0:T(8,128)(2,1)S(1)}, u32[]{:S(2)}, u32[]{:S(2)}) collective-permute-start(bf16[32,3584]{1,0:T(8,128)(2,1)S(1)} %get-tuple-element.103), channel_id=1, source_target_pairs={{0,8},{1,9},{2,10},{3,11},{4,12},{5,13},{6,14},{7,15},{8,64},{9,65... | collective-permute-start | bytes 688136 | tf_op jit(solution)/shard_map/ppermute | solution.py:40
  148.1 8.4 %collective-permute-start.41 = (bf16[2,64,576]{2,1,0:T(8,128)(2,1)S(1)}, bf16[2,64,576]{2,1,0:T(8,128)(2,1)S(1)}, u32[]{:S(2)}, u32[]{:S(2)}) collective-permute-start(bf16[2,64,576]{2,1,0:T(8,128)(2,1)S(1)} %pick.4.mine_ref), channel_id=1, source_target_pairs={{0,64},{16,80},{32,96},{48,112},{64,0},{80,16},{96,32},{112,48},{1... | collective-permute-start | bytes 442376 | tf_op jit(solution)/shard_map/ppermute | solution.py:478
  148.2 10.5 %collective-permute-start.36 = (bf16[32,3584]{1,0:T(8,128)(2,1)S(1)}, bf16[32,3584]{1,0:T(8,128)(2,1)S(1)}, u32[]{:S(2)}, u32[]{:S(2)}) collective-permute-start(bf16[32,3584]{1,0:T(8,128)(2,1)S(1)} %get-tuple-element.101), channel_id=1, source_target_pairs={{0,4},{1,5},{2,6},{3,7},{4,0},{5,1},{6,2},{7,3},{8,12},{9,13},{10,... | collective-permute-start | bytes 688136 | tf_op jit(solution)/shard_map/ppermute | solution.py:40
  149.6 9.1 %collective-permute-start.31 = (bf16[32,3584]{1,0:T(8,128)(2,1)S(1)}, bf16[32,3584]{1,0:T(8,128)(2,1)S(1)}, u32[]{:S(2)}, u32[]{:S(2)}) collective-permute-start(bf16[32,3584]{1,0:T(8,128)(2,1)S(1)} %get-tuple-element.97), channel_id=1, source_target_pairs={{0,72},{1,73},{2,74},{3,75},{4,76},{5,77},{6,78},{7,79},{8,0},{9,1... | collective-permute-start | bytes 688136 | tf_op jit(solution)/shard_map/ppermute | solution.py:40
  153.4 10.2 %collective-permute-start.35 = (bf16[32,3584]{1,0:T(8,128)(2,1)S(1)}, bf16[32,3584]{1,0:T(8,128)(2,1)S(1)}, u32[]{:S(2)}, u32[]{:S(2)}) collective-permute-start(bf16[32,3584]{1,0:T(8,128)(2,1)S(1)} %fold.6), channel_id=1, source_target_pairs={{0,6},{1,7},{2,0},{3,1},{4,2},{5,3},{6,4},{7,5},{8,14},{9,15},{10,... | collective-permute-start | bytes 688136 | tf_op jit(solution)/shard_map/ppermute | solution.py:40
  156.4 7.2 %collective-permute-start.33 = (bf16[32,3584]{1,0:T(8,128)(2,1)S(1)}, bf16[32,3584]{1,0:T(8,128)(2,1)S(1)}, u32[]{:S(2)}, u32[]{:S(2)}) collective-permute-start(bf16[32,3584]{1,0:T(8,128)(2,1)S(1)} %collective-permute-done.32), channel_id=1, source_target_pairs={{0,8},{1,9},{2,10},{3,11},{4,12},{5,13},{6,14},{7,15},{8,64},{9,65... | collective-permute-start | bytes 688136 | tf_op jit(solution)/shard_map/ppermute | solution.py:40
  156.5 7.3 %collective-permute-start.38 = (bf16[32,3584]{1,0:T(8,128)(2,1)S(1)}, bf16[32,3584]{1,0:T(8,128)(2,1)S(1)}, u32[]{:S(2)}, u32[]{:S(2)}) collective-permute-start(bf16[32,3584]{1,0:T(8,128)(2,1)S(1)} %fold.7), channel_id=1, source_target_pairs={{0,2},{1,3},{2,4},{3,5},{4,6},{5,7},{6,0},{7,1},{8,10},{9,11},{10,... | collective-permute-start | bytes 688136 | tf_op jit(solution)/shard_map/ppermute | solution.py:40
  (5 other events, 19.9 us)

commit v2 on v1

--- a/solution.py
+++ b/solution.py
@@ -136,7 +136,12 @@
 
 
 HBM_SPEC = pl.BlockSpec(memory_space=pltpu.HBM)
+ANY_SPEC = pl.BlockSpec(memory_space=pl.ANY)
 VMEM_SPEC = pl.BlockSpec(memory_space=pltpu.VMEM)
+
+
+def in_hbm(value):
+    return pltpu.with_memory_space_constraint(value, pltpu.HBM)
 
 
 def run_copies(copies):
@@ -160,7 +165,7 @@
 def hold_projection(up_own, up_other, out_own, out_other):
     return pl.pallas_call(
         hold_projection_kernel,
-        in_specs=[HBM_SPEC] * 4,
+        in_specs=[HBM_SPEC, ANY_SPEC] * 2,
         out_specs=[VMEM_SPEC] * 2,
         out_shape=[
             vmem_out((16,) + up_own.shape[1:]),
@@ -170,7 +175,7 @@
         cost_estimate=pl.CostEstimate(flops=0, bytes_accessed=17_000_000, transcendentals=0),
         compiler_params=pltpu.CompilerParams(vmem_limit_bytes=16 * 1024 * 1024),
         name="hold_projection",
-    )(up_own, up_other, out_own, out_other)
+    )(in_hbm(up_own), up_other, in_hbm(out_own), out_other)
 
 
 def hold_feed_kernel(g0, g1, u0, u1, d0, d1, own_ref, other_ref, down_ref, sems):
@@ -191,14 +196,14 @@
     tiles = units // 128
     return pl.pallas_call(
         hold_feed_kernel,
-        in_specs=[HBM_SPEC] * 6,
+        in_specs=[HBM_SPEC, ANY_SPEC] * 3,
         out_specs=[VMEM_SPEC] * 3,
         out_shape=[vmem_out((tiles, width, 256))] * 2 + [vmem_out((2 * units, width))],
         scratch_shapes=[pltpu.SemaphoreType.DMA((4 * tiles + 2,))],
         cost_estimate=pl.CostEstimate(flops=0, bytes_accessed=27_500_000, transcendentals=0),
         compiler_params=pltpu.CompilerParams(vmem_limit_bytes=16 * 1024 * 1024),
         name="hold_feed",
-    )(g0, g1, u0, u1, d0, d1)
+    )(in_hbm(g0), g1, in_hbm(u0), u1, in_hbm(d0), d1)
 
 
 def values_kernel(*refs, blocks):
@@ -459,7 +464,7 @@
         compiler_params=SMALL,
         cost_estimate=pl.CostEstimate(flops=1_000, bytes_accessed=400_000, transcendentals=0),
         name="pages",
-    )(ids, partner.reshape(-1), moved_request, moved_pages, cache)
+    )(ids, partner.reshape(-1), moved_request, moved_pages, in_hbm(cache))
 
 
 def pick_kernel(offset_ref, mine_ref, other_ref, out_ref, *, bit):
@@ -474,8 +479,11 @@
         out_ref[...] = mine_ref[...]
 
 
-def page_step(block, offset, bit):
-    other = lax.ppermute(block, "dp", [(d, d ^ (1 << bit)) for d in range(8)])
+def page_trade(block, bit):
+    return lax.ppermute(block, "dp", [(d, d ^ (1 << bit)) for d in range(8)])
+
+
+def page_pick(block, other, offset, bit):
     return pl.pallas_call(
         functools.partial(pick_kernel, bit=bit),
         in_specs=[pl.BlockSpec(memory_space=pltpu.SMEM), VMEM_SPEC, VMEM_SPEC],
@@ -518,6 +526,10 @@
     go1, go3, own2 = after(go1, up_other), after(go3, up_other), after(own2, up_other)
     far_in1, far_in3 = shift(go1, dz=1), shift(go3, dz=-1)
     near2 = shift(own2, dx=2)
+    block, offset = page_block(
+        after(where, go1), partner, moved_request, moved_pages, request_latent_cache
+    )
+    traded = page_trade(block, 0)
     first = (near2, far_in1, far_in3, out_other, gate_other)
     far1 = shift(after(far_in1, *first), dx=1)
     far3 = shift(after(far_in3, *first), dx=3)
@@ -526,12 +538,11 @@
     near1 = shift(after(own1, far_in0, far_in2), dx=1)
     near3 = shift(after(own3, far_in0, far_in2), dx=3)
     up2, out2 = hold_projection(value_up_weight, up_other, w_out, out_other)
-    second = (far_in0, far_in2, far1, far3)
+    block = page_pick(block, after(traded, *first), offset, 0)
+    traded = page_trade(block, 1)
+    second = (far_in0, far_in2, far1, far3, block)
     fup_other = swap_cores(after(w_up, *second))
     down_other = swap_cores(after(w_down, *second))
-    block, offset = page_block(
-        after(where, *first), partner, moved_request, moved_pages, request_latent_cache
-    )
     (hidden32,) = glue(
         flatten_kernel, "flatten", (after(hidden_in, *first),), [((n, width), jnp.float32)]
     )
@@ -539,9 +550,9 @@
     values_a = values_of([after(own0, near2), near2], up2)
     values_b = values_of([far_in0, far1], up2)
     values_c = values_of([far2, far3], up2)
-    far = project(
-        [(values_b, 0, 2 * n), (values_c, 0, 2 * n)], out2, far_shapes
-    )
+    block = page_pick(block, after(traded, far2), offset, 1)
+    values_b = after(values_b, values_a, block)
+    far = project([(values_b, 0, 2 * n), (values_c, 0, 2 * n)], out2, far_shapes)
     back1, back3 = shift(far[1], dz=-1), shift(far[3], dz=1)
     aside, back0 = shift(far[2], dx=-2), shift(far[0], dz=-1)
     values_d = values_of([after(near1, far[0]), near3], up2)
@@ -560,19 +571,18 @@
     row1, row3 = shift(normed, dx=1), shift(normed, dx=3)
     over, under = shift(normed, dz=1), shift(normed, dz=-1)
     row2 = shift(normed, dx=2)
+    traded = page_trade(after(block, normed), 2)
     far_row1, far_row3 = shift(row1, dz=1), shift(row3, dz=-1)
     far_row2 = shift(under, dx=2)
-    block = page_step(after(block, normed), offset, 0)
     near = feed([normed, row1, row2, row3], held, near_shapes)
     home2 = shift(near[2], dx=-2)
-    far = feed([after(over, near[0]), far_row1, far_row2, far_row3], held, far_shapes)
+    block = page_pick(block, after(traded, near[0]), offset, 2)
+    far = feed([after(over, near[0], block), far_row1, far_row2, far_row3], held, far_shapes)
     back1, back3 = shift(far[1], dz=-1), shift(far[3], dz=1)
     aside, back0 = shift(far[2], dx=-2), shift(far[0], dz=-1)
-    block = page_step(after(block, far[0]), offset, 1)
     fold1, fold3 = fold(near[1], back1), fold(near[3], back3)
     home1, home3 = shift(fold1, dx=-1), shift(fold3, dx=-3)
     back2 = shift(aside, dz=1)
-    block = page_step(after(block, fold1), offset, 2)
     (out,) = glue(
         finish_kernel, "finish", (residual, near[0], back0, back2, home1, home2, home3),
         [((n, width), jnp.bfloat16)],

time: 165 us -> 152 us (0.921)
  waiting for transfers between devices: 47.2 us -> 32.5 us
  local copies, waits for them, and re-layouts: 8.76 us -> 2.39 us
  starting transfers between devices: 53.7 us -> 59.5 us
  Pallas kernels: 52.1 us -> 54.9 us
    ppermute x34, waiting for transfers between devices: 44.6 us -> 26.9 us  [shift(): return lax.ppermute(value, GRID, pairs)]
    unnamed x22 -> x12, local copies, waits for them, and re-layouts: 7.97 us -> 1.6 us
    ppermute x34, starting transfers between devices: 47.6 us -> 53.4 us  [shift(): return lax.ppermute(value, GRID, pairs)]
    ppermute x3, waiting for transfers between devices: 2.62 us -> 5.52 us  [page_trade(): return lax.ppermute(block, 'dp', [(d, d ^ 1 << bit) for d in range(8)])]
  transfers between devices with their start and end apart: 42 -> 42, of which waited for: 15 -> 13; matrix products, arithmetic and copies ran while one was open for 0% -> 0% of each run, Pallas kernels for 31% -> 31%
where the time goes in v2:
time: 152 us
  starting transfers between devices  59.5 us (39%)
  Pallas kernels  54.9 us (36%)
  waiting for transfers between devices  32.5 us (21%)
  local copies, waits for them, and re-layouts  2.39 us (2%)
  between operations  2.28 us (1%)
    ppermute x34, starting transfers between devices, shift(): return lax.ppermute(value, GRID, pairs)  53.4 us
    ppermute x34, waiting for transfers between devices, shift(): return lax.ppermute(value, GRID, pairs)  26.9 us
    pallas_call x2, Pallas kernels, feed(): pl.pallas_call(functools.partial(feed_kernel, blocks=len(blocks)), in_spe...  13.5 us
    pallas_call x1, Pallas kernels, attend(): pl.pallas_call(functools.partial(attend_kernel, first_request=first), gri...  9.23 us
    pallas_call x1, Pallas kernels, hold_feed(): pl.pallas_call(hold_feed_kernel, in_specs=[HBM_SPEC, ANY_SPEC] * 3, out_s...  8.26 us
    pallas_call x2, Pallas kernels, project(): pl.pallas_call(functools.partial(project_kernel, parts=parts), in_specs=[...  6.4 us
    pallas_call x4, Pallas kernels, values_of(): pl.pallas_call(functools.partial(values_kernel, blocks=len(blocks)), in_s...  6.12 us
    pallas_call x1, Pallas kernels, hold_projection(): pl.pallas_call(hold_projection_kernel, in_specs=[HBM_SPEC, ANY_SPEC] * 2,...  5.6 us
  transfers between devices with their start and end apart: 42, of which 13 were waited for; matrix products, arithmetic and copies ran while one was open for 0% of the time, Pallas kernels for 31%

profile of v2, /device:TPU:0, one launch (start us, length us, event | category | flops | bytes accessed | tf_op | source)
XLA Modules:
  0.0 152.1 jit_solution(7334294786679988750)
XLA Ops:
  2.0 9.2 %attend.1 = (bf16[32,16,512]{2,1,0:T(8,128)(2,1)}, bf16[32,16,512]{2,1,0:T(8,128)(2,1)}, bf16[32,16,512]{2,1,0:T(8,128)(2,1)}, bf16[32,16,512]{2,1,0:T(8,128)(2,...) custom-call(s32[4]{0:T(128)} %pad_add_fusion.where_ref.ids_ref, ...), custom_call_target="tpu_custom_call" | custom-call | flops 2281701376 | bytes 12800000 | tf_op jit(solution)/shard_map/attend/pallas_call | solution.py:107
  11.2 3.1 %collective-permute-start.1 = (bf16[32,16,512]{2,1,0:T(8,128)(2,1)}, bf16[32,16,512]{2,1,0:T(8,128)(2,1)S(1)}, u32[]{:S(2)}, u32[]{:S(2)}) collective-permute-start(bf16[32,16,512]{2,1,0:T(8,128)(2,1)} %get-tuple-element.59), channel_id=1, source_target_pairs={{0,4},{1,5},{2,6},{3,7},{4,0},{5,1},{6,2},{7,3},{8,12},{9,13},{10,... | collective-permute-start | bytes 1572872 | tf_op jit(solution)/shard_map/ppermute | solution.py:40
  14.4 1.9 %collective-permute-start.2 = (bf16[32,16,512]{2,1,0:T(8,128)(2,1)}, bf16[32,16,512]{2,1,0:T(8,128)(2,1)S(1)}, u32[]{:S(2)}, u32[]{:S(2)}) collective-permute-start(bf16[32,16,512]{2,1,0:T(8,128)(2,1)} %get-tuple-element.61), channel_id=1, source_target_pairs={{0,8},{1,9},{2,10},{3,11},{4,12},{5,13},{6,14},{7,15},{8,64},{9,65... | collective-permute-start | bytes 1572872 | tf_op jit(solution)/shard_map/ppermute | solution.py:40
  16.3 2.1 %collective-permute-start.3 = (bf16[32,16,512]{2,1,0:T(8,128)(2,1)}, bf16[32,16,512]{2,1,0:T(8,128)(2,1)S(1)}, u32[]{:S(2)}, u32[]{:S(2)}) collective-permute-start(bf16[32,16,512]{2,1,0:T(8,128)(2,1)} %get-tuple-element.63), channel_id=1, source_target_pairs={{0,72},{1,73},{2,74},{3,75},{4,76},{5,77},{6,78},{7,79},{8,0},{9,1... | collective-permute-start | bytes 1572872 | tf_op jit(solution)/shard_map/ppermute | solution.py:40
  18.4 8.8 %collective-permute-done.1.refs_1_ = bf16[32,16,512]{2,1,0:T(8,128)(2,1)S(1)} collective-permute-done((bf16[32,16,512]{2,1,0:T(8,128)(2,1)}, bf16[32,16,512]{2,1,0:T(8,128)(2,1)S(1)}, u32[]{:S(2)}, u32[]{:S(2)}) %collective-permute-start.1) | collective-permute-done | bytes 524320 | tf_op jit(solution)/shard_map/ppermute | solution.py:40
  27.2 3.6 %collective-permute-done.2 = bf16[32,16,512]{2,1,0:T(8,128)(2,1)S(1)} collective-permute-done((bf16[32,16,512]{2,1,0:T(8,128)(2,1)}, bf16[32,16,512]{2,1,0:T(8,128)(2,1)S(1)}, u32[]{:S(2)}, u32[]{:S(2)}) %collective-permute-start.2) | collective-permute-done | bytes 524320 | tf_op jit(solution)/shard_map/ppermute | solution.py:40
  30.8 1.3 collective-permute-start.6
  32.1 2.0 %collective-permute-start.7 = (bf16[32,16,512]{2,1,0:T(8,128)(2,1)}, bf16[32,16,512]{2,1,0:T(8,128)(2,1)S(1)}, u32[]{:S(2)}, u32[]{:S(2)}) collective-permute-start(bf16[32,16,512]{2,1,0:T(8,128)(2,1)} %get-tuple-element.72), channel_id=1, source_target_pairs={{0,72},{1,73},{2,74},{3,75},{4,76},{5,77},{6,78},{7,79},{8,0},{9,1... | collective-permute-start | bytes 1572872 | tf_op jit(solution)/shard_map/ppermute | solution.py:40
  34.7 2.6 %collective-permute-start.13 = (bf16[32,16,512]{2,1,0:T(8,128)(2,1)S(1)}, bf16[32,16,512]{2,1,0:T(8,128)(2,1)S(1)}, u32[]{:S(2)}, u32[]{:S(2)}) collective-permute-start(bf16[32,16,512]{2,1,0:T(8,128)(2,1)S(1)} %collective-permute-done.3), channel_id=1, source_target_pairs={{0,6},{1,7},{2,0},{3,1},{4,2},{5,3},{6,4},{7,5},{8,14},{9,15},{10,... | collective-permute-start | bytes 1572872 | tf_op jit(solution)/shard_map/ppermute | solution.py:40
  38.7 2.0 %pages.1 = (bf16[2,64,576]{2,1,0:T(8,128)(2,1)S(1)}, s32[1]{0:T(128)}) custom-call(s32[4]{0:T(128)S(1)} %copy-done.2, s32[8]{0:T(128)S(1)} %bitcast.6, s32[1]{0:T(128)S(6)} %copy.16.request_ref, s32[1]{0:T(128)S(6)} %copy.17.count_ref, bf16[16,192,576]{2,1,0:T(8,128)(2,1)} %cache_ref.3), custom_call_target="tpu_custom_call" | custom-call | flops 1000 | bytes 400000 | tf_op jit(solution)/shard_map/pages/pallas_call | solution.py:449
  40.7 1.7 %collective-permute-start.10 = (bf16[2,64,576]{2,1,0:T(8,128)(2,1)S(1)}, bf16[2,64,576]{2,1,0:T(8,128)(2,1)S(1)}, u32[]{:S(2)}, u32[]{:S(2)}) collective-permute-start(bf16[2,64,576]{2,1,0:T(8,128)(2,1)S(1)} %get-tuple-element.77.mine_ref), channel_id=1, source_target_pairs={{0,16},{16,0},{32,48},{48,32},{64,80},{80,64},{96,112},{112,96},{1... | collective-permute-start | bytes 442376 | tf_op jit(solution)/shard_map/ppermute | solution.py:483
  42.4 3.7 %collective-permute-done.10.other_ref = bf16[2,64,576]{2,1,0:T(8,128)(2,1)S(1)} collective-permute-done((bf16[2,64,576]{2,1,0:T(8,128)(2,1)S(1)}, bf16[2,64,576]{2,1,0:T(8,128)(2,1)S(1)}, u32[]{:S(2)}, u32[]{:S(2)}) %collective-permute-start.10) | collective-permute-done | bytes 147488 | tf_op jit(solution)/shard_map/ppermute | solution.py:483
  46.8 1.5 collective-permute-done.9.refs_1_
  48.8 1.5 collective-permute-start.12
  50.3 3.2 %collective-permute-start.11 = (bf16[2,64,576]{2,1,0:T(8,128)(2,1)S(1)}, bf16[2,64,576]{2,1,0:T(8,128)(2,1)S(1)}, u32[]{:S(2)}, u32[]{:S(2)}) collective-permute-start(bf16[2,64,576]{2,1,0:T(8,128)(2,1)S(1)} %pick.3.mine_ref), channel_id=1, source_target_pairs={{0,32},{16,48},{32,0},{48,16},{64,96},{80,112},{96,64},{112,80},{1... | collective-permute-start | bytes 442376 | tf_op jit(solution)/shard_map/ppermute | solution.py:483
  53.5 2.3 %collective-permute-start.8 = (bf16[32,16,512]{2,1,0:T(8,128)(2,1)}, bf16[32,16,512]{2,1,0:T(8,128)(2,1)S(1)}, u32[]{:S(2)}, u32[]{:S(2)}) collective-permute-start(bf16[32,16,512]{2,1,0:T(8,128)(2,1)} %get-tuple-element.73), channel_id=1, source_target_pairs={{0,2},{1,3},{2,4},{3,5},{4,6},{5,7},{6,0},{7,1},{8,10},{9,11},{10,... | collective-permute-start | bytes 1572872 | tf_op jit(solution)/shard_map/ppermute | solution.py:40
  55.8 1.8 %collective-permute-done.11.other_ref = bf16[2,64,576]{2,1,0:T(8,128)(2,1)S(1)} collective-permute-done((bf16[2,64,576]{2,1,0:T(8,128)(2,1)S(1)}, bf16[2,64,576]{2,1,0:T(8,128)(2,1)S(1)}, u32[]{:S(2)}, u32[]{:S(2)}) %collective-permute-start.11) | collective-permute-done | bytes 147488 | tf_op jit(solution)/shard_map/ppermute | solution.py:483
  57.6 1.8 %collective-permute-start.14 = (bf16[32,16,512]{2,1,0:T(8,128)(2,1)}, bf16[32,16,512]{2,1,0:T(8,128)(2,1)S(1)}, u32[]{:S(2)}, u32[]{:S(2)}) collective-permute-start(bf16[32,16,512]{2,1,0:T(8,128)(2,1)} %get-tuple-element.86), channel_id=1, source_target_pairs={{0,6},{1,7},{2,0},{3,1},{4,2},{5,3},{6,4},{7,5},{8,14},{9,15},{10,... | collective-permute-start | bytes 1572872 | tf_op jit(solution)/shard_map/ppermute | solution.py:40
  59.4 5.6 %hold_projection.1 = (bf16[16,512,128]{2,1,0:T(8,128)(2,1)S(1)}, bf16[2048,3584]{1,0:T(8,128)(2,1)S(1)}) custom-call(bf16[8,512,128]{2,1,0:T(8,128)(2,1)} %up_own.1, bf16[8,512,128]{2,1,0:T(8,128)(2,1)S(1)} %collective-permute-done.up_other, bf16[1024,3584]{1,0:T(8,128)(2,1)} %out_own.1, bf16[1024,3584]{1,0:T(8,128)(2,1)} %collective-permute-done.4.out_other), custom_call_target="tpu_custom_call" | custom-call | bytes 17000000 | tf_op jit(solution)/shard_map/hold_projection/pallas_call | solution.py:166
  65.0 1.5 %values.4.refs_0_.refs_2_ = bf16[64,2048]{1,0:T(8,128)(2,1)S(1)} custom-call(bf16[32,16,512]{2,1,0:T(8,128)(2,1)S(1)} %copy-done, bf16[32,16,512]{2,1,0:T(8,128)(2,1)S(1)} %collective-permute-done.1.refs_1_, bf16[16,512,128]{2,1,0:T(8,128)(2,1)S(1)} %get-tuple-element.67.refs_2_), custom_call_target="tpu_custom_call" | custom-call | flops 134217728 | bytes 4000000 | tf_op jit(solution)/shard_map/values/pallas_call | solution.py:235
  66.5 1.5 %values.5.refs_0_ = bf16[64,2048]{1,0:T(8,128)(2,1)S(1)} custom-call(bf16[32,16,512]{2,1,0:T(8,128)(2,1)S(1)} %collective-permute-done.6.refs_0_, bf16[32,16,512]{2,1,0:T(8,128)(2,1)S(1)} %collective-permute-done.9.refs_1_, bf16[16,512,128]{2,1,0:T(8,128)(2,1)S(1)} %get-tuple-element.67.refs_2_), custom_call_target="tpu_custom_call" | custom-call | flops 134217728 | bytes 4000000 | tf_op jit(solution)/shard_map/values/pallas_call | solution.py:235
  68.7 1.5 %values.6.refs_1_ = bf16[64,2048]{1,0:T(8,128)(2,1)S(1)} custom-call(bf16[32,16,512]{2,1,0:T(8,128)(2,1)S(1)} %collective-permute-done.12.refs_0_, bf16[32,16,512]{2,1,0:T(8,128)(2,1)S(1)} %collective-permute-done.13.refs_1_, bf16[16,512,128]{2,1,0:T(8,128)(2,1)S(1)} %get-tuple-element.67.refs_2_), custom_call_target="tpu_custom_call" | custom-call | flops 134217728 | bytes 4000000 | tf_op jit(solution)/shard_map/values/pallas_call | solution.py:235
  70.3 3.2 %project.2 = (bf16[32,3584]{1,0:T(8,128)(2,1)S(1)}, bf16[32,3584]{1,0:T(8,128)(2,1)S(1)}, bf16[32,3584]{1,0:T(8,128)(2,1)S(1)}, bf16[32,3584]{1,0:T(8,128)(2,1)S(1)}) custom-call(bf16[64,2048]{1,0:T(8,128)(2,1)S(1)} %values.5.refs_0_, bf16[64,2048]{1,0:T(8,128)(2,1)S(1)} %values.6.refs_1_, bf16[2048,3584]{1,0:T(8,128)(2,1)S(1)} %get-tuple-element.82.refs_2_.refs_4_), custom_call_target="tpu_custom_call" | custom-call | flops 1879048192 | bytes 17000000 | tf_op jit(solution)/shard_map/project/pallas_call | solution.py:278
  73.5 1.4 collective-permute-start.18
  75.7 2.6 %collective-permute-start.16 = (bf16[32,3584]{1,0:T(8,128)(2,1)S(1)}, bf16[32,3584]{1,0:T(8,128)(2,1)S(1)}, u32[]{:S(2)}, u32[]{:S(2)}) collective-permute-start(bf16[32,3584]{1,0:T(8,128)(2,1)S(1)} %get-tuple-element.88), channel_id=1, source_target_pairs={{0,4},{1,5},{2,6},{3,7},{4,0},{5,1},{6,2},{7,3},{8,12},{9,13},{10,... | collective-permute-start | bytes 688136 | tf_op jit(solution)/shard_map/ppermute | solution.py:40
  78.3 1.5 %values.7.refs_1_.refs_3_ = bf16[64,2048]{1,0:T(8,128)(2,1)S(1)} custom-call(bf16[32,16,512]{2,1,0:T(8,128)(2,1)S(1)} %collective-permute-done.8.refs_0_, bf16[32,16,512]{2,1,0:T(8,128)(2,1)S(1)} %collective-permute-done.14.refs_1_, bf16[16,512,128]{2,1,0:T(8,128)(2,1)S(1)} %get-tuple-element.67.refs_2_), custom_call_target="tpu_custom_call" | custom-call | flops 134217728 | bytes 4000000 | tf_op jit(solution)/shard_map/values/pallas_call | solution.py:235
  79.8 3.2 %project.3 = (f32[32,3584]{1,0:T(8,128)S(1)}, f32[32,3584]{1,0:T(8,128)S(1)}, bf16[32,3584]{1,0:T(8,128)(2,1)S(1)}, f32[32,3584]{1,0:T(8,128)S(1)}) custom-call(bf16[64,2048]{1,0:T(8,128)(2,1)S(1)} %values.4.refs_0_.refs_2_, bf16[64,2048]{1,0:T(8,128)(2,1)S(1)} %values.7.refs_1_.refs_3_, bf16[64,2048]{1,0:T(8,128)(2,1)S(1)} %values.4.refs_0_.refs_2_, ...), custom_call_target="tpu_custom_call" | custom-call | flops 1879048192 | bytes 17000000 | tf_op jit(solution)/shard_map/project/pallas_call | solution.py:278
  83.0 2.6 %collective-permute-start.15 = (bf16[32,3584]{1,0:T(8,128)(2,1)S(1)}, bf16[32,3584]{1,0:T(8,128)(2,1)S(1)}, u32[]{:S(2)}, u32[]{:S(2)}) collective-permute-start(bf16[32,3584]{1,0:T(8,128)(2,1)S(1)} %get-tuple-element.83), channel_id=1, source_target_pairs={{0,72},{1,73},{2,74},{3,75},{4,76},{5,77},{6,78},{7,79},{8,0},{9,1... | collective-permute-start | bytes 688136 | tf_op jit(solution)/shard_map/ppermute | solution.py:40
  86.5 1.2 collective-permute-start.23
  89.0 1.6 %copy-done.4 = bf16[640,3584]{1,0:T(8,128)(2,1)} copy-done((bf16[640,3584]{1,0:T(8,128)(2,1)}, bf16[640,3584]{1,0:T(8,128)(2,1)S(1)}, u32[]{:S(2)}) %copy-start.4) | copy-done | bytes 4587544
  90.5 8.3 %hold_feed.1 = (bf16[5,3584,256]{2,1,0:T(8,128)(2,1)S(1)}, bf16[5,3584,256]{2,1,0:T(8,128)(2,1)S(1)}, bf16[1280,3584]{1,0:T(8,128)(2,1)S(1)}) custom-call(bf16[3584,640]{1,0:T(8,128)(2,1)} %g0, bf16[3584,640]{1,0:T(8,128)(2,1)} %collective-permute-done.5.g1, bf16[3584,640]{1,0:T(8,128)(2,1)} %u0.1, bf16[3584,640]{1,0:T(8,128)(2,1)S(1)} %collective-permute-done.21.u1, ...), custom_call_target="tpu_custom_call" | custom-call | bytes 27500000 | tf_op jit(solution)/shard_map/hold_feed/pallas_call | solution.py:197
  99.9 3.2 %collective-permute-start.26 = (bf16[32,3584]{1,0:T(8,128)(2,1)S(1)}, bf16[32,3584]{1,0:T(8,128)(2,1)S(1)}, u32[]{:S(2)}, u32[]{:S(2)}) collective-permute-start(bf16[32,3584]{1,0:T(8,128)(2,1)S(1)} %get-tuple-element.100.refs_0_), channel_id=1, source_target_pairs={{0,4},{1,5},{2,6},{3,7},{4,0},{5,1},{6,2},{7,3},{8,12},{9,13},{10,... | collective-permute-start | bytes 688136 | tf_op jit(solution)/shard_map/ppermute | solution.py:40
  103.1 3.2 %collective-permute-start.31 = (bf16[32,3584]{1,0:T(8,128)(2,1)S(1)}, bf16[32,3584]{1,0:T(8,128)(2,1)S(1)}, u32[]{:S(2)}, u32[]{:S(2)}) collective-permute-start(bf16[32,3584]{1,0:T(8,128)(2,1)S(1)} %get-tuple-element.100.refs_0_), channel_id=1, source_target_pairs={{0,72},{1,73},{2,74},{3,75},{4,76},{5,77},{6,78},{7,79},{8,0},{9,1... | collective-permute-start | bytes 688136 | tf_op jit(solution)/shard_map/ppermute | solution.py:40
  107.0 4.6 %collective-permute-done.25.refs_1_ = bf16[32,3584]{1,0:T(8,128)(2,1)S(1)} collective-permute-done((bf16[32,3584]{1,0:T(8,128)(2,1)S(1)}, bf16[32,3584]{1,0:T(8,128)(2,1)S(1)}, u32[]{:S(2)}, u32[]{:S(2)}) %collective-permute-start.25) | collective-permute-done | bytes 229408 | tf_op jit(solution)/shard_map/ppermute | solution.py:40
  112.6 1.1 collective-permute-start.32
  113.6 1.2 collective-permute-done.27.refs_3_
  114.8 2.5 %collective-permute-start.33 = (bf16[32,3584]{1,0:T(8,128)(2,1)S(1)}, bf16[32,3584]{1,0:T(8,128)(2,1)S(1)}, u32[]{:S(2)}, u32[]{:S(2)}) collective-permute-start(bf16[32,3584]{1,0:T(8,128)(2,1)S(1)} %collective-permute-done.27.refs_3_), channel_id=1, source_target_pairs={{0,72},{1,73},{2,74},{3,75},{4,76},{5,77},{6,78},{7,79},{8,0},{9,1... | collective-permute-start | bytes 688136 | tf_op jit(solution)/shard_map/ppermute | solution.py:40
  117.2 6.8 %feed.2 = (f32[32,3584]{1,0:T(8,128)S(1)}, f32[32,3584]{1,0:T(8,128)S(1)}, bf16[32,3584]{1,0:T(8,128)(2,1)S(1)}, f32[32,3584]{1,0:T(8,128)S(1)}) custom-call(bf16[32,3584]{1,0:T(8,128)(2,1)S(1)} %get-tuple-element.100.refs_0_, bf16[32,3584]{1,0:T(8,128)(2,1)S(1)} %collective-permute-done.25.refs_1_, bf16[32,3584]{1,0:T(8,128)(2,1)S(1)} %collective-permute-done.26.refs_2_, ...), custom_call_target="tpu_custom_call" | custom-call | flops 3523215360 | bytes 28000000 | tf_op jit(solution)/shard_map/feed/pallas_call | solution.py:323
  124.0 1.3 pick.5
  125.4 6.8 %feed.3 = (bf16[32,3584]{1,0:T(8,128)(2,1)S(1)}, bf16[32,3584]{1,0:T(8,128)(2,1)S(1)}, bf16[32,3584]{1,0:T(8,128)(2,1)S(1)}, bf16[32,3584]{1,0:T(8,128)(2,1)S(1)}) custom-call(bf16[32,3584]{1,0:T(8,128)(2,1)S(1)} %collective-permute-done.28.refs_0_, bf16[32,3584]{1,0:T(8,128)(2,1)S(1)} %collective-permute-done.30.refs_1_, ...), custom_call_target="tpu_custom_call" | custom-call | flops 3523215360 | bytes 28000000 | tf_op jit(solution)/shard_map/feed/pallas_call | solution.py:323
  132.1 1.2 collective-permute-start.37
  133.3 2.2 %collective-permute-start.35 = (bf16[32,3584]{1,0:T(8,128)(2,1)S(1)}, bf16[32,3584]{1,0:T(8,128)(2,1)S(1)}, u32[]{:S(2)}, u32[]{:S(2)}) collective-permute-start(bf16[32,3584]{1,0:T(8,128)(2,1)S(1)} %get-tuple-element.108), channel_id=1, source_target_pairs={{0,4},{1,5},{2,6},{3,7},{4,0},{5,1},{6,2},{7,3},{8,12},{9,13},{10,... | collective-permute-start | bytes 688136 | tf_op jit(solution)/shard_map/ppermute | solution.py:40
  135.8 2.0 %collective-permute-start.39 = (bf16[32,3584]{1,0:T(8,128)(2,1)S(1)}, bf16[32,3584]{1,0:T(8,128)(2,1)S(1)}, u32[]{:S(2)}, u32[]{:S(2)}) collective-permute-start(bf16[32,3584]{1,0:T(8,128)(2,1)S(1)} %get-tuple-element.111), channel_id=1, source_target_pairs={{0,4},{1,5},{2,6},{3,7},{4,0},{5,1},{6,2},{7,3},{8,12},{9,13},{10,... | collective-permute-start | bytes 688136 | tf_op jit(solution)/shard_map/ppermute | solution.py:40
  137.8 2.3 %collective-permute-start.34 = (bf16[32,3584]{1,0:T(8,128)(2,1)S(1)}, bf16[32,3584]{1,0:T(8,128)(2,1)S(1)}, u32[]{:S(2)}, u32[]{:S(2)}) collective-permute-start(bf16[32,3584]{1,0:T(8,128)(2,1)S(1)} %get-tuple-element.107), channel_id=1, source_target_pairs={{0,72},{1,73},{2,74},{3,75},{4,76},{5,77},{6,78},{7,79},{8,0},{9,1... | collective-permute-start | bytes 688136 | tf_op jit(solution)/shard_map/ppermute | solution.py:40
  140.6 1.5 %collective-permute-start.38 = (bf16[32,3584]{1,0:T(8,128)(2,1)S(1)}, bf16[32,3584]{1,0:T(8,128)(2,1)S(1)}, u32[]{:S(2)}, u32[]{:S(2)}) collective-permute-start(bf16[32,3584]{1,0:T(8,128)(2,1)S(1)} %fold.6), channel_id=1, source_target_pairs={{0,6},{1,7},{2,0},{3,1},{4,2},{5,3},{6,4},{7,5},{8,14},{9,15},{10,... | collective-permute-start | bytes 688136 | tf_op jit(solution)/shard_map/ppermute | solution.py:40
  143.4 2.2 %collective-permute-start.41 = (bf16[32,3584]{1,0:T(8,128)(2,1)S(1)}, bf16[32,3584]{1,0:T(8,128)(2,1)S(1)}, u32[]{:S(2)}, u32[]{:S(2)}) collective-permute-start(bf16[32,3584]{1,0:T(8,128)(2,1)S(1)} %fold.7), channel_id=1, source_target_pairs={{0,2},{1,3},{2,4},{3,5},{4,6},{5,7},{6,0},{7,1},{8,10},{9,11},{10,... | collective-permute-start | bytes 688136 | tf_op jit(solution)/shard_map/ppermute | solution.py:40
  145.6 3.7 %collective-permute-done.36.refs_1_ = bf16[32,3584]{1,0:T(8,128)(2,1)S(1)} collective-permute-done((bf16[32,3584]{1,0:T(8,128)(2,1)S(1)}, bf16[32,3584]{1,0:T(8,128)(2,1)S(1)}, u32[]{:S(2)}, u32[]{:S(2)}) %collective-permute-start.36) | collective-permute-done | bytes 229408 | tf_op jit(solution)/shard_map/ppermute | solution.py:40
  149.3 1.8 %collective-permute-done.41.refs_4_ = bf16[32,3584]{1,0:T(8,128)(2,1)S(1)} collective-permute-done((bf16[32,3584]{1,0:T(8,128)(2,1)S(1)}, bf16[32,3584]{1,0:T(8,128)(2,1)S(1)}, u32[]{:S(2)}, u32[]{:S(2)}) %collective-permute-start.41) | collective-permute-done | bytes 229408 | tf_op jit(solution)/shard_map/ppermute | solution.py:40
  (73 shorter events, 12.4 us)
Async XLA Ops:
  0.6 38.1 %copy-start.3 = (s32[8,1]{0,1:T(1,128)S(1)}, s32[8,1]{0,1:T(1,128)}, u32[]{:S(2)}) copy-start(s32[8,1]{0,1:T(1,128)} %param.25) | copy-start | bytes 100
  0.6 30.2 %collective-permute-start.4 = (bf16[1024,3584]{1,0:T(8,128)(2,1)}, bf16[1024,3584]{1,0:T(8,128)(2,1)}, u32[]{:S(2)}, u32[]{:S(2)}) collective-permute-start(bf16[1024,3584]{1,0:T(8,128)(2,1)} %out_own.1), channel_id=1, source_target_pairs={{0,1},{1,0},{2,3},{3,2},{4,5},{5,4},{6,7},{7,6},{8,9},{9,8},{10,11... | collective-permute-start | bytes 22020104 | tf_op jit(solution)/shard_map/ppermute | solution.py:44
  0.7 30.1 %collective-permute-start.5 = (bf16[3584,640]{1,0:T(8,128)(2,1)}, bf16[3584,640]{1,0:T(8,128)(2,1)}, u32[]{:S(2)}, u32[]{:S(2)}) collective-permute-start(bf16[3584,640]{1,0:T(8,128)(2,1)} %g0), channel_id=1, source_target_pairs={{0,1},{1,0},{2,3},{3,2},{4,5},{5,4},{6,7},{7,6},{8,9},{9,8},{10,11... | collective-permute-start | bytes 13762568 | tf_op jit(solution)/shard_map/ppermute | solution.py:44
  1.2 10.0 %collective-permute-start = (bf16[8,512,128]{2,1,0:T(8,128)(2,1)}, bf16[8,512,128]{2,1,0:T(8,128)(2,1)S(1)}, u32[]{:S(2)}, u32[]{:S(2)}) collective-permute-start(bf16[8,512,128]{2,1,0:T(8,128)(2,1)} %up_own.1), channel_id=1, source_target_pairs={{0,1},{1,0},{2,3},{3,2},{4,5},{5,4},{6,7},{7,6},{8,9},{9,8},{10,11... | collective-permute-start | bytes 3145736 | tf_op jit(solution)/shard_map/ppermute | solution.py:44
  2.0 36.7 %copy-start.2 = (s32[4]{0:T(128)S(1)}, s32[4]{0:T(128)}, u32[]{:S(2)}) copy-start(s32[4]{0:T(128)} %pad_add_fusion.where_ref.ids_ref) | copy-start | bytes 52
  11.2 16.0 %collective-permute-start.1 = (bf16[32,16,512]{2,1,0:T(8,128)(2,1)}, bf16[32,16,512]{2,1,0:T(8,128)(2,1)S(1)}, u32[]{:S(2)}, u32[]{:S(2)}) collective-permute-start(bf16[32,16,512]{2,1,0:T(8,128)(2,1)} %get-tuple-element.59), channel_id=1, source_target_pairs={{0,4},{1,5},{2,6},{3,7},{4,0},{5,1},{6,2},{7,3},{8,12},{9,13},{10,... | collective-permute-start | bytes 1572872 | tf_op jit(solution)/shard_map/ppermute | solution.py:40
  14.4 16.5 %collective-permute-start.2 = (bf16[32,16,512]{2,1,0:T(8,128)(2,1)}, bf16[32,16,512]{2,1,0:T(8,128)(2,1)S(1)}, u32[]{:S(2)}, u32[]{:S(2)}) collective-permute-start(bf16[32,16,512]{2,1,0:T(8,128)(2,1)} %get-tuple-element.61), channel_id=1, source_target_pairs={{0,8},{1,9},{2,10},{3,11},{4,12},{5,13},{6,14},{7,15},{8,64},{9,65... | collective-permute-start | bytes 1572872 | tf_op jit(solution)/shard_map/ppermute | solution.py:40
  16.3 14.6 %collective-permute-start.3 = (bf16[32,16,512]{2,1,0:T(8,128)(2,1)}, bf16[32,16,512]{2,1,0:T(8,128)(2,1)S(1)}, u32[]{:S(2)}, u32[]{:S(2)}) collective-permute-start(bf16[32,16,512]{2,1,0:T(8,128)(2,1)} %get-tuple-element.63), channel_id=1, source_target_pairs={{0,72},{1,73},{2,74},{3,75},{4,76},{5,77},{6,78},{7,79},{8,0},{9,1... | collective-permute-start | bytes 1572872 | tf_op jit(solution)/shard_map/ppermute | solution.py:40
  30.8 16.0 %collective-permute-start.6 = (bf16[32,16,512]{2,1,0:T(8,128)(2,1)}, bf16[32,16,512]{2,1,0:T(8,128)(2,1)S(1)}, u32[]{:S(2)}, u32[]{:S(2)}) collective-permute-start(bf16[32,16,512]{2,1,0:T(8,128)(2,1)} %get-tuple-element.70), channel_id=1, source_target_pairs={{0,8},{1,9},{2,10},{3,11},{4,12},{5,13},{6,14},{7,15},{8,64},{9,65... | collective-permute-start | bytes 1572872 | tf_op jit(solution)/shard_map/ppermute | solution.py:40
  32.1 14.7 %collective-permute-start.7 = (bf16[32,16,512]{2,1,0:T(8,128)(2,1)}, bf16[32,16,512]{2,1,0:T(8,128)(2,1)S(1)}, u32[]{:S(2)}, u32[]{:S(2)}) collective-permute-start(bf16[32,16,512]{2,1,0:T(8,128)(2,1)} %get-tuple-element.72), channel_id=1, source_target_pairs={{0,72},{1,73},{2,74},{3,75},{4,76},{5,77},{6,78},{7,79},{8,0},{9,1... | collective-permute-start | bytes 1572872 | tf_op jit(solution)/shard_map/ppermute | solution.py:40
  34.1 14.1 %collective-permute-start.9 = (bf16[32,16,512]{2,1,0:T(8,128)(2,1)S(1)}, bf16[32,16,512]{2,1,0:T(8,128)(2,1)S(1)}, u32[]{:S(2)}, u32[]{:S(2)}) collective-permute-start(bf16[32,16,512]{2,1,0:T(8,128)(2,1)S(1)} %collective-permute-done.2), channel_id=1, source_target_pairs={{0,2},{1,3},{2,4},{3,5},{4,6},{5,7},{6,0},{7,1},{8,10},{9,11},{10,... | collective-permute-start | bytes 1572872 | tf_op jit(solution)/shard_map/ppermute | solution.py:40
  34.7 13.5 %collective-permute-start.13 = (bf16[32,16,512]{2,1,0:T(8,128)(2,1)S(1)}, bf16[32,16,512]{2,1,0:T(8,128)(2,1)S(1)}, u32[]{:S(2)}, u32[]{:S(2)}) collective-permute-start(bf16[32,16,512]{2,1,0:T(8,128)(2,1)S(1)} %collective-permute-done.3), channel_id=1, source_target_pairs={{0,6},{1,7},{2,0},{3,1},{4,2},{5,3},{6,4},{7,5},{8,14},{9,15},{10,... | collective-permute-start | bytes 1572872 | tf_op jit(solution)/shard_map/ppermute | solution.py:40
  40.7 5.4 %collective-permute-start.10 = (bf16[2,64,576]{2,1,0:T(8,128)(2,1)S(1)}, bf16[2,64,576]{2,1,0:T(8,128)(2,1)S(1)}, u32[]{:S(2)}, u32[]{:S(2)}) collective-permute-start(bf16[2,64,576]{2,1,0:T(8,128)(2,1)S(1)} %get-tuple-element.77.mine_ref), channel_id=1, source_target_pairs={{0,16},{16,0},{32,48},{48,32},{64,80},{80,64},{96,112},{112,96},{1... | collective-permute-start | bytes 442376 | tf_op jit(solution)/shard_map/ppermute | solution.py:483
  48.3 39.5 %collective-permute-start.21 = (bf16[3584,640]{1,0:T(8,128)(2,1)}, bf16[3584,640]{1,0:T(8,128)(2,1)S(1)}, u32[]{:S(2)}, u32[]{:S(2)}) collective-permute-start(bf16[3584,640]{1,0:T(8,128)(2,1)} %u0.1), channel_id=1, source_target_pairs={{0,1},{1,0},{2,3},{3,2},{4,5},{5,4},{6,7},{7,6},{8,9},{9,8},{10,11... | collective-permute-start | bytes 13762568 | tf_op jit(solution)/shard_map/ppermute | solution.py:44
  48.3 40.2 %collective-permute-start.22 = (bf16[640,3584]{1,0:T(8,128)(2,1)}, bf16[640,3584]{1,0:T(8,128)(2,1)S(1)}, u32[]{:S(2)}, u32[]{:S(2)}) collective-permute-start(bf16[640,3584]{1,0:T(8,128)(2,1)} %d0.1), channel_id=1, source_target_pairs={{0,1},{1,0},{2,3},{3,2},{4,5},{5,4},{6,7},{7,6},{8,9},{9,8},{10,11... | collective-permute-start | bytes 13762568 | tf_op jit(solution)/shard_map/ppermute | solution.py:44
  48.8 19.3 %collective-permute-start.12 = (bf16[32,16,512]{2,1,0:T(8,128)(2,1)S(1)}, bf16[32,16,512]{2,1,0:T(8,128)(2,1)S(1)}, u32[]{:S(2)}, u32[]{:S(2)}) collective-permute-start(bf16[32,16,512]{2,1,0:T(8,128)(2,1)S(1)} %collective-permute-done.7), channel_id=1, source_target_pairs={{0,4},{1,5},{2,6},{3,7},{4,0},{5,1},{6,2},{7,3},{8,12},{9,13},{10,... | collective-permute-start | bytes 1572872 | tf_op jit(solution)/shard_map/ppermute | solution.py:40
  50.3 7.3 %collective-permute-start.11 = (bf16[2,64,576]{2,1,0:T(8,128)(2,1)S(1)}, bf16[2,64,576]{2,1,0:T(8,128)(2,1)S(1)}, u32[]{:S(2)}, u32[]{:S(2)}) collective-permute-start(bf16[2,64,576]{2,1,0:T(8,128)(2,1)S(1)} %pick.3.mine_ref), channel_id=1, source_target_pairs={{0,32},{16,48},{32,0},{48,16},{64,96},{80,112},{96,64},{112,80},{1... | collective-permute-start | bytes 442376 | tf_op jit(solution)/shard_map/ppermute | solution.py:483
  53.5 21.9 %collective-permute-start.8 = (bf16[32,16,512]{2,1,0:T(8,128)(2,1)}, bf16[32,16,512]{2,1,0:T(8,128)(2,1)S(1)}, u32[]{:S(2)}, u32[]{:S(2)}) collective-permute-start(bf16[32,16,512]{2,1,0:T(8,128)(2,1)} %get-tuple-element.73), channel_id=1, source_target_pairs={{0,2},{1,3},{2,4},{3,5},{4,6},{5,7},{6,0},{7,1},{8,10},{9,11},{10,... | collective-permute-start | bytes 1572872 | tf_op jit(solution)/shard_map/ppermute | solution.py:40
  57.6 18.1 %collective-permute-start.14 = (bf16[32,16,512]{2,1,0:T(8,128)(2,1)}, bf16[32,16,512]{2,1,0:T(8,128)(2,1)S(1)}, u32[]{:S(2)}, u32[]{:S(2)}) collective-permute-start(bf16[32,16,512]{2,1,0:T(8,128)(2,1)} %get-tuple-element.86), channel_id=1, source_target_pairs={{0,6},{1,7},{2,0},{3,1},{4,2},{5,3},{6,4},{7,5},{8,14},{9,15},{10,... | collective-permute-start | bytes 1572872 | tf_op jit(solution)/shard_map/ppermute | solution.py:40
  59.4 5.6 %copy-start = (bf16[32,16,512]{2,1,0:T(8,128)(2,1)S(1)}, bf16[32,16,512]{2,1,0:T(8,128)(2,1)}, u32[]{:S(2)}) copy-start(bf16[32,16,512]{2,1,0:T(8,128)(2,1)} %get-tuple-element.66.refs_0_) | copy-start | bytes 1572868
  73.5 9.5 %collective-permute-start.18 = (bf16[32,3584]{1,0:T(8,128)(2,1)S(1)}, bf16[32,3584]{1,0:T(8,128)(2,1)S(1)}, u32[]{:S(2)}, u32[]{:S(2)}) collective-permute-start(bf16[32,3584]{1,0:T(8,128)(2,1)S(1)} %get-tuple-element.90), channel_id=1, source_target_pairs={{0,72},{1,73},{2,74},{3,75},{4,76},{5,77},{6,78},{7,79},{8,0},{9,1... | collective-permute-start | bytes 688136 | tf_op jit(solution)/shard_map/ppermute | solution.py:40
  75.4 10.3 %collective-permute-start.20 = (bf16[32,3584]{1,0:T(8,128)(2,1)S(1)}, bf16[32,3584]{1,0:T(8,128)(2,1)S(1)}, u32[]{:S(2)}, u32[]{:S(2)}) collective-permute-start(bf16[32,3584]{1,0:T(8,128)(2,1)S(1)} %get-tuple-element.92), channel_id=1, source_target_pairs={{0,8},{1,9},{2,10},{3,11},{4,12},{5,13},{6,14},{7,15},{8,64},{9,65... | collective-permute-start | bytes 688136 | tf_op jit(solution)/shard_map/ppermute | solution.py:40
  75.7 10.8 %collective-permute-start.16 = (bf16[32,3584]{1,0:T(8,128)(2,1)S(1)}, bf16[32,3584]{1,0:T(8,128)(2,1)S(1)}, u32[]{:S(2)}, u32[]{:S(2)}) collective-permute-start(bf16[32,3584]{1,0:T(8,128)(2,1)S(1)} %get-tuple-element.88), channel_id=1, source_target_pairs={{0,4},{1,5},{2,6},{3,7},{4,0},{5,1},{6,2},{7,3},{8,12},{9,13},{10,... | collective-permute-start | bytes 688136 | tf_op jit(solution)/shard_map/ppermute | solution.py:40
  79.8 9.0 %copy-start.5 = (f32[3584]{0:T(1024)S(1)}, f32[3584]{0:T(1024)}, u32[]{:S(2)}) copy-start(f32[3584]{0:T(1024)} %param.21) | copy-start | bytes 43012
  79.8 9.0 %copy-start.1 = (bf16[16,2,3584]{2,1,0:T(2,128)(2,1)S(1)}, bf16[16,2,3584]{2,1,0:T(2,128)(2,1)}, u32[]{:S(2)}) copy-start(bf16[16,2,3584]{2,1,0:T(2,128)(2,1)} %hidden_ref) | copy-start | bytes 688132
  83.0 15.8 %collective-permute-start.15 = (bf16[32,3584]{1,0:T(8,128)(2,1)S(1)}, bf16[32,3584]{1,0:T(8,128)(2,1)S(1)}, u32[]{:S(2)}, u32[]{:S(2)}) collective-permute-start(bf16[32,3584]{1,0:T(8,128)(2,1)S(1)} %get-tuple-element.83), channel_id=1, source_target_pairs={{0,72},{1,73},{2,74},{3,75},{4,76},{5,77},{6,78},{7,79},{8,0},{9,1... | collective-permute-start | bytes 688136 | tf_op jit(solution)/shard_map/ppermute | solution.py:40
  85.7 13.1 %collective-permute-start.19 = (bf16[32,3584]{1,0:T(8,128)(2,1)S(1)}, bf16[32,3584]{1,0:T(8,128)(2,1)S(1)}, u32[]{:S(2)}, u32[]{:S(2)}) collective-permute-start(bf16[32,3584]{1,0:T(8,128)(2,1)S(1)} %fold.4), channel_id=1, source_target_pairs={{0,6},{1,7},{2,0},{3,1},{4,2},{5,3},{6,4},{7,5},{8,14},{9,15},{10,... | collective-permute-start | bytes 688136 | tf_op jit(solution)/shard_map/ppermute | solution.py:40
  86.5 12.3 %collective-permute-start.23 = (bf16[32,3584]{1,0:T(8,128)(2,1)S(1)}, bf16[32,3584]{1,0:T(8,128)(2,1)S(1)}, u32[]{:S(2)}, u32[]{:S(2)}) collective-permute-start(bf16[32,3584]{1,0:T(8,128)(2,1)S(1)} %get-tuple-element.98), channel_id=1, source_target_pairs={{0,4},{1,5},{2,6},{3,7},{4,0},{5,1},{6,2},{7,3},{8,12},{9,13},{10,... | collective-permute-start | bytes 688136 | tf_op jit(solution)/shard_map/ppermute | solution.py:40
  87.7 11.1 %collective-permute-start.17 = (bf16[32,3584]{1,0:T(8,128)(2,1)S(1)}, bf16[32,3584]{1,0:T(8,128)(2,1)S(1)}, u32[]{:S(2)}, u32[]{:S(2)}) collective-permute-start(bf16[32,3584]{1,0:T(8,128)(2,1)S(1)} %collective-permute-done.16), channel_id=1, source_target_pairs={{0,8},{1,9},{2,10},{3,11},{4,12},{5,13},{6,14},{7,15},{8,64},{9,65... | collective-permute-start | bytes 688136 | tf_op jit(solution)/shard_map/ppermute | solution.py:40
  88.4 2.1 %copy-start.4 = (bf16[640,3584]{1,0:T(8,128)(2,1)}, bf16[640,3584]{1,0:T(8,128)(2,1)S(1)}, u32[]{:S(2)}) copy-start(bf16[640,3584]{1,0:T(8,128)(2,1)S(1)} %collective-permute-done.22.d1) | copy-start | bytes 13762564
  88.4 10.4 %collective-permute-start.24 = (bf16[32,3584]{1,0:T(8,128)(2,1)S(1)}, bf16[32,3584]{1,0:T(8,128)(2,1)S(1)}, u32[]{:S(2)}, u32[]{:S(2)}) collective-permute-start(bf16[32,3584]{1,0:T(8,128)(2,1)S(1)} %fold.5), channel_id=1, source_target_pairs={{0,2},{1,3},{2,4},{3,5},{4,6},{5,7},{6,0},{7,1},{8,10},{9,11},{10,... | collective-permute-start | bytes 688136 | tf_op jit(solution)/shard_map/ppermute | solution.py:40
  99.3 12.3 %collective-permute-start.25 = (bf16[32,3584]{1,0:T(8,128)(2,1)S(1)}, bf16[32,3584]{1,0:T(8,128)(2,1)S(1)}, u32[]{:S(2)}, u32[]{:S(2)}) collective-permute-start(bf16[32,3584]{1,0:T(8,128)(2,1)S(1)} %get-tuple-element.100.refs_0_), channel_id=1, source_target_pairs={{0,2},{1,3},{2,4},{3,5},{4,6},{5,7},{6,0},{7,1},{8,10},{9,11},{10,... | collective-permute-start | bytes 688136 | tf_op jit(solution)/shard_map/ppermute | solution.py:40
  99.9 11.7 %collective-permute-start.26 = (bf16[32,3584]{1,0:T(8,128)(2,1)S(1)}, bf16[32,3584]{1,0:T(8,128)(2,1)S(1)}, u32[]{:S(2)}, u32[]{:S(2)}) collective-permute-start(bf16[32,3584]{1,0:T(8,128)(2,1)S(1)} %get-tuple-element.100.refs_0_), channel_id=1, source_target_pairs={{0,4},{1,5},{2,6},{3,7},{4,0},{5,1},{6,2},{7,3},{8,12},{9,13},{10,... | collective-permute-start | bytes 688136 | tf_op jit(solution)/shard_map/ppermute | solution.py:40
  103.1 9.5 %collective-permute-start.31 = (bf16[32,3584]{1,0:T(8,128)(2,1)S(1)}, bf16[32,3584]{1,0:T(8,128)(2,1)S(1)}, u32[]{:S(2)}, u32[]{:S(2)}) collective-permute-start(bf16[32,3584]{1,0:T(8,128)(2,1)S(1)} %get-tuple-element.100.refs_0_), channel_id=1, source_target_pairs={{0,72},{1,73},{2,74},{3,75},{4,76},{5,77},{6,78},{7,79},{8,0},{9,1... | collective-permute-start | bytes 688136 | tf_op jit(solution)/shard_map/ppermute | solution.py:40
  106.3 8.5 %collective-permute-start.27 = (bf16[32,3584]{1,0:T(8,128)(2,1)S(1)}, bf16[32,3584]{1,0:T(8,128)(2,1)S(1)}, u32[]{:S(2)}, u32[]{:S(2)}) collective-permute-start(bf16[32,3584]{1,0:T(8,128)(2,1)S(1)} %get-tuple-element.100.refs_0_), channel_id=1, source_target_pairs={{0,6},{1,7},{2,0},{3,1},{4,2},{5,3},{6,4},{7,5},{8,14},{9,15},{10,... | collective-permute-start | bytes 688136 | tf_op jit(solution)/shard_map/ppermute | solution.py:40
  107.0 18.4 %collective-permute-start.28 = (bf16[32,3584]{1,0:T(8,128)(2,1)S(1)}, bf16[32,3584]{1,0:T(8,128)(2,1)S(1)}, u32[]{:S(2)}, u32[]{:S(2)}) collective-permute-start(bf16[32,3584]{1,0:T(8,128)(2,1)S(1)} %get-tuple-element.100.refs_0_), channel_id=1, source_target_pairs={{0,8},{1,9},{2,10},{3,11},{4,12},{5,13},{6,14},{7,15},{8,64},{9,65... | collective-permute-start | bytes 688136 | tf_op jit(solution)/shard_map/ppermute | solution.py:40
  111.6 12.4 %collective-permute-start.29 = (bf16[2,64,576]{2,1,0:T(8,128)(2,1)S(1)}, bf16[2,64,576]{2,1,0:T(8,128)(2,1)S(1)}, u32[]{:S(2)}, u32[]{:S(2)}) collective-permute-start(bf16[2,64,576]{2,1,0:T(8,128)(2,1)S(1)} %pick.4.mine_ref), channel_id=1, source_target_pairs={{0,64},{16,80},{32,96},{48,112},{64,0},{80,16},{96,32},{112,48},{1... | collective-permute-start | bytes 442376 | tf_op jit(solution)/shard_map/ppermute | solution.py:483
  111.6 13.8 %collective-permute-start.30 = (bf16[32,3584]{1,0:T(8,128)(2,1)S(1)}, bf16[32,3584]{1,0:T(8,128)(2,1)S(1)}, u32[]{:S(2)}, u32[]{:S(2)}) collective-permute-start(bf16[32,3584]{1,0:T(8,128)(2,1)S(1)} %collective-permute-done.25.refs_1_), channel_id=1, source_target_pairs={{0,8},{1,9},{2,10},{3,11},{4,12},{5,13},{6,14},{7,15},{8,64},{9,65... | collective-permute-start | bytes 688136 | tf_op jit(solution)/shard_map/ppermute | solution.py:40
  112.6 12.8 %collective-permute-start.32 = (bf16[32,3584]{1,0:T(8,128)(2,1)S(1)}, bf16[32,3584]{1,0:T(8,128)(2,1)S(1)}, u32[]{:S(2)}, u32[]{:S(2)}) collective-permute-start(bf16[32,3584]{1,0:T(8,128)(2,1)S(1)} %collective-permute-done.31), channel_id=1, source_target_pairs={{0,4},{1,5},{2,6},{3,7},{4,0},{5,1},{6,2},{7,3},{8,12},{9,13},{10,... | collective-permute-start | bytes 688136 | tf_op jit(solution)/shard_map/ppermute | solution.py:40
  114.8 10.6 %collective-permute-start.33 = (bf16[32,3584]{1,0:T(8,128)(2,1)S(1)}, bf16[32,3584]{1,0:T(8,128)(2,1)S(1)}, u32[]{:S(2)}, u32[]{:S(2)}) collective-permute-start(bf16[32,3584]{1,0:T(8,128)(2,1)S(1)} %collective-permute-done.27.refs_3_), channel_id=1, source_target_pairs={{0,72},{1,73},{2,74},{3,75},{4,76},{5,77},{6,78},{7,79},{8,0},{9,1... | collective-permute-start | bytes 688136 | tf_op jit(solution)/shard_map/ppermute | solution.py:40
  132.1 8.3 %collective-permute-start.37 = (bf16[32,3584]{1,0:T(8,128)(2,1)S(1)}, bf16[32,3584]{1,0:T(8,128)(2,1)S(1)}, u32[]{:S(2)}, u32[]{:S(2)}) collective-permute-start(bf16[32,3584]{1,0:T(8,128)(2,1)S(1)} %get-tuple-element.110), channel_id=1, source_target_pairs={{0,72},{1,73},{2,74},{3,75},{4,76},{5,77},{6,78},{7,79},{8,0},{9,1... | collective-permute-start | bytes 688136 | tf_op jit(solution)/shard_map/ppermute | solution.py:40
  133.3 8.8 %collective-permute-start.35 = (bf16[32,3584]{1,0:T(8,128)(2,1)S(1)}, bf16[32,3584]{1,0:T(8,128)(2,1)S(1)}, u32[]{:S(2)}, u32[]{:S(2)}) collective-permute-start(bf16[32,3584]{1,0:T(8,128)(2,1)S(1)} %get-tuple-element.108), channel_id=1, source_target_pairs={{0,4},{1,5},{2,6},{3,7},{4,0},{5,1},{6,2},{7,3},{8,12},{9,13},{10,... | collective-permute-start | bytes 688136 | tf_op jit(solution)/shard_map/ppermute | solution.py:40
  135.6 7.8 %collective-permute-start.40 = (bf16[32,3584]{1,0:T(8,128)(2,1)S(1)}, bf16[32,3584]{1,0:T(8,128)(2,1)S(1)}, u32[]{:S(2)}, u32[]{:S(2)}) collective-permute-start(bf16[32,3584]{1,0:T(8,128)(2,1)S(1)} %get-tuple-element.113), channel_id=1, source_target_pairs={{0,8},{1,9},{2,10},{3,11},{4,12},{5,13},{6,14},{7,15},{8,64},{9,65... | collective-permute-start | bytes 688136 | tf_op jit(solution)/shard_map/ppermute | solution.py:40
  135.8 9.8 %collective-permute-start.39 = (bf16[32,3584]{1,0:T(8,128)(2,1)S(1)}, bf16[32,3584]{1,0:T(8,128)(2,1)S(1)}, u32[]{:S(2)}, u32[]{:S(2)}) collective-permute-start(bf16[32,3584]{1,0:T(8,128)(2,1)S(1)} %get-tuple-element.111), channel_id=1, source_target_pairs={{0,4},{1,5},{2,6},{3,7},{4,0},{5,1},{6,2},{7,3},{8,12},{9,13},{10,... | collective-permute-start | bytes 688136 | tf_op jit(solution)/shard_map/ppermute | solution.py:40
  137.8 7.8 %collective-permute-start.34 = (bf16[32,3584]{1,0:T(8,128)(2,1)S(1)}, bf16[32,3584]{1,0:T(8,128)(2,1)S(1)}, u32[]{:S(2)}, u32[]{:S(2)}) collective-permute-start(bf16[32,3584]{1,0:T(8,128)(2,1)S(1)} %get-tuple-element.107), channel_id=1, source_target_pairs={{0,72},{1,73},{2,74},{3,75},{4,76},{5,77},{6,78},{7,79},{8,0},{9,1... | collective-permute-start | bytes 688136 | tf_op jit(solution)/shard_map/ppermute | solution.py:40
  140.6 8.8 %collective-permute-start.38 = (bf16[32,3584]{1,0:T(8,128)(2,1)S(1)}, bf16[32,3584]{1,0:T(8,128)(2,1)S(1)}, u32[]{:S(2)}, u32[]{:S(2)}) collective-permute-start(bf16[32,3584]{1,0:T(8,128)(2,1)S(1)} %fold.6), channel_id=1, source_target_pairs={{0,6},{1,7},{2,0},{3,1},{4,2},{5,3},{6,4},{7,5},{8,14},{9,15},{10,... | collective-permute-start | bytes 688136 | tf_op jit(solution)/shard_map/ppermute | solution.py:40
  142.1 7.2 %collective-permute-start.36 = (bf16[32,3584]{1,0:T(8,128)(2,1)S(1)}, bf16[32,3584]{1,0:T(8,128)(2,1)S(1)}, u32[]{:S(2)}, u32[]{:S(2)}) collective-permute-start(bf16[32,3584]{1,0:T(8,128)(2,1)S(1)} %collective-permute-done.35), channel_id=1, source_target_pairs={{0,8},{1,9},{2,10},{3,11},{4,12},{5,13},{6,14},{7,15},{8,64},{9,65... | collective-permute-start | bytes 688136 | tf_op jit(solution)/shard_map/ppermute | solution.py:40
  143.4 7.7 %collective-permute-start.41 = (bf16[32,3584]{1,0:T(8,128)(2,1)S(1)}, bf16[32,3584]{1,0:T(8,128)(2,1)S(1)}, u32[]{:S(2)}, u32[]{:S(2)}) collective-permute-start(bf16[32,3584]{1,0:T(8,128)(2,1)S(1)} %fold.7), channel_id=1, source_target_pairs={{0,2},{1,3},{2,4},{3,5},{4,6},{5,7},{6,0},{7,1},{8,10},{9,11},{10,... | collective-permute-start | bytes 688136 | tf_op jit(solution)/shard_map/ppermute | solution.py:40

commit v3 on v2

--- a/solution.py
+++ b/solution.py
@@ -15,7 +15,7 @@
 N_Y = 4
 GRID = ("dp", "tp")
 T_PAD = 208
-GROUP = 4
+GROUP = 8
 
 score_scale = 192.0 ** (-0.5)
 masked_score = -1e30
@@ -44,7 +44,7 @@
     return lax.ppermute(value, "tp", [(t, t ^ 1) for t in range(16)])
 
 
-def attend_kernel(where_ref, lens_ref, q_ref, cache_ref, fresh_ref, *rest, first_request):
+def attend_kernel(lens_ref, q_ref, cache_ref, fresh_ref, *rest, first_request):
     *outs, keys, rows = rest
     i = pl.program_id(0)
     reqs, steps, width, heads = q_ref.shape
@@ -58,7 +58,8 @@
     position = lax.broadcasted_iota(jnp.int32, (total, steps * heads), 0)
     column = lax.broadcasted_iota(jnp.int32, (total, steps * heads), 1)
     fresh_ok = (position >= capacity) & (position - capacity <= column // heads)
-    z, x, c = where_ref[0], where_ref[1], where_ref[2]
+    t = lax.axis_index("tp")
+    z, x, c = t // 8, lax.rem(t // 2, N_X), lax.rem(t, 2)
     group = keys.shape[0]
     for first in range(0, reqs, group):
         scores, probs = [], []
@@ -98,23 +99,23 @@
                         out[at + s] = jnp.concatenate(picked, axis=0).astype(jnp.bfloat16)
 
 
-def attend(where, lengths, queries, cache, fresh, first, count):
+def attend(lengths, queries, cache, fresh, first, count):
     reqs, steps, width, heads = queries.shape
     capacity = cache.shape[1]
-    part = 4
+    part = 8
     n = count * steps
     base = first // part
     return pl.pallas_call(
         functools.partial(attend_kernel, first_request=first),
         grid_spec=pltpu.PrefetchScalarGridSpec(
-            num_scalar_prefetch=2,
+            num_scalar_prefetch=1,
             grid=(count // part,),
             in_specs=[
-                pl.BlockSpec((part, steps, width, heads), lambda i, w, l: (base + i, 0, 0, 0)),
-                pl.BlockSpec((part, capacity, width), lambda i, w, l: (base + i, 0, 0)),
-                pl.BlockSpec((part, steps, width), lambda i, w, l: (base + i, 0, 0)),
+                pl.BlockSpec((part, steps, width, heads), lambda i, l: (base + i, 0, 0, 0)),
+                pl.BlockSpec((part, capacity, width), lambda i, l: (base + i, 0, 0)),
+                pl.BlockSpec((part, steps, width), lambda i, l: (base + i, 0, 0)),
             ],
-            out_specs=[pl.BlockSpec((n, 16, LATENT_WIDTH), lambda i, w, l: (0, 0, 0))] * (2 * N_X),
+            out_specs=[pl.BlockSpec((n, 16, LATENT_WIDTH), lambda i, l: (0, 0, 0))] * (2 * N_X),
             scratch_shapes=[
                 pltpu.VMEM((GROUP, T_PAD, width), jnp.bfloat16),
                 pltpu.VMEM((GROUP, steps * heads, LATENT_WIDTH), jnp.float32),
@@ -128,7 +129,7 @@
             transcendentals=n * heads * 256,
         ),
         name="attend",
-    )(where, lengths, queries, cache, fresh)
+    )(lengths, queries, cache, fresh)
 
 
 def vmem_out(shape, dtype=jnp.bfloat16):
@@ -436,24 +437,24 @@
     column_loop(own_ref.shape[1], body)
 
 
-def page_kernel(ids_ref, partner_ref, request_ref, count_ref, cache_ref, block_ref, offset_ref):
-    dp = ids_ref[3]
+def page_kernel(partner_ref, request_ref, count_ref, cache_ref, block_ref, offset_ref):
+    dp = lax.axis_index("dp")
     offset_ref[0] = jnp.bitwise_xor(partner_ref[dp], dp)
     for k in range(MIG_MAX):
         rows = cache_ref[0, k * PAGE : (k + 1) * PAGE, :]
         block_ref[k] = jnp.where(k < count_ref[0], rows, jnp.zeros_like(rows))
 
 
-def page_block(ids, partner, moved_request, moved_pages, cache):
+def page_block(partner, moved_request, moved_pages, cache):
     width = cache.shape[2]
     return pl.pallas_call(
         page_kernel,
         grid_spec=pltpu.PrefetchScalarGridSpec(
-            num_scalar_prefetch=4,
+            num_scalar_prefetch=3,
             grid=(1,),
-            in_specs=[pl.BlockSpec((1,) + cache.shape[1:], lambda i, ids, p, r, c: (r[0], 0, 0))],
+            in_specs=[pl.BlockSpec((1,) + cache.shape[1:], lambda i, p, r, c: (r[0], 0, 0))],
             out_specs=[
-                pl.BlockSpec((MIG_MAX, PAGE, width), lambda i, ids, p, r, c: (0, 0, 0)),
+                pl.BlockSpec((MIG_MAX, PAGE, width), lambda i, p, r, c: (0, 0, 0)),
                 pl.BlockSpec(memory_space=pltpu.SMEM),
             ],
         ),
@@ -464,7 +465,7 @@
         compiler_params=SMALL,
         cost_estimate=pl.CostEstimate(flops=1_000, bytes_accessed=400_000, transcendentals=0),
         name="pages",
-    )(ids, partner.reshape(-1), moved_request, moved_pages, in_hbm(cache))
+    )(partner.reshape(-1), moved_request, moved_pages, in_hbm(cache))
 
 
 def pick_kernel(offset_ref, mine_ref, other_ref, out_ref, *, bit):
@@ -513,12 +514,10 @@
 ):
     req_here, steps_here, width = hidden_in.shape
     n = req_here * steps_here
-    t = lax.axis_index("tp")
-    where = jnp.stack([t // 8, (t // 2) % N_X, t % 2, lax.axis_index("dp")])
     up_other, out_other, gate_other = swap_cores(value_up_weight), swap_cores(w_out), swap_cores(w_gate)
     turned = jnp.swapaxes(queries, 2, 3)
     own0, own1, own2, own3, go0, go1, go2, go3 = attend(
-        where, lengths, turned, request_latent_cache, incoming_keys, 0, req_here
+        lengths, turned, request_latent_cache, incoming_keys, 0, req_here
     )
     near_shapes = [(n, jnp.float32), (n, jnp.float32), (n, jnp.bfloat16), (n, jnp.float32)]
     far_shapes = [(n, jnp.bfloat16)] * N_X
@@ -526,20 +525,20 @@
     go1, go3, own2 = after(go1, up_other), after(go3, up_other), after(own2, up_other)
     far_in1, far_in3 = shift(go1, dz=1), shift(go3, dz=-1)
     near2 = shift(own2, dx=2)
+    up2, out2 = hold_projection(value_up_weight, up_other, w_out, out_other)
     block, offset = page_block(
-        after(where, go1), partner, moved_request, moved_pages, request_latent_cache
+        partner, after(moved_request, out2), moved_pages, request_latent_cache
     )
     traded = page_trade(block, 0)
-    first = (near2, far_in1, far_in3, out_other, gate_other)
+    first = (near2, far_in1, far_in3, out2, gate_other, traded)
     far1 = shift(after(far_in1, *first), dx=1)
     far3 = shift(after(far_in3, *first), dx=3)
     far_in2, far_in0 = shift(after(go2, *first), dz=-1), shift(after(go0, *first), dz=1)
     far2 = shift(far_in2, dx=2)
     near1 = shift(after(own1, far_in0, far_in2), dx=1)
     near3 = shift(after(own3, far_in0, far_in2), dx=3)
-    up2, out2 = hold_projection(value_up_weight, up_other, w_out, out_other)
     block = page_pick(block, after(traded, *first), offset, 0)
-    traded = page_trade(block, 1)
+    block = page_pick(block, after(page_trade(block, 1), far_in0, far_in2), offset, 1)
     second = (far_in0, far_in2, far1, far3, block)
     fup_other = swap_cores(after(w_up, *second))
     down_other = swap_cores(after(w_down, *second))
@@ -547,14 +546,14 @@
         flatten_kernel, "flatten", (after(hidden_in, *first),), [((n, width), jnp.float32)]
     )
     gain = norm_gain.reshape(1, width)
-    values_a = values_of([after(own0, near2), near2], up2)
+    values_a = values_of([after(own0, far_in0), near2], up2)
     values_b = values_of([far_in0, far1], up2)
     values_c = values_of([far2, far3], up2)
-    block = page_pick(block, after(traded, far2), offset, 1)
-    values_b = after(values_b, values_a, block)
+    block = page_pick(block, after(page_trade(block, 2), far2), offset, 2)
+    values_b = after(values_b, values_a, block, fup_other, down_other)
     far = project([(values_b, 0, 2 * n), (values_c, 0, 2 * n)], out2, far_shapes)
     back1, back3 = shift(far[1], dz=-1), shift(far[3], dz=1)
-    aside, back0 = shift(far[2], dx=-2), shift(far[0], dz=-1)
+    aside = shift(far[2], dx=-2)
     values_d = values_of([after(near1, far[0]), near3], up2)
     near = project(
         [(values_a, 0, n), (values_d, 0, n), (values_a, n, n), (values_d, n, n)], out2, near_shapes
@@ -563,6 +562,7 @@
     back2 = shift(aside, dz=1)
     fold1, fold3 = fold(near[1], back1), fold(near[3], back3)
     home1, home3 = shift(fold1, dx=-1), shift(fold3, dx=-3)
+    back0 = shift(after(far[0], fold1, fold3), dz=-1)
     held = hold_feed(after(w_gate, fold1, fold3), gate_other, w_up, fup_other, w_down, down_other)
     residual, normed = norm(
         near[0], [back0, back2, after(home1, held[0]), home2, home3], hidden32, gain
@@ -571,13 +571,11 @@
     row1, row3 = shift(normed, dx=1), shift(normed, dx=3)
     over, under = shift(normed, dz=1), shift(normed, dz=-1)
     row2 = shift(normed, dx=2)
-    traded = page_trade(after(block, normed), 2)
     far_row1, far_row3 = shift(row1, dz=1), shift(row3, dz=-1)
     far_row2 = shift(under, dx=2)
     near = feed([normed, row1, row2, row3], held, near_shapes)
     home2 = shift(near[2], dx=-2)
-    block = page_pick(block, after(traded, near[0]), offset, 2)
-    far = feed([after(over, near[0], block), far_row1, far_row2, far_row3], held, far_shapes)
+    far = feed([after(over, near[0]), far_row1, far_row2, far_row3], held, far_shapes)
     back1, back3 = shift(far[1], dz=-1), shift(far[3], dz=1)
     aside, back0 = shift(far[2], dx=-2), shift(far[0], dz=-1)
     fold1, fold3 = fold(near[1], back1), fold(near[3], back3)

time: 152 us -> 151 us (level)
  local copies, waits for them, and re-layouts: 2.39 us -> 0.85 us
    ppermute x34, waiting for transfers between devices: 26.9 us -> 22.9 us  [shift(): return lax.ppermute(value, GRID, pairs)]
    ppermute x3, waiting for transfers between devices: 5.52 us -> 8.84 us  [page_trade(): return lax.ppermute(block, 'dp', [(d, d ^ 1 << bit) for d in range(8)])]
    unnamed x12 -> x24, local copies, waits for them, and re-layouts: 1.6 us -> 0.06 us
  transfers between devices with their start and end apart: 42 -> 42, of which waited for: 13 -> 15; matrix products, arithmetic and copies ran while one was open for 0% -> 0% of each run, Pallas kernels for 31% -> 31%
where the time goes in v3:
time: 151 us
  starting transfers between devices  60.5 us (40%)
  Pallas kernels  54.7 us (36%)
  waiting for transfers between devices  32.8 us (22%)
  between operations  2.41 us (2%)
    ppermute x34, starting transfers between devices, shift(): return lax.ppermute(value, GRID, pairs)  53.2 us
    ppermute x34, waiting for transfers between devices, shift(): return lax.ppermute(value, GRID, pairs)  22.9 us
    pallas_call x2, Pallas kernels, feed(): pl.pallas_call(functools.partial(feed_kernel, blocks=len(blocks)), in_spe...  13.5 us
    ppermute x3, waiting for transfers between devices, page_trade(): return lax.ppermute(block, 'dp', [(d, d ^ 1 << bit) for d in range(8)])  8.84 us
    pallas_call x1, Pallas kernels, attend(): pl.pallas_call(functools.partial(attend_kernel, first_request=first), gri...  8.32 us
    pallas_call x1, Pallas kernels, hold_feed(): pl.pallas_call(hold_feed_kernel, in_specs=[HBM_SPEC, ANY_SPEC] * 3, out_s...  8.27 us
    pallas_call x2, Pallas kernels, project(): pl.pallas_call(functools.partial(project_kernel, parts=parts), in_specs=[...  6.39 us
    pallas_call x1, Pallas kernels, hold_projection(): pl.pallas_call(hold_projection_kernel, in_specs=[HBM_SPEC, ANY_SPEC] * 2,...  6.29 us
  transfers between devices with their start and end apart: 42, of which 15 were waited for; matrix products, arithmetic and copies ran while one was open for 0% of the time, Pallas kernels for 31%

profile of v3, /device:TPU:0, one launch (start us, length us, event | category | flops | bytes accessed | tf_op | source)
XLA Modules:
  0.0 151.2 jit_solution(17126562403489317163)
XLA Ops:
  1.3 8.3 %attend.1 = (bf16[32,16,512]{2,1,0:T(8,128)(2,1)}, bf16[32,16,512]{2,1,0:T(8,128)(2,1)}, bf16[32,16,512]{2,1,0:T(8,128)(2,1)}, bf16[32,16,512]{2,1,0:T(8,128)(2,...) custom-call(s32[16]{0:T(128)} %lens_ref.1, ...), custom_call_target="tpu_custom_call" | custom-call | flops 2281701376 | bytes 12800000 | tf_op jit(solution)/shard_map/attend/pallas_call | solution.py:108
  9.6 1.1 collective-permute-done.up_other
  10.7 4.1 %collective-permute-start.3 = (bf16[32,16,512]{2,1,0:T(8,128)(2,1)}, bf16[32,16,512]{2,1,0:T(8,128)(2,1)S(1)}, u32[]{:S(2)}, u32[]{:S(2)}) collective-permute-start(bf16[32,16,512]{2,1,0:T(8,128)(2,1)} %get-tuple-element.63), channel_id=1, source_target_pairs={{0,72},{1,73},{2,74},{3,75},{4,76},{5,77},{6,78},{7,79},{8,0},{9,1... | collective-permute-start | bytes 1572872 | tf_op jit(solution)/shard_map/ppermute | solution.py:40
  14.8 3.0 %collective-permute-start.1 = (bf16[32,16,512]{2,1,0:T(8,128)(2,1)}, bf16[32,16,512]{2,1,0:T(8,128)(2,1)S(1)}, u32[]{:S(2)}, u32[]{:S(2)}) collective-permute-start(bf16[32,16,512]{2,1,0:T(8,128)(2,1)} %get-tuple-element.59), channel_id=1, source_target_pairs={{0,4},{1,5},{2,6},{3,7},{4,0},{5,1},{6,2},{7,3},{8,12},{9,13},{10,... | collective-permute-start | bytes 1572872 | tf_op jit(solution)/shard_map/ppermute | solution.py:40
  19.2 2.0 %pages.1 = (bf16[2,64,576]{2,1,0:T(8,128)(2,1)S(1)}, s32[1]{0:T(128)}) custom-call(s32[8]{0:T(128)S(1)} %bitcast.2, s32[1]{0:T(128)S(6)} %copy.16.request_ref, s32[1]{0:T(128)S(6)} %copy.17.count_ref, bf16[16,192,576]{2,1,0:T(8,128)(2,1)} %cache_ref.3), custom_call_target="tpu_custom_call" | custom-call | flops 1000 | bytes 400000 | tf_op jit(solution)/shard_map/pages/pallas_call | solution.py:450
  21.3 1.7 %collective-permute-start.6 = (bf16[2,64,576]{2,1,0:T(8,128)(2,1)S(1)}, bf16[2,64,576]{2,1,0:T(8,128)(2,1)S(1)}, u32[]{:S(2)}, u32[]{:S(2)}) collective-permute-start(bf16[2,64,576]{2,1,0:T(8,128)(2,1)S(1)} %get-tuple-element.66.mine_ref), channel_id=1, source_target_pairs={{0,16},{16,0},{32,48},{48,32},{64,80},{80,64},{96,112},{112,96},{1... | collective-permute-start | bytes 442376 | tf_op jit(solution)/shard_map/ppermute | solution.py:484
  23.0 6.3 %hold_projection.1 = (bf16[16,512,128]{2,1,0:T(8,128)(2,1)S(1)}, bf16[2048,3584]{1,0:T(8,128)(2,1)S(1)}) custom-call(bf16[8,512,128]{2,1,0:T(8,128)(2,1)} %up_own.1, bf16[8,512,128]{2,1,0:T(8,128)(2,1)S(1)} %collective-permute-done.up_other, bf16[1024,3584]{1,0:T(8,128)(2,1)} %out_own.1, bf16[1024,3584]{1,0:T(8,128)(2,1)} %collective-permute-done.4.out_other), custom_call_target="tpu_custom_call" | custom-call | bytes 17000000 | tf_op jit(solution)/shard_map/hold_projection/pallas_call | solution.py:167
  29.3 0.9 collective-permute-done.2
  30.5 3.2 %collective-permute-start.8 = (bf16[32,16,512]{2,1,0:T(8,128)(2,1)S(1)}, bf16[32,16,512]{2,1,0:T(8,128)(2,1)S(1)}, u32[]{:S(2)}, u32[]{:S(2)}) collective-permute-start(bf16[32,16,512]{2,1,0:T(8,128)(2,1)S(1)} %copy-done.6), channel_id=1, source_target_pairs={{0,72},{1,73},{2,74},{3,75},{4,76},{5,77},{6,78},{7,79},{8,0},{9,1... | collective-permute-start | bytes 1572872 | tf_op jit(solution)/shard_map/ppermute | solution.py:40
  33.7 1.5 collective-permute-start.10
  35.2 1.7 %collective-permute-start.14 = (bf16[32,16,512]{2,1,0:T(8,128)(2,1)S(1)}, bf16[32,16,512]{2,1,0:T(8,128)(2,1)S(1)}, u32[]{:S(2)}, u32[]{:S(2)}) collective-permute-start(bf16[32,16,512]{2,1,0:T(8,128)(2,1)S(1)} %collective-permute-done.3), channel_id=1, source_target_pairs={{0,6},{1,7},{2,0},{3,1},{4,2},{5,3},{6,4},{7,5},{8,14},{9,15},{10,... | collective-permute-start | bytes 1572872 | tf_op jit(solution)/shard_map/ppermute | solution.py:40
  37.6 3.3 %collective-permute-start.11 = (bf16[2,64,576]{2,1,0:T(8,128)(2,1)S(1)}, bf16[2,64,576]{2,1,0:T(8,128)(2,1)S(1)}, u32[]{:S(2)}, u32[]{:S(2)}) collective-permute-start(bf16[2,64,576]{2,1,0:T(8,128)(2,1)S(1)} %pick.3.mine_ref), channel_id=1, source_target_pairs={{0,32},{16,48},{32,0},{48,16},{64,96},{80,112},{96,64},{112,80},{1... | collective-permute-start | bytes 442376 | tf_op jit(solution)/shard_map/ppermute | solution.py:484
  40.9 3.6 %collective-permute-done.11.other_ref = bf16[2,64,576]{2,1,0:T(8,128)(2,1)S(1)} collective-permute-done((bf16[2,64,576]{2,1,0:T(8,128)(2,1)S(1)}, bf16[2,64,576]{2,1,0:T(8,128)(2,1)S(1)}, u32[]{:S(2)}, u32[]{:S(2)}) %collective-permute-start.11) | collective-permute-done | bytes 147488 | tf_op jit(solution)/shard_map/ppermute | solution.py:484
  45.4 2.0 %collective-permute-done.10.refs_1_ = bf16[32,16,512]{2,1,0:T(8,128)(2,1)S(1)} collective-permute-done((bf16[32,16,512]{2,1,0:T(8,128)(2,1)S(1)}, bf16[32,16,512]{2,1,0:T(8,128)(2,1)S(1)}, u32[]{:S(2)}, u32[]{:S(2)}) %collective-permute-start.10) | collective-permute-done | bytes 524320 | tf_op jit(solution)/shard_map/ppermute | solution.py:40
  48.0 2.6 %collective-permute-start.13 = (bf16[32,16,512]{2,1,0:T(8,128)(2,1)S(1)}, bf16[32,16,512]{2,1,0:T(8,128)(2,1)S(1)}, u32[]{:S(2)}, u32[]{:S(2)}) collective-permute-start(bf16[32,16,512]{2,1,0:T(8,128)(2,1)S(1)} %collective-permute-done.8), channel_id=1, source_target_pairs={{0,4},{1,5},{2,6},{3,7},{4,0},{5,1},{6,2},{7,3},{8,12},{9,13},{10,... | collective-permute-start | bytes 1572872 | tf_op jit(solution)/shard_map/ppermute | solution.py:40
  50.7 1.1 collective-permute-start.12
  51.8 1.1 collective-permute-start.9
  52.9 5.2 %collective-permute-done.12.other_ref = bf16[2,64,576]{2,1,0:T(8,128)(2,1)S(1)} collective-permute-done((bf16[2,64,576]{2,1,0:T(8,128)(2,1)S(1)}, bf16[2,64,576]{2,1,0:T(8,128)(2,1)S(1)}, u32[]{:S(2)}, u32[]{:S(2)}) %collective-permute-start.12) | collective-permute-done | bytes 147488 | tf_op jit(solution)/shard_map/ppermute | solution.py:484
  58.1 1.4 collective-permute-start.17
  59.6 1.5 %values.5.refs_0_ = bf16[64,2048]{1,0:T(8,128)(2,1)S(1)} custom-call(bf16[32,16,512]{2,1,0:T(8,128)(2,1)S(1)} %collective-permute-done.7.refs_0_, bf16[32,16,512]{2,1,0:T(8,128)(2,1)S(1)} %collective-permute-done.10.refs_1_, bf16[16,512,128]{2,1,0:T(8,128)(2,1)S(1)} %get-tuple-element.72.refs_2_), custom_call_target="tpu_custom_call" | custom-call | flops 134217728 | bytes 4000000 | tf_op jit(solution)/shard_map/values/pallas_call | solution.py:236
  61.1 1.5 %values.4.refs_0_.refs_2_ = bf16[64,2048]{1,0:T(8,128)(2,1)S(1)} custom-call(bf16[32,16,512]{2,1,0:T(8,128)(2,1)S(1)} %copy-done, bf16[32,16,512]{2,1,0:T(8,128)(2,1)S(1)} %collective-permute-done.1.refs_1_, bf16[16,512,128]{2,1,0:T(8,128)(2,1)S(1)} %get-tuple-element.72.refs_2_), custom_call_target="tpu_custom_call" | custom-call | flops 134217728 | bytes 4000000 | tf_op jit(solution)/shard_map/values/pallas_call | solution.py:236
  62.7 1.7 %collective-permute-done.13.refs_0_ = bf16[32,16,512]{2,1,0:T(8,128)(2,1)S(1)} collective-permute-done((bf16[32,16,512]{2,1,0:T(8,128)(2,1)S(1)}, bf16[32,16,512]{2,1,0:T(8,128)(2,1)S(1)}, u32[]{:S(2)}, u32[]{:S(2)}) %collective-permute-start.13) | collective-permute-done | bytes 524320 | tf_op jit(solution)/shard_map/ppermute | solution.py:40
  64.4 1.3 pick.5
  65.7 1.5 %values.6.refs_1_ = bf16[64,2048]{1,0:T(8,128)(2,1)S(1)} custom-call(bf16[32,16,512]{2,1,0:T(8,128)(2,1)S(1)} %collective-permute-done.13.refs_0_, bf16[32,16,512]{2,1,0:T(8,128)(2,1)S(1)} %collective-permute-done.14.refs_1_, bf16[16,512,128]{2,1,0:T(8,128)(2,1)S(1)} %get-tuple-element.72.refs_2_), custom_call_target="tpu_custom_call" | custom-call | flops 134217728 | bytes 4000000 | tf_op jit(solution)/shard_map/values/pallas_call | solution.py:236
  67.2 3.2 %project.2 = (bf16[32,3584]{1,0:T(8,128)(2,1)S(1)}, bf16[32,3584]{1,0:T(8,128)(2,1)S(1)}, bf16[32,3584]{1,0:T(8,128)(2,1)S(1)}, bf16[32,3584]{1,0:T(8,128)(2,1)S(1)}) custom-call(bf16[64,2048]{1,0:T(8,128)(2,1)S(1)} %values.5.refs_0_, bf16[64,2048]{1,0:T(8,128)(2,1)S(1)} %values.6.refs_1_, bf16[2048,3584]{1,0:T(8,128)(2,1)S(1)} %get-tuple-element.64.refs_2_.refs_4_), custom_call_target="tpu_custom_call" | custom-call | flops 1879048192 | bytes 17000000 | tf_op jit(solution)/shard_map/project/pallas_call | solution.py:279
  70.5 1.7 %collective-permute-start.18 = (bf16[32,3584]{1,0:T(8,128)(2,1)S(1)}, bf16[32,3584]{1,0:T(8,128)(2,1)S(1)}, u32[]{:S(2)}, u32[]{:S(2)}) collective-permute-start(bf16[32,3584]{1,0:T(8,128)(2,1)S(1)} %get-tuple-element.92), channel_id=1, source_target_pairs={{0,72},{1,73},{2,74},{3,75},{4,76},{5,77},{6,78},{7,79},{8,0},{9,1... | collective-permute-start | bytes 688136 | tf_op jit(solution)/shard_map/ppermute | solution.py:40
  72.7 2.6 %collective-permute-start.21 = (bf16[32,3584]{1,0:T(8,128)(2,1)S(1)}, bf16[32,3584]{1,0:T(8,128)(2,1)S(1)}, u32[]{:S(2)}, u32[]{:S(2)}) collective-permute-start(bf16[32,3584]{1,0:T(8,128)(2,1)S(1)} %get-tuple-element.96), channel_id=1, source_target_pairs={{0,4},{1,5},{2,6},{3,7},{4,0},{5,1},{6,2},{7,3},{8,12},{9,13},{10,... | collective-permute-start | bytes 688136 | tf_op jit(solution)/shard_map/ppermute | solution.py:40
  75.4 1.5 %values.7.refs_1_.refs_3_ = bf16[64,2048]{1,0:T(8,128)(2,1)S(1)} custom-call(bf16[32,16,512]{2,1,0:T(8,128)(2,1)S(1)} %collective-permute-done.9.refs_0_, bf16[32,16,512]{2,1,0:T(8,128)(2,1)S(1)} %collective-permute-done.17.refs_1_, bf16[16,512,128]{2,1,0:T(8,128)(2,1)S(1)} %get-tuple-element.72.refs_2_), custom_call_target="tpu_custom_call" | custom-call | flops 134217728 | bytes 4000000 | tf_op jit(solution)/shard_map/values/pallas_call | solution.py:236
  76.9 3.2 %project.3 = (f32[32,3584]{1,0:T(8,128)S(1)}, f32[32,3584]{1,0:T(8,128)S(1)}, bf16[32,3584]{1,0:T(8,128)(2,1)S(1)}, f32[32,3584]{1,0:T(8,128)S(1)}) custom-call(bf16[64,2048]{1,0:T(8,128)(2,1)S(1)} %values.4.refs_0_.refs_2_, bf16[64,2048]{1,0:T(8,128)(2,1)S(1)} %values.7.refs_1_.refs_3_, bf16[64,2048]{1,0:T(8,128)(2,1)S(1)} %values.4.refs_0_.refs_2_, ...), custom_call_target="tpu_custom_call" | custom-call | flops 1879048192 | bytes 17000000 | tf_op jit(solution)/shard_map/project/pallas_call | solution.py:279
  80.1 2.1 %collective-permute-start.24 = (bf16[32,3584]{1,0:T(8,128)(2,1)S(1)}, bf16[32,3584]{1,0:T(8,128)(2,1)S(1)}, u32[]{:S(2)}, u32[]{:S(2)}) collective-permute-start(bf16[32,3584]{1,0:T(8,128)(2,1)S(1)} %get-tuple-element.100), channel_id=1, source_target_pairs={{0,4},{1,5},{2,6},{3,7},{4,0},{5,1},{6,2},{7,3},{8,12},{9,13},{10,... | collective-permute-start | bytes 688136 | tf_op jit(solution)/shard_map/ppermute | solution.py:40
  82.3 1.8 %collective-permute-start.23 = (bf16[32,3584]{1,0:T(8,128)(2,1)S(1)}, bf16[32,3584]{1,0:T(8,128)(2,1)S(1)}, u32[]{:S(2)}, u32[]{:S(2)}) collective-permute-start(bf16[32,3584]{1,0:T(8,128)(2,1)S(1)} %fold.4), channel_id=1, source_target_pairs={{0,6},{1,7},{2,0},{3,1},{4,2},{5,3},{6,4},{7,5},{8,14},{9,15},{10,... | collective-permute-start | bytes 688136 | tf_op jit(solution)/shard_map/ppermute | solution.py:40
  84.5 2.5 %collective-permute-start.20 = (bf16[32,3584]{1,0:T(8,128)(2,1)S(1)}, bf16[32,3584]{1,0:T(8,128)(2,1)S(1)}, u32[]{:S(2)}, u32[]{:S(2)}) collective-permute-start(bf16[32,3584]{1,0:T(8,128)(2,1)S(1)} %get-tuple-element.95), channel_id=1, source_target_pairs={{0,72},{1,73},{2,74},{3,75},{4,76},{5,77},{6,78},{7,79},{8,0},{9,1... | collective-permute-start | bytes 688136 | tf_op jit(solution)/shard_map/ppermute | solution.py:40
  87.2 8.3 %hold_feed.1 = (bf16[5,3584,256]{2,1,0:T(8,128)(2,1)S(1)}, bf16[5,3584,256]{2,1,0:T(8,128)(2,1)S(1)}, bf16[1280,3584]{1,0:T(8,128)(2,1)S(1)}) custom-call(bf16[3584,640]{1,0:T(8,128)(2,1)} %g0, bf16[3584,640]{1,0:T(8,128)(2,1)} %collective-permute-done.5.g1, bf16[3584,640]{1,0:T(8,128)(2,1)} %u0.1, bf16[3584,640]{1,0:T(8,128)(2,1)S(1)} %collective-permute-done.15.u1, ...), custom_call_target="tpu_custom_call" | custom-call | bytes 27500000 | tf_op jit(solution)/shard_map/hold_feed/pallas_call | solution.py:198
  95.9 3.3 %collective-permute-start.31 = (bf16[32,3584]{1,0:T(8,128)(2,1)S(1)}, bf16[32,3584]{1,0:T(8,128)(2,1)S(1)}, u32[]{:S(2)}, u32[]{:S(2)}) collective-permute-start(bf16[32,3584]{1,0:T(8,128)(2,1)S(1)} %get-tuple-element.102.refs_0_), channel_id=1, source_target_pairs={{0,72},{1,73},{2,74},{3,75},{4,76},{5,77},{6,78},{7,79},{8,0},{9,1... | collective-permute-start | bytes 688136 | tf_op jit(solution)/shard_map/ppermute | solution.py:40
  99.2 3.2 %collective-permute-start.28 = (bf16[32,3584]{1,0:T(8,128)(2,1)S(1)}, bf16[32,3584]{1,0:T(8,128)(2,1)S(1)}, u32[]{:S(2)}, u32[]{:S(2)}) collective-permute-start(bf16[32,3584]{1,0:T(8,128)(2,1)S(1)} %get-tuple-element.102.refs_0_), channel_id=1, source_target_pairs={{0,6},{1,7},{2,0},{3,1},{4,2},{5,3},{6,4},{7,5},{8,14},{9,15},{10,... | collective-permute-start | bytes 688136 | tf_op jit(solution)/shard_map/ppermute | solution.py:40
  102.4 1.5 collective-permute-start.27
  103.9 2.1 %collective-permute-start.32 = (bf16[32,3584]{1,0:T(8,128)(2,1)S(1)}, bf16[32,3584]{1,0:T(8,128)(2,1)S(1)}, u32[]{:S(2)}, u32[]{:S(2)}) collective-permute-start(bf16[32,3584]{1,0:T(8,128)(2,1)S(1)} %collective-permute-done.31), channel_id=1, source_target_pairs={{0,4},{1,5},{2,6},{3,7},{4,0},{5,1},{6,2},{7,3},{8,12},{9,13},{10,... | collective-permute-start | bytes 688136 | tf_op jit(solution)/shard_map/ppermute | solution.py:40
  105.9 9.2 %collective-permute-done.28.refs_3_ = bf16[32,3584]{1,0:T(8,128)(2,1)S(1)} collective-permute-done((bf16[32,3584]{1,0:T(8,128)(2,1)S(1)}, bf16[32,3584]{1,0:T(8,128)(2,1)S(1)}, u32[]{:S(2)}, u32[]{:S(2)}) %collective-permute-start.28) | collective-permute-done | bytes 229408 | tf_op jit(solution)/shard_map/ppermute | solution.py:40
  115.4 2.1 %collective-permute-done.26.refs_1_ = bf16[32,3584]{1,0:T(8,128)(2,1)S(1)} collective-permute-done((bf16[32,3584]{1,0:T(8,128)(2,1)S(1)}, bf16[32,3584]{1,0:T(8,128)(2,1)S(1)}, u32[]{:S(2)}, u32[]{:S(2)}) %collective-permute-start.26) | collective-permute-done | bytes 229408 | tf_op jit(solution)/shard_map/ppermute | solution.py:40
  117.4 6.8 %feed.2 = (f32[32,3584]{1,0:T(8,128)S(1)}, f32[32,3584]{1,0:T(8,128)S(1)}, bf16[32,3584]{1,0:T(8,128)(2,1)S(1)}, f32[32,3584]{1,0:T(8,128)S(1)}) custom-call(bf16[32,3584]{1,0:T(8,128)(2,1)S(1)} %get-tuple-element.102.refs_0_, bf16[32,3584]{1,0:T(8,128)(2,1)S(1)} %collective-permute-done.26.refs_1_, bf16[32,3584]{1,0:T(8,128)(2,1)S(1)} %collective-permute-done.27.refs_2_, ...), custom_call_target="tpu_custom_call" | custom-call | flops 3523215360 | bytes 28000000 | tf_op jit(solution)/shard_map/feed/pallas_call | solution.py:324
  124.7 6.8 %feed.3 = (bf16[32,3584]{1,0:T(8,128)(2,1)S(1)}, bf16[32,3584]{1,0:T(8,128)(2,1)S(1)}, bf16[32,3584]{1,0:T(8,128)(2,1)S(1)}, bf16[32,3584]{1,0:T(8,128)(2,1)S(1)}) custom-call(bf16[32,3584]{1,0:T(8,128)(2,1)S(1)} %collective-permute-done.29.refs_0_, bf16[32,3584]{1,0:T(8,128)(2,1)S(1)} %collective-permute-done.30.refs_1_, ...), custom_call_target="tpu_custom_call" | custom-call | flops 3523215360 | bytes 28000000 | tf_op jit(solution)/shard_map/feed/pallas_call | solution.py:324
  131.4 2.9 %collective-permute-start.37 = (bf16[32,3584]{1,0:T(8,128)(2,1)S(1)}, bf16[32,3584]{1,0:T(8,128)(2,1)S(1)}, u32[]{:S(2)}, u32[]{:S(2)}) collective-permute-start(bf16[32,3584]{1,0:T(8,128)(2,1)S(1)} %get-tuple-element.110), channel_id=1, source_target_pairs={{0,72},{1,73},{2,74},{3,75},{4,76},{5,77},{6,78},{7,79},{8,0},{9,1... | collective-permute-start | bytes 688136 | tf_op jit(solution)/shard_map/ppermute | solution.py:40
  134.3 3.5 %collective-permute-start.39 = (bf16[32,3584]{1,0:T(8,128)(2,1)S(1)}, bf16[32,3584]{1,0:T(8,128)(2,1)S(1)}, u32[]{:S(2)}, u32[]{:S(2)}) collective-permute-start(bf16[32,3584]{1,0:T(8,128)(2,1)S(1)} %get-tuple-element.111), channel_id=1, source_target_pairs={{0,4},{1,5},{2,6},{3,7},{4,0},{5,1},{6,2},{7,3},{8,12},{9,13},{10,... | collective-permute-start | bytes 688136 | tf_op jit(solution)/shard_map/ppermute | solution.py:40
  137.9 3.2 %collective-permute-start.34 = (bf16[32,3584]{1,0:T(8,128)(2,1)S(1)}, bf16[32,3584]{1,0:T(8,128)(2,1)S(1)}, u32[]{:S(2)}, u32[]{:S(2)}) collective-permute-start(bf16[32,3584]{1,0:T(8,128)(2,1)S(1)} %get-tuple-element.107), channel_id=1, source_target_pairs={{0,72},{1,73},{2,74},{3,75},{4,76},{5,77},{6,78},{7,79},{8,0},{9,1... | collective-permute-start | bytes 688136 | tf_op jit(solution)/shard_map/ppermute | solution.py:40
  141.2 1.7 %collective-permute-start.38 = (bf16[32,3584]{1,0:T(8,128)(2,1)S(1)}, bf16[32,3584]{1,0:T(8,128)(2,1)S(1)}, u32[]{:S(2)}, u32[]{:S(2)}) collective-permute-start(bf16[32,3584]{1,0:T(8,128)(2,1)S(1)} %fold.6), channel_id=1, source_target_pairs={{0,6},{1,7},{2,0},{3,1},{4,2},{5,3},{6,4},{7,5},{8,14},{9,15},{10,... | collective-permute-start | bytes 688136 | tf_op jit(solution)/shard_map/ppermute | solution.py:40
  142.9 1.2 collective-permute-start.41
  144.6 5.4 %collective-permute-done.36.refs_1_ = bf16[32,3584]{1,0:T(8,128)(2,1)S(1)} collective-permute-done((bf16[32,3584]{1,0:T(8,128)(2,1)S(1)}, bf16[32,3584]{1,0:T(8,128)(2,1)S(1)}, u32[]{:S(2)}, u32[]{:S(2)}) %collective-permute-start.36) | collective-permute-done | bytes 229408 | tf_op jit(solution)/shard_map/ppermute | solution.py:40
  150.5 0.8 reshape.15
  (86 shorter events, 6.5 us)
Async XLA Ops:
  0.6 20.6 %collective-permute-start.4 = (bf16[1024,3584]{1,0:T(8,128)(2,1)}, bf16[1024,3584]{1,0:T(8,128)(2,1)}, u32[]{:S(2)}, u32[]{:S(2)}) collective-permute-start(bf16[1024,3584]{1,0:T(8,128)(2,1)} %out_own.1), channel_id=1, source_target_pairs={{0,1},{1,0},{2,3},{3,2},{4,5},{5,4},{6,7},{7,6},{8,9},{9,8},{10,11... | collective-permute-start | bytes 22020104 | tf_op jit(solution)/shard_map/ppermute | solution.py:44
  0.7 29.7 %collective-permute-start.5 = (bf16[3584,640]{1,0:T(8,128)(2,1)}, bf16[3584,640]{1,0:T(8,128)(2,1)}, u32[]{:S(2)}, u32[]{:S(2)}) collective-permute-start(bf16[3584,640]{1,0:T(8,128)(2,1)} %g0), channel_id=1, source_target_pairs={{0,1},{1,0},{2,3},{3,2},{4,5},{5,4},{6,7},{7,6},{8,9},{9,8},{10,11... | collective-permute-start | bytes 13762568 | tf_op jit(solution)/shard_map/ppermute | solution.py:44
  1.2 9.5 %collective-permute-start = (bf16[8,512,128]{2,1,0:T(8,128)(2,1)}, bf16[8,512,128]{2,1,0:T(8,128)(2,1)S(1)}, u32[]{:S(2)}, u32[]{:S(2)}) collective-permute-start(bf16[8,512,128]{2,1,0:T(8,128)(2,1)} %up_own.1), channel_id=1, source_target_pairs={{0,1},{1,0},{2,3},{3,2},{4,5},{5,4},{6,7},{7,6},{8,9},{9,8},{10,11... | collective-permute-start | bytes 3145736 | tf_op jit(solution)/shard_map/ppermute | solution.py:44
  10.7 18.6 %collective-permute-start.3 = (bf16[32,16,512]{2,1,0:T(8,128)(2,1)}, bf16[32,16,512]{2,1,0:T(8,128)(2,1)S(1)}, u32[]{:S(2)}, u32[]{:S(2)}) collective-permute-start(bf16[32,16,512]{2,1,0:T(8,128)(2,1)} %get-tuple-element.63), channel_id=1, source_target_pairs={{0,72},{1,73},{2,74},{3,75},{4,76},{5,77},{6,78},{7,79},{8,0},{9,1... | collective-permute-start | bytes 1572872 | tf_op jit(solution)/shard_map/ppermute | solution.py:40
  14.8 15.3 %collective-permute-start.2 = (bf16[32,16,512]{2,1,0:T(8,128)(2,1)}, bf16[32,16,512]{2,1,0:T(8,128)(2,1)S(1)}, u32[]{:S(2)}, u32[]{:S(2)}) collective-permute-start(bf16[32,16,512]{2,1,0:T(8,128)(2,1)} %get-tuple-element.61), channel_id=1, source_target_pairs={{0,8},{1,9},{2,10},{3,11},{4,12},{5,13},{6,14},{7,15},{8,64},{9,65... | collective-permute-start | bytes 1572872 | tf_op jit(solution)/shard_map/ppermute | solution.py:40
  14.8 15.6 %collective-permute-start.1 = (bf16[32,16,512]{2,1,0:T(8,128)(2,1)}, bf16[32,16,512]{2,1,0:T(8,128)(2,1)S(1)}, u32[]{:S(2)}, u32[]{:S(2)}) collective-permute-start(bf16[32,16,512]{2,1,0:T(8,128)(2,1)} %get-tuple-element.59), channel_id=1, source_target_pairs={{0,4},{1,5},{2,6},{3,7},{4,0},{5,1},{6,2},{7,3},{8,12},{9,13},{10,... | collective-permute-start | bytes 1572872 | tf_op jit(solution)/shard_map/ppermute | solution.py:40
  21.2 26.2 %slice-start = ((s8[4587520]{0:T(1024)(128)(4,1)}), s8[4194304]{0:T(1024)(128)(4,1)S(1)}, s32[]{:S(2)}) async-start(s8[4587520]{0:T(1024)(128)(4,1)} %bitcast.4), calls=%async_computation | async-start | bytes 8388608
  21.2 26.3 %slice-start.2 = ((s8[4587520]{0:T(1024)(128)(4,1)}), s8[4194304]{0:T(1024)(128)(4,1)S(1)}, s32[]{:S(2)}) async-start(s8[4587520]{0:T(1024)(128)(4,1)} %bitcast.6), calls=%async_computation.2 | async-start | bytes 8388608
  21.3 26.3 %slice-start.3 = ((s8[4587520]{0:T(1024)(128)(4,1)}), s8[393216]{0:T(1024)(128)(4,1)S(1)}, s32[]{:S(2)}) async-start(s8[4587520]{0:T(1024)(128)(4,1)} %bitcast.6), calls=%async_computation.3 | async-start | bytes 786432
  21.3 30.6 %copy-start.5 = (bf16[32,16,512]{2,1,0:T(8,128)(2,1)S(1)}, bf16[32,16,512]{2,1,0:T(8,128)(2,1)}, u32[]{:S(2)}) copy-start(bf16[32,16,512]{2,1,0:T(8,128)(2,1)} %get-tuple-element.76) | copy-start | bytes 1572868
  21.3 36.8 %copy-start.4 = (bf16[32,16,512]{2,1,0:T(8,128)(2,1)S(1)}, bf16[32,16,512]{2,1,0:T(8,128)(2,1)}, u32[]{:S(2)}) copy-start(bf16[32,16,512]{2,1,0:T(8,128)(2,1)} %get-tuple-element.89) | copy-start | bytes 1572868
  21.3 8.0 %collective-permute-start.6 = (bf16[2,64,576]{2,1,0:T(8,128)(2,1)S(1)}, bf16[2,64,576]{2,1,0:T(8,128)(2,1)S(1)}, u32[]{:S(2)}, u32[]{:S(2)}) collective-permute-start(bf16[2,64,576]{2,1,0:T(8,128)(2,1)S(1)} %get-tuple-element.66.mine_ref), channel_id=1, source_target_pairs={{0,16},{16,0},{32,48},{48,32},{64,80},{80,64},{96,112},{112,96},{1... | collective-permute-start | bytes 442376 | tf_op jit(solution)/shard_map/ppermute | solution.py:484
  29.3 31.8 %copy-start = (bf16[32,16,512]{2,1,0:T(8,128)(2,1)S(1)}, bf16[32,16,512]{2,1,0:T(8,128)(2,1)}, u32[]{:S(2)}) copy-start(bf16[32,16,512]{2,1,0:T(8,128)(2,1)} %get-tuple-element.71.refs_0_) | copy-start | bytes 1572868
  30.5 14.3 %collective-permute-start.7 = (bf16[32,16,512]{2,1,0:T(8,128)(2,1)S(1)}, bf16[32,16,512]{2,1,0:T(8,128)(2,1)S(1)}, u32[]{:S(2)}, u32[]{:S(2)}) collective-permute-start(bf16[32,16,512]{2,1,0:T(8,128)(2,1)S(1)} %copy-done.7), channel_id=1, source_target_pairs={{0,8},{1,9},{2,10},{3,11},{4,12},{5,13},{6,14},{7,15},{8,64},{9,65... | collective-permute-start | bytes 1572872 | tf_op jit(solution)/shard_map/ppermute | solution.py:40
  30.5 14.3 %collective-permute-start.8 = (bf16[32,16,512]{2,1,0:T(8,128)(2,1)S(1)}, bf16[32,16,512]{2,1,0:T(8,128)(2,1)S(1)}, u32[]{:S(2)}, u32[]{:S(2)}) collective-permute-start(bf16[32,16,512]{2,1,0:T(8,128)(2,1)S(1)} %copy-done.6), channel_id=1, source_target_pairs={{0,72},{1,73},{2,74},{3,75},{4,76},{5,77},{6,78},{7,79},{8,0},{9,1... | collective-permute-start | bytes 1572872 | tf_op jit(solution)/shard_map/ppermute | solution.py:40
  33.7 13.7 %collective-permute-start.10 = (bf16[32,16,512]{2,1,0:T(8,128)(2,1)S(1)}, bf16[32,16,512]{2,1,0:T(8,128)(2,1)S(1)}, u32[]{:S(2)}, u32[]{:S(2)}) collective-permute-start(bf16[32,16,512]{2,1,0:T(8,128)(2,1)S(1)} %collective-permute-done.2), channel_id=1, source_target_pairs={{0,2},{1,3},{2,4},{3,5},{4,6},{5,7},{6,0},{7,1},{8,10},{9,11},{10,... | collective-permute-start | bytes 1572872 | tf_op jit(solution)/shard_map/ppermute | solution.py:40
  35.2 12.2 %collective-permute-start.14 = (bf16[32,16,512]{2,1,0:T(8,128)(2,1)S(1)}, bf16[32,16,512]{2,1,0:T(8,128)(2,1)S(1)}, u32[]{:S(2)}, u32[]{:S(2)}) collective-permute-start(bf16[32,16,512]{2,1,0:T(8,128)(2,1)S(1)} %collective-permute-done.3), channel_id=1, source_target_pairs={{0,6},{1,7},{2,0},{3,1},{4,2},{5,3},{6,4},{7,5},{8,14},{9,15},{10,... | collective-permute-start | bytes 1572872 | tf_op jit(solution)/shard_map/ppermute | solution.py:40
  37.6 6.9 %collective-permute-start.11 = (bf16[2,64,576]{2,1,0:T(8,128)(2,1)S(1)}, bf16[2,64,576]{2,1,0:T(8,128)(2,1)S(1)}, u32[]{:S(2)}, u32[]{:S(2)}) collective-permute-start(bf16[2,64,576]{2,1,0:T(8,128)(2,1)S(1)} %pick.3.mine_ref), channel_id=1, source_target_pairs={{0,32},{16,48},{32,0},{48,16},{64,96},{80,112},{96,64},{112,80},{1... | collective-permute-start | bytes 442376 | tf_op jit(solution)/shard_map/ppermute | solution.py:484
  47.5 19.8 %collective-permute-start.15 = (bf16[3584,640]{1,0:T(8,128)(2,1)S(1)}, bf16[3584,640]{1,0:T(8,128)(2,1)S(1)}, u32[]{:S(2)}, u32[]{:S(2)}) collective-permute-start(bf16[3584,640]{1,0:T(8,128)(2,1)S(1)} %bitcast.5), channel_id=1, source_target_pairs={{0,1},{1,0},{2,3},{3,2},{4,5},{5,4},{6,7},{7,6},{8,9},{9,8},{10,11... | collective-permute-start | bytes 13762568 | tf_op jit(solution)/shard_map/ppermute | solution.py:44
  47.6 19.7 %collective-permute-start.16 = (bf16[640,3584]{1,0:T(8,128)(2,1)S(1)}, bf16[640,3584]{1,0:T(8,128)(2,1)}, u32[]{:S(2)}, u32[]{:S(2)}) collective-permute-start(bf16[640,3584]{1,0:T(8,128)(2,1)S(1)} %bitcast.7), channel_id=1, source_target_pairs={{0,1},{1,0},{2,3},{3,2},{4,5},{5,4},{6,7},{7,6},{8,9},{9,8},{10,11... | collective-permute-start | bytes 13762568 | tf_op jit(solution)/shard_map/ppermute | solution.py:44
  48.0 16.3 %collective-permute-start.13 = (bf16[32,16,512]{2,1,0:T(8,128)(2,1)S(1)}, bf16[32,16,512]{2,1,0:T(8,128)(2,1)S(1)}, u32[]{:S(2)}, u32[]{:S(2)}) collective-permute-start(bf16[32,16,512]{2,1,0:T(8,128)(2,1)S(1)} %collective-permute-done.8), channel_id=1, source_target_pairs={{0,4},{1,5},{2,6},{3,7},{4,0},{5,1},{6,2},{7,3},{8,12},{9,13},{10,... | collective-permute-start | bytes 1572872 | tf_op jit(solution)/shard_map/ppermute | solution.py:40
  50.7 7.4 %collective-permute-start.12 = (bf16[2,64,576]{2,1,0:T(8,128)(2,1)S(1)}, bf16[2,64,576]{2,1,0:T(8,128)(2,1)S(1)}, u32[]{:S(2)}, u32[]{:S(2)}) collective-permute-start(bf16[2,64,576]{2,1,0:T(8,128)(2,1)S(1)} %pick.4.mine_ref), channel_id=1, source_target_pairs={{0,64},{16,80},{32,96},{48,112},{64,0},{80,16},{96,32},{112,48},{1... | collective-permute-start | bytes 442376 | tf_op jit(solution)/shard_map/ppermute | solution.py:484
  51.8 23.5 %collective-permute-start.9 = (bf16[32,16,512]{2,1,0:T(8,128)(2,1)S(1)}, bf16[32,16,512]{2,1,0:T(8,128)(2,1)S(1)}, u32[]{:S(2)}, u32[]{:S(2)}) collective-permute-start(bf16[32,16,512]{2,1,0:T(8,128)(2,1)S(1)} %copy-done.5), channel_id=1, source_target_pairs={{0,2},{1,3},{2,4},{3,5},{4,6},{5,7},{6,0},{7,1},{8,10},{9,11},{10,... | collective-permute-start | bytes 1572872 | tf_op jit(solution)/shard_map/ppermute | solution.py:40
  58.1 17.3 %collective-permute-start.17 = (bf16[32,16,512]{2,1,0:T(8,128)(2,1)S(1)}, bf16[32,16,512]{2,1,0:T(8,128)(2,1)S(1)}, u32[]{:S(2)}, u32[]{:S(2)}) collective-permute-start(bf16[32,16,512]{2,1,0:T(8,128)(2,1)S(1)} %copy-done.4), channel_id=1, source_target_pairs={{0,6},{1,7},{2,0},{3,1},{4,2},{5,3},{6,4},{7,5},{8,14},{9,15},{10,... | collective-permute-start | bytes 1572872 | tf_op jit(solution)/shard_map/ppermute | solution.py:40
  70.5 11.7 %collective-permute-start.18 = (bf16[32,3584]{1,0:T(8,128)(2,1)S(1)}, bf16[32,3584]{1,0:T(8,128)(2,1)S(1)}, u32[]{:S(2)}, u32[]{:S(2)}) collective-permute-start(bf16[32,3584]{1,0:T(8,128)(2,1)S(1)} %get-tuple-element.92), channel_id=1, source_target_pairs={{0,72},{1,73},{2,74},{3,75},{4,76},{5,77},{6,78},{7,79},{8,0},{9,1... | collective-permute-start | bytes 688136 | tf_op jit(solution)/shard_map/ppermute | solution.py:40
  72.1 12.0 %collective-permute-start.19 = (bf16[32,3584]{1,0:T(8,128)(2,1)S(1)}, bf16[32,3584]{1,0:T(8,128)(2,1)S(1)}, u32[]{:S(2)}, u32[]{:S(2)}) collective-permute-start(bf16[32,3584]{1,0:T(8,128)(2,1)S(1)} %get-tuple-element.94), channel_id=1, source_target_pairs={{0,8},{1,9},{2,10},{3,11},{4,12},{5,13},{6,14},{7,15},{8,64},{9,65... | collective-permute-start | bytes 688136 | tf_op jit(solution)/shard_map/ppermute | solution.py:40
  72.7 14.3 %collective-permute-start.21 = (bf16[32,3584]{1,0:T(8,128)(2,1)S(1)}, bf16[32,3584]{1,0:T(8,128)(2,1)S(1)}, u32[]{:S(2)}, u32[]{:S(2)}) collective-permute-start(bf16[32,3584]{1,0:T(8,128)(2,1)S(1)} %get-tuple-element.96), channel_id=1, source_target_pairs={{0,4},{1,5},{2,6},{3,7},{4,0},{5,1},{6,2},{7,3},{8,12},{9,13},{10,... | collective-permute-start | bytes 688136 | tf_op jit(solution)/shard_map/ppermute | solution.py:40
  80.1 15.3 %collective-permute-start.24 = (bf16[32,3584]{1,0:T(8,128)(2,1)S(1)}, bf16[32,3584]{1,0:T(8,128)(2,1)S(1)}, u32[]{:S(2)}, u32[]{:S(2)}) collective-permute-start(bf16[32,3584]{1,0:T(8,128)(2,1)S(1)} %get-tuple-element.100), channel_id=1, source_target_pairs={{0,4},{1,5},{2,6},{3,7},{4,0},{5,1},{6,2},{7,3},{8,12},{9,13},{10,... | collective-permute-start | bytes 688136 | tf_op jit(solution)/shard_map/ppermute | solution.py:40
  82.3 13.2 %collective-permute-start.23 = (bf16[32,3584]{1,0:T(8,128)(2,1)S(1)}, bf16[32,3584]{1,0:T(8,128)(2,1)S(1)}, u32[]{:S(2)}, u32[]{:S(2)}) collective-permute-start(bf16[32,3584]{1,0:T(8,128)(2,1)S(1)} %fold.4), channel_id=1, source_target_pairs={{0,6},{1,7},{2,0},{3,1},{4,2},{5,3},{6,4},{7,5},{8,14},{9,15},{10,... | collective-permute-start | bytes 688136 | tf_op jit(solution)/shard_map/ppermute | solution.py:40
  84.2 11.3 %collective-permute-start.25 = (bf16[32,3584]{1,0:T(8,128)(2,1)S(1)}, bf16[32,3584]{1,0:T(8,128)(2,1)S(1)}, u32[]{:S(2)}, u32[]{:S(2)}) collective-permute-start(bf16[32,3584]{1,0:T(8,128)(2,1)S(1)} %fold.5), channel_id=1, source_target_pairs={{0,2},{1,3},{2,4},{3,5},{4,6},{5,7},{6,0},{7,1},{8,10},{9,11},{10,... | collective-permute-start | bytes 688136 | tf_op jit(solution)/shard_map/ppermute | solution.py:40
  84.5 10.9 %collective-permute-start.20 = (bf16[32,3584]{1,0:T(8,128)(2,1)S(1)}, bf16[32,3584]{1,0:T(8,128)(2,1)S(1)}, u32[]{:S(2)}, u32[]{:S(2)}) collective-permute-start(bf16[32,3584]{1,0:T(8,128)(2,1)S(1)} %get-tuple-element.95), channel_id=1, source_target_pairs={{0,72},{1,73},{2,74},{3,75},{4,76},{5,77},{6,78},{7,79},{8,0},{9,1... | collective-permute-start | bytes 688136 | tf_op jit(solution)/shard_map/ppermute | solution.py:40
  87.0 8.5 %collective-permute-start.22 = (bf16[32,3584]{1,0:T(8,128)(2,1)S(1)}, bf16[32,3584]{1,0:T(8,128)(2,1)S(1)}, u32[]{:S(2)}, u32[]{:S(2)}) collective-permute-start(bf16[32,3584]{1,0:T(8,128)(2,1)S(1)} %collective-permute-done.21), channel_id=1, source_target_pairs={{0,8},{1,9},{2,10},{3,11},{4,12},{5,13},{6,14},{7,15},{8,64},{9,65... | collective-permute-start | bytes 688136 | tf_op jit(solution)/shard_map/ppermute | solution.py:40
  95.9 7.9 %collective-permute-start.31 = (bf16[32,3584]{1,0:T(8,128)(2,1)S(1)}, bf16[32,3584]{1,0:T(8,128)(2,1)S(1)}, u32[]{:S(2)}, u32[]{:S(2)}) collective-permute-start(bf16[32,3584]{1,0:T(8,128)(2,1)S(1)} %get-tuple-element.102.refs_0_), channel_id=1, source_target_pairs={{0,72},{1,73},{2,74},{3,75},{4,76},{5,77},{6,78},{7,79},{8,0},{9,1... | collective-permute-start | bytes 688136 | tf_op jit(solution)/shard_map/ppermute | solution.py:40
  99.2 15.9 %collective-permute-start.28 = (bf16[32,3584]{1,0:T(8,128)(2,1)S(1)}, bf16[32,3584]{1,0:T(8,128)(2,1)S(1)}, u32[]{:S(2)}, u32[]{:S(2)}) collective-permute-start(bf16[32,3584]{1,0:T(8,128)(2,1)S(1)} %get-tuple-element.102.refs_0_), channel_id=1, source_target_pairs={{0,6},{1,7},{2,0},{3,1},{4,2},{5,3},{6,4},{7,5},{8,14},{9,15},{10,... | collective-permute-start | bytes 688136 | tf_op jit(solution)/shard_map/ppermute | solution.py:40
  102.4 15.0 %collective-permute-start.26 = (bf16[32,3584]{1,0:T(8,128)(2,1)S(1)}, bf16[32,3584]{1,0:T(8,128)(2,1)S(1)}, u32[]{:S(2)}, u32[]{:S(2)}) collective-permute-start(bf16[32,3584]{1,0:T(8,128)(2,1)S(1)} %get-tuple-element.102.refs_0_), channel_id=1, source_target_pairs={{0,2},{1,3},{2,4},{3,5},{4,6},{5,7},{6,0},{7,1},{8,10},{9,11},{10,... | collective-permute-start | bytes 688136 | tf_op jit(solution)/shard_map/ppermute | solution.py:40
  102.4 15.1 %collective-permute-start.27 = (bf16[32,3584]{1,0:T(8,128)(2,1)S(1)}, bf16[32,3584]{1,0:T(8,128)(2,1)S(1)}, u32[]{:S(2)}, u32[]{:S(2)}) collective-permute-start(bf16[32,3584]{1,0:T(8,128)(2,1)S(1)} %get-tuple-element.102.refs_0_), channel_id=1, source_target_pairs={{0,4},{1,5},{2,6},{3,7},{4,0},{5,1},{6,2},{7,3},{8,12},{9,13},{10,... | collective-permute-start | bytes 688136 | tf_op jit(solution)/shard_map/ppermute | solution.py:40
  103.8 20.4 %collective-permute-start.29 = (bf16[32,3584]{1,0:T(8,128)(2,1)S(1)}, bf16[32,3584]{1,0:T(8,128)(2,1)S(1)}, u32[]{:S(2)}, u32[]{:S(2)}) collective-permute-start(bf16[32,3584]{1,0:T(8,128)(2,1)S(1)} %get-tuple-element.102.refs_0_), channel_id=1, source_target_pairs={{0,8},{1,9},{2,10},{3,11},{4,12},{5,13},{6,14},{7,15},{8,64},{9,65... | collective-permute-start | bytes 688136 | tf_op jit(solution)/shard_map/ppermute | solution.py:40
  103.9 20.4 %collective-permute-start.32 = (bf16[32,3584]{1,0:T(8,128)(2,1)S(1)}, bf16[32,3584]{1,0:T(8,128)(2,1)S(1)}, u32[]{:S(2)}, u32[]{:S(2)}) collective-permute-start(bf16[32,3584]{1,0:T(8,128)(2,1)S(1)} %collective-permute-done.31), channel_id=1, source_target_pairs={{0,4},{1,5},{2,6},{3,7},{4,0},{5,1},{6,2},{7,3},{8,12},{9,13},{10,... | collective-permute-start | bytes 688136 | tf_op jit(solution)/shard_map/ppermute | solution.py:40
  115.1 9.1 %collective-permute-start.33 = (bf16[32,3584]{1,0:T(8,128)(2,1)S(1)}, bf16[32,3584]{1,0:T(8,128)(2,1)S(1)}, u32[]{:S(2)}, u32[]{:S(2)}) collective-permute-start(bf16[32,3584]{1,0:T(8,128)(2,1)S(1)} %collective-permute-done.28.refs_3_), channel_id=1, source_target_pairs={{0,72},{1,73},{2,74},{3,75},{4,76},{5,77},{6,78},{7,79},{8,0},{9,1... | collective-permute-start | bytes 688136 | tf_op jit(solution)/shard_map/ppermute | solution.py:40
  117.4 7.2 %collective-permute-start.30 = (bf16[32,3584]{1,0:T(8,128)(2,1)S(1)}, bf16[32,3584]{1,0:T(8,128)(2,1)S(1)}, u32[]{:S(2)}, u32[]{:S(2)}) collective-permute-start(bf16[32,3584]{1,0:T(8,128)(2,1)S(1)} %collective-permute-done.26.refs_1_), channel_id=1, source_target_pairs={{0,8},{1,9},{2,10},{3,11},{4,12},{5,13},{6,14},{7,15},{8,64},{9,65... | collective-permute-start | bytes 688136 | tf_op jit(solution)/shard_map/ppermute | solution.py:40
  131.4 9.7 %collective-permute-start.37 = (bf16[32,3584]{1,0:T(8,128)(2,1)S(1)}, bf16[32,3584]{1,0:T(8,128)(2,1)S(1)}, u32[]{:S(2)}, u32[]{:S(2)}) collective-permute-start(bf16[32,3584]{1,0:T(8,128)(2,1)S(1)} %get-tuple-element.110), channel_id=1, source_target_pairs={{0,72},{1,73},{2,74},{3,75},{4,76},{5,77},{6,78},{7,79},{8,0},{9,1... | collective-permute-start | bytes 688136 | tf_op jit(solution)/shard_map/ppermute | solution.py:40
  134.3 8.5 %collective-permute-start.35 = (bf16[32,3584]{1,0:T(8,128)(2,1)S(1)}, bf16[32,3584]{1,0:T(8,128)(2,1)S(1)}, u32[]{:S(2)}, u32[]{:S(2)}) collective-permute-start(bf16[32,3584]{1,0:T(8,128)(2,1)S(1)} %get-tuple-element.108), channel_id=1, source_target_pairs={{0,4},{1,5},{2,6},{3,7},{4,0},{5,1},{6,2},{7,3},{8,12},{9,13},{10,... | collective-permute-start | bytes 688136 | tf_op jit(solution)/shard_map/ppermute | solution.py:40
  134.3 8.5 %collective-permute-start.40 = (bf16[32,3584]{1,0:T(8,128)(2,1)S(1)}, bf16[32,3584]{1,0:T(8,128)(2,1)S(1)}, u32[]{:S(2)}, u32[]{:S(2)}) collective-permute-start(bf16[32,3584]{1,0:T(8,128)(2,1)S(1)} %get-tuple-element.113), channel_id=1, source_target_pairs={{0,8},{1,9},{2,10},{3,11},{4,12},{5,13},{6,14},{7,15},{8,64},{9,65... | collective-permute-start | bytes 688136 | tf_op jit(solution)/shard_map/ppermute | solution.py:40
  134.3 10.0 %collective-permute-start.39 = (bf16[32,3584]{1,0:T(8,128)(2,1)S(1)}, bf16[32,3584]{1,0:T(8,128)(2,1)S(1)}, u32[]{:S(2)}, u32[]{:S(2)}) collective-permute-start(bf16[32,3584]{1,0:T(8,128)(2,1)S(1)} %get-tuple-element.111), channel_id=1, source_target_pairs={{0,4},{1,5},{2,6},{3,7},{4,0},{5,1},{6,2},{7,3},{8,12},{9,13},{10,... | collective-permute-start | bytes 688136 | tf_op jit(solution)/shard_map/ppermute | solution.py:40
  137.9 6.8 %collective-permute-start.34 = (bf16[32,3584]{1,0:T(8,128)(2,1)S(1)}, bf16[32,3584]{1,0:T(8,128)(2,1)S(1)}, u32[]{:S(2)}, u32[]{:S(2)}) collective-permute-start(bf16[32,3584]{1,0:T(8,128)(2,1)S(1)} %get-tuple-element.107), channel_id=1, source_target_pairs={{0,72},{1,73},{2,74},{3,75},{4,76},{5,77},{6,78},{7,79},{8,0},{9,1... | collective-permute-start | bytes 688136 | tf_op jit(solution)/shard_map/ppermute | solution.py:40
  141.2 8.9 %collective-permute-start.38 = (bf16[32,3584]{1,0:T(8,128)(2,1)S(1)}, bf16[32,3584]{1,0:T(8,128)(2,1)S(1)}, u32[]{:S(2)}, u32[]{:S(2)}) collective-permute-start(bf16[32,3584]{1,0:T(8,128)(2,1)S(1)} %fold.6), channel_id=1, source_target_pairs={{0,6},{1,7},{2,0},{3,1},{4,2},{5,3},{6,4},{7,5},{8,14},{9,15},{10,... | collective-permute-start | bytes 688136 | tf_op jit(solution)/shard_map/ppermute | solution.py:40
  142.8 7.2 %collective-permute-start.36 = (bf16[32,3584]{1,0:T(8,128)(2,1)S(1)}, bf16[32,3584]{1,0:T(8,128)(2,1)S(1)}, u32[]{:S(2)}, u32[]{:S(2)}) collective-permute-start(bf16[32,3584]{1,0:T(8,128)(2,1)S(1)} %collective-permute-done.35), channel_id=1, source_target_pairs={{0,8},{1,9},{2,10},{3,11},{4,12},{5,13},{6,14},{7,15},{8,64},{9,65... | collective-permute-start | bytes 688136 | tf_op jit(solution)/shard_map/ppermute | solution.py:40
  142.9 7.3 %collective-permute-start.41 = (bf16[32,3584]{1,0:T(8,128)(2,1)S(1)}, bf16[32,3584]{1,0:T(8,128)(2,1)S(1)}, u32[]{:S(2)}, u32[]{:S(2)}) collective-permute-start(bf16[32,3584]{1,0:T(8,128)(2,1)S(1)} %fold.7), channel_id=1, source_target_pairs={{0,2},{1,3},{2,4},{3,5},{4,6},{5,7},{6,0},{7,1},{8,10},{9,11},{10,... | collective-permute-start | bytes 688136 | tf_op jit(solution)/shard_map/ppermute | solution.py:40
  (6 other events, 83.4 us)

commit v4 on v3

--- a/solution.py
+++ b/solution.py
@@ -572,7 +572,7 @@
     over, under = shift(normed, dz=1), shift(normed, dz=-1)
     row2 = shift(normed, dx=2)
     far_row1, far_row3 = shift(row1, dz=1), shift(row3, dz=-1)
-    far_row2 = shift(under, dx=2)
+    far_row2 = shift(after(under, row3), dx=2)
     near = feed([normed, row1, row2, row3], held, near_shapes)
     home2 = shift(near[2], dx=-2)
     far = feed([after(over, near[0]), far_row1, far_row2, far_row3], held, far_shapes)

time: 151 us -> 150 us (level)
  starting transfers between devices: 60.5 us -> 58.6 us
    ppermute x34, starting transfers between devices: 53.2 us -> 51.3 us  [shift(): return lax.ppermute(value, GRID, pairs)]
  transfers between devices with their start and end apart: 42 -> 42, of which waited for: 15 -> 15; matrix products, arithmetic and copies ran while one was open for 0% -> 0% of each run, Pallas kernels for 31% -> 32%
where the time goes in v4:
time: 150 us; the launch traced here: 149 us
  starting transfers between devices  58.6 us (39%)
  Pallas kernels  54.7 us (36%)
  waiting for transfers between devices  32.9 us (22%)
  between operations  2.41 us (2%)
    ppermute x34, starting transfers between devices, shift(): return lax.ppermute(value, GRID, pairs)  51.3 us
    ppermute x34, waiting for transfers between devices, shift(): return lax.ppermute(value, GRID, pairs)  23 us
    pallas_call x2, Pallas kernels, feed(): pl.pallas_call(functools.partial(feed_kernel, blocks=len(blocks)), in_spe...  13.5 us
    ppermute x3, waiting for transfers between devices, page_trade(): return lax.ppermute(block, 'dp', [(d, d ^ 1 << bit) for d in range(8)])  8.84 us
    pallas_call x1, Pallas kernels, attend(): pl.pallas_call(functools.partial(attend_kernel, first_request=first), gri...  8.32 us
    pallas_call x1, Pallas kernels, hold_feed(): pl.pallas_call(hold_feed_kernel, in_specs=[HBM_SPEC, ANY_SPEC] * 3, out_s...  8.27 us
    pallas_call x2, Pallas kernels, project(): pl.pallas_call(functools.partial(project_kernel, parts=parts), in_specs=[...  6.39 us
    pallas_call x1, Pallas kernels, hold_projection(): pl.pallas_call(hold_projection_kernel, in_specs=[HBM_SPEC, ANY_SPEC] * 2,...  6.29 us
  transfers between devices with their start and end apart: 42, of which 15 were waited for; matrix products, arithmetic and copies ran while one was open for 0% of the time, Pallas kernels for 32%

profile of v4, /device:TPU:0, one launch (start us, length us, event | category | flops | bytes accessed | tf_op | source)
XLA Modules:
  0.0 149.5 jit_solution(3465671854871149062)
XLA Ops:
  1.3 8.3 %attend.1 = (bf16[32,16,512]{2,1,0:T(8,128)(2,1)}, bf16[32,16,512]{2,1,0:T(8,128)(2,1)}, bf16[32,16,512]{2,1,0:T(8,128)(2,1)}, bf16[32,16,512]{2,1,0:T(8,128)(2,...) custom-call(s32[16]{0:T(128)} %lens_ref.1, ...), custom_call_target="tpu_custom_call" | custom-call | flops 2281701376 | bytes 12800000 | tf_op jit(solution)/shard_map/attend/pallas_call | solution.py:108
  9.6 1.1 collective-permute-done.up_other
  10.7 4.1 %collective-permute-start.3 = (bf16[32,16,512]{2,1,0:T(8,128)(2,1)}, bf16[32,16,512]{2,1,0:T(8,128)(2,1)S(1)}, u32[]{:S(2)}, u32[]{:S(2)}) collective-permute-start(bf16[32,16,512]{2,1,0:T(8,128)(2,1)} %get-tuple-element.64), channel_id=1, source_target_pairs={{0,72},{1,73},{2,74},{3,75},{4,76},{5,77},{6,78},{7,79},{8,0},{9,1... | collective-permute-start | bytes 1572872 | tf_op jit(solution)/shard_map/ppermute | solution.py:40
  14.8 3.0 %collective-permute-start.1 = (bf16[32,16,512]{2,1,0:T(8,128)(2,1)}, bf16[32,16,512]{2,1,0:T(8,128)(2,1)S(1)}, u32[]{:S(2)}, u32[]{:S(2)}) collective-permute-start(bf16[32,16,512]{2,1,0:T(8,128)(2,1)} %get-tuple-element.60), channel_id=1, source_target_pairs={{0,4},{1,5},{2,6},{3,7},{4,0},{5,1},{6,2},{7,3},{8,12},{9,13},{10,... | collective-permute-start | bytes 1572872 | tf_op jit(solution)/shard_map/ppermute | solution.py:40
  19.2 2.0 %pages.1 = (bf16[2,64,576]{2,1,0:T(8,128)(2,1)S(1)}, s32[1]{0:T(128)}) custom-call(s32[8]{0:T(128)S(1)} %bitcast.2, s32[1]{0:T(128)S(6)} %copy.16.request_ref, s32[1]{0:T(128)S(6)} %copy.17.count_ref, bf16[16,192,576]{2,1,0:T(8,128)(2,1)} %cache_ref.3), custom_call_target="tpu_custom_call" | custom-call | flops 1000 | bytes 400000 | tf_op jit(solution)/shard_map/pages/pallas_call | solution.py:450
  21.3 1.7 %collective-permute-start.6 = (bf16[2,64,576]{2,1,0:T(8,128)(2,1)S(1)}, bf16[2,64,576]{2,1,0:T(8,128)(2,1)S(1)}, u32[]{:S(2)}, u32[]{:S(2)}) collective-permute-start(bf16[2,64,576]{2,1,0:T(8,128)(2,1)S(1)} %get-tuple-element.67.mine_ref), channel_id=1, source_target_pairs={{0,16},{16,0},{32,48},{48,32},{64,80},{80,64},{96,112},{112,96},{1... | collective-permute-start | bytes 442376 | tf_op jit(solution)/shard_map/ppermute | solution.py:484
  23.0 6.3 %hold_projection.1 = (bf16[16,512,128]{2,1,0:T(8,128)(2,1)S(1)}, bf16[2048,3584]{1,0:T(8,128)(2,1)S(1)}) custom-call(bf16[8,512,128]{2,1,0:T(8,128)(2,1)} %up_own.1, bf16[8,512,128]{2,1,0:T(8,128)(2,1)S(1)} %collective-permute-done.up_other, bf16[1024,3584]{1,0:T(8,128)(2,1)} %out_own.1, bf16[1024,3584]{1,0:T(8,128)(2,1)} %collective-permute-done.4.out_other), custom_call_target="tpu_custom_call" | custom-call | bytes 17000000 | tf_op jit(solution)/shard_map/hold_projection/pallas_call | solution.py:167
  29.3 0.9 collective-permute-done.2
  30.5 3.2 %collective-permute-start.8 = (bf16[32,16,512]{2,1,0:T(8,128)(2,1)S(1)}, bf16[32,16,512]{2,1,0:T(8,128)(2,1)S(1)}, u32[]{:S(2)}, u32[]{:S(2)}) collective-permute-start(bf16[32,16,512]{2,1,0:T(8,128)(2,1)S(1)} %copy-done.6), channel_id=1, source_target_pairs={{0,72},{1,73},{2,74},{3,75},{4,76},{5,77},{6,78},{7,79},{8,0},{9,1... | collective-permute-start | bytes 1572872 | tf_op jit(solution)/shard_map/ppermute | solution.py:40
  33.7 1.5 collective-permute-start.10
  35.2 1.7 %collective-permute-start.14 = (bf16[32,16,512]{2,1,0:T(8,128)(2,1)S(1)}, bf16[32,16,512]{2,1,0:T(8,128)(2,1)S(1)}, u32[]{:S(2)}, u32[]{:S(2)}) collective-permute-start(bf16[32,16,512]{2,1,0:T(8,128)(2,1)S(1)} %collective-permute-done.3), channel_id=1, source_target_pairs={{0,6},{1,7},{2,0},{3,1},{4,2},{5,3},{6,4},{7,5},{8,14},{9,15},{10,... | collective-permute-start | bytes 1572872 | tf_op jit(solution)/shard_map/ppermute | solution.py:40
  37.6 3.3 %collective-permute-start.11 = (bf16[2,64,576]{2,1,0:T(8,128)(2,1)S(1)}, bf16[2,64,576]{2,1,0:T(8,128)(2,1)S(1)}, u32[]{:S(2)}, u32[]{:S(2)}) collective-permute-start(bf16[2,64,576]{2,1,0:T(8,128)(2,1)S(1)} %pick.3.mine_ref), channel_id=1, source_target_pairs={{0,32},{16,48},{32,0},{48,16},{64,96},{80,112},{96,64},{112,80},{1... | collective-permute-start | bytes 442376 | tf_op jit(solution)/shard_map/ppermute | solution.py:484
  40.9 3.6 %collective-permute-done.11.other_ref = bf16[2,64,576]{2,1,0:T(8,128)(2,1)S(1)} collective-permute-done((bf16[2,64,576]{2,1,0:T(8,128)(2,1)S(1)}, bf16[2,64,576]{2,1,0:T(8,128)(2,1)S(1)}, u32[]{:S(2)}, u32[]{:S(2)}) %collective-permute-start.11) | collective-permute-done | bytes 147488 | tf_op jit(solution)/shard_map/ppermute | solution.py:484
  45.4 2.0 %collective-permute-done.10.refs_1_ = bf16[32,16,512]{2,1,0:T(8,128)(2,1)S(1)} collective-permute-done((bf16[32,16,512]{2,1,0:T(8,128)(2,1)S(1)}, bf16[32,16,512]{2,1,0:T(8,128)(2,1)S(1)}, u32[]{:S(2)}, u32[]{:S(2)}) %collective-permute-start.10) | collective-permute-done | bytes 524320 | tf_op jit(solution)/shard_map/ppermute | solution.py:40
  48.0 2.6 %collective-permute-start.13 = (bf16[32,16,512]{2,1,0:T(8,128)(2,1)S(1)}, bf16[32,16,512]{2,1,0:T(8,128)(2,1)S(1)}, u32[]{:S(2)}, u32[]{:S(2)}) collective-permute-start(bf16[32,16,512]{2,1,0:T(8,128)(2,1)S(1)} %collective-permute-done.8), channel_id=1, source_target_pairs={{0,4},{1,5},{2,6},{3,7},{4,0},{5,1},{6,2},{7,3},{8,12},{9,13},{10,... | collective-permute-start | bytes 1572872 | tf_op jit(solution)/shard_map/ppermute | solution.py:40
  50.7 1.1 collective-permute-start.12
  51.8 1.1 collective-permute-start.9
  52.9 5.2 %collective-permute-done.12.other_ref = bf16[2,64,576]{2,1,0:T(8,128)(2,1)S(1)} collective-permute-done((bf16[2,64,576]{2,1,0:T(8,128)(2,1)S(1)}, bf16[2,64,576]{2,1,0:T(8,128)(2,1)S(1)}, u32[]{:S(2)}, u32[]{:S(2)}) %collective-permute-start.12) | collective-permute-done | bytes 147488 | tf_op jit(solution)/shard_map/ppermute | solution.py:484
  58.1 1.4 collective-permute-start.17
  59.6 1.5 %values.5.refs_0_ = bf16[64,2048]{1,0:T(8,128)(2,1)S(1)} custom-call(bf16[32,16,512]{2,1,0:T(8,128)(2,1)S(1)} %collective-permute-done.7.refs_0_, bf16[32,16,512]{2,1,0:T(8,128)(2,1)S(1)} %collective-permute-done.10.refs_1_, bf16[16,512,128]{2,1,0:T(8,128)(2,1)S(1)} %get-tuple-element.73.refs_2_), custom_call_target="tpu_custom_call" | custom-call | flops 134217728 | bytes 4000000 | tf_op jit(solution)/shard_map/values/pallas_call | solution.py:236
  61.1 1.5 %values.4.refs_0_.refs_2_ = bf16[64,2048]{1,0:T(8,128)(2,1)S(1)} custom-call(bf16[32,16,512]{2,1,0:T(8,128)(2,1)S(1)} %copy-done, bf16[32,16,512]{2,1,0:T(8,128)(2,1)S(1)} %collective-permute-done.1.refs_1_, bf16[16,512,128]{2,1,0:T(8,128)(2,1)S(1)} %get-tuple-element.73.refs_2_), custom_call_target="tpu_custom_call" | custom-call | flops 134217728 | bytes 4000000 | tf_op jit(solution)/shard_map/values/pallas_call | solution.py:236
  62.7 1.7 %collective-permute-done.13.refs_0_ = bf16[32,16,512]{2,1,0:T(8,128)(2,1)S(1)} collective-permute-done((bf16[32,16,512]{2,1,0:T(8,128)(2,1)S(1)}, bf16[32,16,512]{2,1,0:T(8,128)(2,1)S(1)}, u32[]{:S(2)}, u32[]{:S(2)}) %collective-permute-start.13) | collective-permute-done | bytes 524320 | tf_op jit(solution)/shard_map/ppermute | solution.py:40
  64.4 1.3 pick.5
  65.7 1.5 %values.6.refs_1_ = bf16[64,2048]{1,0:T(8,128)(2,1)S(1)} custom-call(bf16[32,16,512]{2,1,0:T(8,128)(2,1)S(1)} %collective-permute-done.13.refs_0_, bf16[32,16,512]{2,1,0:T(8,128)(2,1)S(1)} %collective-permute-done.14.refs_1_, bf16[16,512,128]{2,1,0:T(8,128)(2,1)S(1)} %get-tuple-element.73.refs_2_), custom_call_target="tpu_custom_call" | custom-call | flops 134217728 | bytes 4000000 | tf_op jit(solution)/shard_map/values/pallas_call | solution.py:236
  67.2 3.2 %project.2 = (bf16[32,3584]{1,0:T(8,128)(2,1)S(1)}, bf16[32,3584]{1,0:T(8,128)(2,1)S(1)}, bf16[32,3584]{1,0:T(8,128)(2,1)S(1)}, bf16[32,3584]{1,0:T(8,128)(2,1)S(1)}) custom-call(bf16[64,2048]{1,0:T(8,128)(2,1)S(1)} %values.5.refs_0_, bf16[64,2048]{1,0:T(8,128)(2,1)S(1)} %values.6.refs_1_, bf16[2048,3584]{1,0:T(8,128)(2,1)S(1)} %get-tuple-element.65.refs_2_.refs_4_), custom_call_target="tpu_custom_call" | custom-call | flops 1879048192 | bytes 17000000 | tf_op jit(solution)/shard_map/project/pallas_call | solution.py:279
  70.5 1.7 %collective-permute-start.18 = (bf16[32,3584]{1,0:T(8,128)(2,1)S(1)}, bf16[32,3584]{1,0:T(8,128)(2,1)S(1)}, u32[]{:S(2)}, u32[]{:S(2)}) collective-permute-start(bf16[32,3584]{1,0:T(8,128)(2,1)S(1)} %get-tuple-element.93), channel_id=1, source_target_pairs={{0,72},{1,73},{2,74},{3,75},{4,76},{5,77},{6,78},{7,79},{8,0},{9,1... | collective-permute-start | bytes 688136 | tf_op jit(solution)/shard_map/ppermute | solution.py:40
  72.7 2.6 %collective-permute-start.21 = (bf16[32,3584]{1,0:T(8,128)(2,1)S(1)}, bf16[32,3584]{1,0:T(8,128)(2,1)S(1)}, u32[]{:S(2)}, u32[]{:S(2)}) collective-permute-start(bf16[32,3584]{1,0:T(8,128)(2,1)S(1)} %get-tuple-element.97), channel_id=1, source_target_pairs={{0,4},{1,5},{2,6},{3,7},{4,0},{5,1},{6,2},{7,3},{8,12},{9,13},{10,... | collective-permute-start | bytes 688136 | tf_op jit(solution)/shard_map/ppermute | solution.py:40
  75.4 1.5 %values.7.refs_1_.refs_3_ = bf16[64,2048]{1,0:T(8,128)(2,1)S(1)} custom-call(bf16[32,16,512]{2,1,0:T(8,128)(2,1)S(1)} %collective-permute-done.9.refs_0_, bf16[32,16,512]{2,1,0:T(8,128)(2,1)S(1)} %collective-permute-done.17.refs_1_, bf16[16,512,128]{2,1,0:T(8,128)(2,1)S(1)} %get-tuple-element.73.refs_2_), custom_call_target="tpu_custom_call" | custom-call | flops 134217728 | bytes 4000000 | tf_op jit(solution)/shard_map/values/pallas_call | solution.py:236
  76.9 3.2 %project.3 = (f32[32,3584]{1,0:T(8,128)S(1)}, f32[32,3584]{1,0:T(8,128)S(1)}, bf16[32,3584]{1,0:T(8,128)(2,1)S(1)}, f32[32,3584]{1,0:T(8,128)S(1)}) custom-call(bf16[64,2048]{1,0:T(8,128)(2,1)S(1)} %values.4.refs_0_.refs_2_, bf16[64,2048]{1,0:T(8,128)(2,1)S(1)} %values.7.refs_1_.refs_3_, bf16[64,2048]{1,0:T(8,128)(2,1)S(1)} %values.4.refs_0_.refs_2_, ...), custom_call_target="tpu_custom_call" | custom-call | flops 1879048192 | bytes 17000000 | tf_op jit(solution)/shard_map/project/pallas_call | solution.py:279
  80.1 2.1 %collective-permute-start.24 = (bf16[32,3584]{1,0:T(8,128)(2,1)S(1)}, bf16[32,3584]{1,0:T(8,128)(2,1)S(1)}, u32[]{:S(2)}, u32[]{:S(2)}) collective-permute-start(bf16[32,3584]{1,0:T(8,128)(2,1)S(1)} %get-tuple-element.101), channel_id=1, source_target_pairs={{0,4},{1,5},{2,6},{3,7},{4,0},{5,1},{6,2},{7,3},{8,12},{9,13},{10,... | collective-permute-start | bytes 688136 | tf_op jit(solution)/shard_map/ppermute | solution.py:40
  82.3 1.8 %collective-permute-start.23 = (bf16[32,3584]{1,0:T(8,128)(2,1)S(1)}, bf16[32,3584]{1,0:T(8,128)(2,1)S(1)}, u32[]{:S(2)}, u32[]{:S(2)}) collective-permute-start(bf16[32,3584]{1,0:T(8,128)(2,1)S(1)} %fold.4), channel_id=1, source_target_pairs={{0,6},{1,7},{2,0},{3,1},{4,2},{5,3},{6,4},{7,5},{8,14},{9,15},{10,... | collective-permute-start | bytes 688136 | tf_op jit(solution)/shard_map/ppermute | solution.py:40
  84.5 2.5 %collective-permute-start.20 = (bf16[32,3584]{1,0:T(8,128)(2,1)S(1)}, bf16[32,3584]{1,0:T(8,128)(2,1)S(1)}, u32[]{:S(2)}, u32[]{:S(2)}) collective-permute-start(bf16[32,3584]{1,0:T(8,128)(2,1)S(1)} %get-tuple-element.96), channel_id=1, source_target_pairs={{0,72},{1,73},{2,74},{3,75},{4,76},{5,77},{6,78},{7,79},{8,0},{9,1... | collective-permute-start | bytes 688136 | tf_op jit(solution)/shard_map/ppermute | solution.py:40
  87.2 8.3 %hold_feed.1 = (bf16[5,3584,256]{2,1,0:T(8,128)(2,1)S(1)}, bf16[5,3584,256]{2,1,0:T(8,128)(2,1)S(1)}, bf16[1280,3584]{1,0:T(8,128)(2,1)S(1)}) custom-call(bf16[3584,640]{1,0:T(8,128)(2,1)} %g0, bf16[3584,640]{1,0:T(8,128)(2,1)} %collective-permute-done.5.g1, bf16[3584,640]{1,0:T(8,128)(2,1)} %u0.1, bf16[3584,640]{1,0:T(8,128)(2,1)S(1)} %collective-permute-done.15.u1, ...), custom_call_target="tpu_custom_call" | custom-call | bytes 27500000 | tf_op jit(solution)/shard_map/hold_feed/pallas_call | solution.py:198
  95.9 3.3 %collective-permute-start.31 = (bf16[32,3584]{1,0:T(8,128)(2,1)S(1)}, bf16[32,3584]{1,0:T(8,128)(2,1)S(1)}, u32[]{:S(2)}, u32[]{:S(2)}) collective-permute-start(bf16[32,3584]{1,0:T(8,128)(2,1)S(1)} %get-tuple-element.103.refs_0_), channel_id=1, source_target_pairs={{0,72},{1,73},{2,74},{3,75},{4,76},{5,77},{6,78},{7,79},{8,0},{9,1... | collective-permute-start | bytes 688136 | tf_op jit(solution)/shard_map/ppermute | solution.py:40
  99.2 3.2 %collective-permute-start.28 = (bf16[32,3584]{1,0:T(8,128)(2,1)S(1)}, bf16[32,3584]{1,0:T(8,128)(2,1)S(1)}, u32[]{:S(2)}, u32[]{:S(2)}) collective-permute-start(bf16[32,3584]{1,0:T(8,128)(2,1)S(1)} %get-tuple-element.103.refs_0_), channel_id=1, source_target_pairs={{0,6},{1,7},{2,0},{3,1},{4,2},{5,3},{6,4},{7,5},{8,14},{9,15},{10,... | collective-permute-start | bytes 688136 | tf_op jit(solution)/shard_map/ppermute | solution.py:40
  102.4 1.5 collective-permute-start.27
  103.9 8.8 %collective-permute-done.28.refs_3_ = bf16[32,3584]{1,0:T(8,128)(2,1)S(1)} collective-permute-done((bf16[32,3584]{1,0:T(8,128)(2,1)S(1)}, bf16[32,3584]{1,0:T(8,128)(2,1)S(1)}, u32[]{:S(2)}, u32[]{:S(2)}) %collective-permute-start.28) | collective-permute-done | bytes 229408 | tf_op jit(solution)/shard_map/ppermute | solution.py:40
  112.9 2.0 %collective-permute-done.26.refs_1_ = bf16[32,3584]{1,0:T(8,128)(2,1)S(1)} collective-permute-done((bf16[32,3584]{1,0:T(8,128)(2,1)S(1)}, bf16[32,3584]{1,0:T(8,128)(2,1)S(1)}, u32[]{:S(2)}, u32[]{:S(2)}) %collective-permute-start.26) | collective-permute-done | bytes 229408 | tf_op jit(solution)/shard_map/ppermute | solution.py:40
  115.0 6.8 %feed.2 = (f32[32,3584]{1,0:T(8,128)S(1)}, f32[32,3584]{1,0:T(8,128)S(1)}, bf16[32,3584]{1,0:T(8,128)(2,1)S(1)}, f32[32,3584]{1,0:T(8,128)S(1)}) custom-call(bf16[32,3584]{1,0:T(8,128)(2,1)S(1)} %get-tuple-element.103.refs_0_, bf16[32,3584]{1,0:T(8,128)(2,1)S(1)} %collective-permute-done.26.refs_1_, bf16[32,3584]{1,0:T(8,128)(2,1)S(1)} %collective-permute-done.27.refs_2_, ...), custom_call_target="tpu_custom_call" | custom-call | flops 3523215360 | bytes 28000000 | tf_op jit(solution)/shard_map/feed/pallas_call | solution.py:324
  122.2 6.8 %feed.3 = (bf16[32,3584]{1,0:T(8,128)(2,1)S(1)}, bf16[32,3584]{1,0:T(8,128)(2,1)S(1)}, bf16[32,3584]{1,0:T(8,128)(2,1)S(1)}, bf16[32,3584]{1,0:T(8,128)(2,1)S(1)}) custom-call(bf16[32,3584]{1,0:T(8,128)(2,1)S(1)} %collective-permute-done.29.refs_0_, bf16[32,3584]{1,0:T(8,128)(2,1)S(1)} %collective-permute-done.30.refs_1_, ...), custom_call_target="tpu_custom_call" | custom-call | flops 3523215360 | bytes 28000000 | tf_op jit(solution)/shard_map/feed/pallas_call | solution.py:324
  129.0 2.9 %collective-permute-start.37 = (bf16[32,3584]{1,0:T(8,128)(2,1)S(1)}, bf16[32,3584]{1,0:T(8,128)(2,1)S(1)}, u32[]{:S(2)}, u32[]{:S(2)}) collective-permute-start(bf16[32,3584]{1,0:T(8,128)(2,1)S(1)} %get-tuple-element.112), channel_id=1, source_target_pairs={{0,72},{1,73},{2,74},{3,75},{4,76},{5,77},{6,78},{7,79},{8,0},{9,1... | collective-permute-start | bytes 688136 | tf_op jit(solution)/shard_map/ppermute | solution.py:40
  131.9 1.5 collective-permute-start.35
  133.9 1.5 collective-permute-start.39
  135.4 3.2 %collective-permute-start.34 = (bf16[32,3584]{1,0:T(8,128)(2,1)S(1)}, bf16[32,3584]{1,0:T(8,128)(2,1)S(1)}, u32[]{:S(2)}, u32[]{:S(2)}) collective-permute-start(bf16[32,3584]{1,0:T(8,128)(2,1)S(1)} %get-tuple-element.109), channel_id=1, source_target_pairs={{0,72},{1,73},{2,74},{3,75},{4,76},{5,77},{6,78},{7,79},{8,0},{9,1... | collective-permute-start | bytes 688136 | tf_op jit(solution)/shard_map/ppermute | solution.py:40
  138.7 1.7 %collective-permute-start.38 = (bf16[32,3584]{1,0:T(8,128)(2,1)S(1)}, bf16[32,3584]{1,0:T(8,128)(2,1)S(1)}, u32[]{:S(2)}, u32[]{:S(2)}) collective-permute-start(bf16[32,3584]{1,0:T(8,128)(2,1)S(1)} %fold.6), channel_id=1, source_target_pairs={{0,6},{1,7},{2,0},{3,1},{4,2},{5,3},{6,4},{7,5},{8,14},{9,15},{10,... | collective-permute-start | bytes 688136 | tf_op jit(solution)/shard_map/ppermute | solution.py:40
  141.2 1.4 collective-permute-start.41
  142.6 0.9 collective-permute-done.39.refs_3_
  143.5 4.8 %collective-permute-done.36.refs_1_ = bf16[32,3584]{1,0:T(8,128)(2,1)S(1)} collective-permute-done((bf16[32,3584]{1,0:T(8,128)(2,1)S(1)}, bf16[32,3584]{1,0:T(8,128)(2,1)S(1)}, u32[]{:S(2)}, u32[]{:S(2)}) %collective-permute-start.36) | collective-permute-done | bytes 229408 | tf_op jit(solution)/shard_map/ppermute | solution.py:40
  (86 shorter events, 8.1 us)
Async XLA Ops:
  0.6 20.6 %collective-permute-start.4 = (bf16[1024,3584]{1,0:T(8,128)(2,1)}, bf16[1024,3584]{1,0:T(8,128)(2,1)}, u32[]{:S(2)}, u32[]{:S(2)}) collective-permute-start(bf16[1024,3584]{1,0:T(8,128)(2,1)} %out_own.1), channel_id=1, source_target_pairs={{0,1},{1,0},{2,3},{3,2},{4,5},{5,4},{6,7},{7,6},{8,9},{9,8},{10,11... | collective-permute-start | bytes 22020104 | tf_op jit(solution)/shard_map/ppermute | solution.py:44
  0.7 29.7 %collective-permute-start.5 = (bf16[3584,640]{1,0:T(8,128)(2,1)}, bf16[3584,640]{1,0:T(8,128)(2,1)}, u32[]{:S(2)}, u32[]{:S(2)}) collective-permute-start(bf16[3584,640]{1,0:T(8,128)(2,1)} %g0), channel_id=1, source_target_pairs={{0,1},{1,0},{2,3},{3,2},{4,5},{5,4},{6,7},{7,6},{8,9},{9,8},{10,11... | collective-permute-start | bytes 13762568 | tf_op jit(solution)/shard_map/ppermute | solution.py:44
  1.2 9.5 %collective-permute-start = (bf16[8,512,128]{2,1,0:T(8,128)(2,1)}, bf16[8,512,128]{2,1,0:T(8,128)(2,1)S(1)}, u32[]{:S(2)}, u32[]{:S(2)}) collective-permute-start(bf16[8,512,128]{2,1,0:T(8,128)(2,1)} %up_own.1), channel_id=1, source_target_pairs={{0,1},{1,0},{2,3},{3,2},{4,5},{5,4},{6,7},{7,6},{8,9},{9,8},{10,11... | collective-permute-start | bytes 3145736 | tf_op jit(solution)/shard_map/ppermute | solution.py:44
  10.7 18.6 %collective-permute-start.3 = (bf16[32,16,512]{2,1,0:T(8,128)(2,1)}, bf16[32,16,512]{2,1,0:T(8,128)(2,1)S(1)}, u32[]{:S(2)}, u32[]{:S(2)}) collective-permute-start(bf16[32,16,512]{2,1,0:T(8,128)(2,1)} %get-tuple-element.64), channel_id=1, source_target_pairs={{0,72},{1,73},{2,74},{3,75},{4,76},{5,77},{6,78},{7,79},{8,0},{9,1... | collective-permute-start | bytes 1572872 | tf_op jit(solution)/shard_map/ppermute | solution.py:40
  14.8 15.3 %collective-permute-start.2 = (bf16[32,16,512]{2,1,0:T(8,128)(2,1)}, bf16[32,16,512]{2,1,0:T(8,128)(2,1)S(1)}, u32[]{:S(2)}, u32[]{:S(2)}) collective-permute-start(bf16[32,16,512]{2,1,0:T(8,128)(2,1)} %get-tuple-element.62), channel_id=1, source_target_pairs={{0,8},{1,9},{2,10},{3,11},{4,12},{5,13},{6,14},{7,15},{8,64},{9,65... | collective-permute-start | bytes 1572872 | tf_op jit(solution)/shard_map/ppermute | solution.py:40
  14.8 15.6 %collective-permute-start.1 = (bf16[32,16,512]{2,1,0:T(8,128)(2,1)}, bf16[32,16,512]{2,1,0:T(8,128)(2,1)S(1)}, u32[]{:S(2)}, u32[]{:S(2)}) collective-permute-start(bf16[32,16,512]{2,1,0:T(8,128)(2,1)} %get-tuple-element.60), channel_id=1, source_target_pairs={{0,4},{1,5},{2,6},{3,7},{4,0},{5,1},{6,2},{7,3},{8,12},{9,13},{10,... | collective-permute-start | bytes 1572872 | tf_op jit(solution)/shard_map/ppermute | solution.py:40
  21.2 26.2 %slice-start = ((s8[4587520]{0:T(1024)(128)(4,1)}), s8[4194304]{0:T(1024)(128)(4,1)S(1)}, s32[]{:S(2)}) async-start(s8[4587520]{0:T(1024)(128)(4,1)} %bitcast.4), calls=%async_computation | async-start | bytes 8388608
  21.2 26.3 %slice-start.2 = ((s8[4587520]{0:T(1024)(128)(4,1)}), s8[4194304]{0:T(1024)(128)(4,1)S(1)}, s32[]{:S(2)}) async-start(s8[4587520]{0:T(1024)(128)(4,1)} %bitcast.6), calls=%async_computation.2 | async-start | bytes 8388608
  21.3 26.3 %slice-start.3 = ((s8[4587520]{0:T(1024)(128)(4,1)}), s8[393216]{0:T(1024)(128)(4,1)S(1)}, s32[]{:S(2)}) async-start(s8[4587520]{0:T(1024)(128)(4,1)} %bitcast.6), calls=%async_computation.3 | async-start | bytes 786432
  21.3 30.6 %copy-start.5 = (bf16[32,16,512]{2,1,0:T(8,128)(2,1)S(1)}, bf16[32,16,512]{2,1,0:T(8,128)(2,1)}, u32[]{:S(2)}) copy-start(bf16[32,16,512]{2,1,0:T(8,128)(2,1)} %get-tuple-element.77) | copy-start | bytes 1572868
  21.3 36.8 %copy-start.4 = (bf16[32,16,512]{2,1,0:T(8,128)(2,1)S(1)}, bf16[32,16,512]{2,1,0:T(8,128)(2,1)}, u32[]{:S(2)}) copy-start(bf16[32,16,512]{2,1,0:T(8,128)(2,1)} %get-tuple-element.90) | copy-start | bytes 1572868
  21.3 8.0 %collective-permute-start.6 = (bf16[2,64,576]{2,1,0:T(8,128)(2,1)S(1)}, bf16[2,64,576]{2,1,0:T(8,128)(2,1)S(1)}, u32[]{:S(2)}, u32[]{:S(2)}) collective-permute-start(bf16[2,64,576]{2,1,0:T(8,128)(2,1)S(1)} %get-tuple-element.67.mine_ref), channel_id=1, source_target_pairs={{0,16},{16,0},{32,48},{48,32},{64,80},{80,64},{96,112},{112,96},{1... | collective-permute-start | bytes 442376 | tf_op jit(solution)/shard_map/ppermute | solution.py:484
  29.3 31.8 %copy-start = (bf16[32,16,512]{2,1,0:T(8,128)(2,1)S(1)}, bf16[32,16,512]{2,1,0:T(8,128)(2,1)}, u32[]{:S(2)}) copy-start(bf16[32,16,512]{2,1,0:T(8,128)(2,1)} %get-tuple-element.72.refs_0_) | copy-start | bytes 1572868
  30.5 14.3 %collective-permute-start.7 = (bf16[32,16,512]{2,1,0:T(8,128)(2,1)S(1)}, bf16[32,16,512]{2,1,0:T(8,128)(2,1)S(1)}, u32[]{:S(2)}, u32[]{:S(2)}) collective-permute-start(bf16[32,16,512]{2,1,0:T(8,128)(2,1)S(1)} %copy-done.7), channel_id=1, source_target_pairs={{0,8},{1,9},{2,10},{3,11},{4,12},{5,13},{6,14},{7,15},{8,64},{9,65... | collective-permute-start | bytes 1572872 | tf_op jit(solution)/shard_map/ppermute | solution.py:40
  30.5 14.3 %collective-permute-start.8 = (bf16[32,16,512]{2,1,0:T(8,128)(2,1)S(1)}, bf16[32,16,512]{2,1,0:T(8,128)(2,1)S(1)}, u32[]{:S(2)}, u32[]{:S(2)}) collective-permute-start(bf16[32,16,512]{2,1,0:T(8,128)(2,1)S(1)} %copy-done.6), channel_id=1, source_target_pairs={{0,72},{1,73},{2,74},{3,75},{4,76},{5,77},{6,78},{7,79},{8,0},{9,1... | collective-permute-start | bytes 1572872 | tf_op jit(solution)/shard_map/ppermute | solution.py:40
  33.7 13.7 %collective-permute-start.10 = (bf16[32,16,512]{2,1,0:T(8,128)(2,1)S(1)}, bf16[32,16,512]{2,1,0:T(8,128)(2,1)S(1)}, u32[]{:S(2)}, u32[]{:S(2)}) collective-permute-start(bf16[32,16,512]{2,1,0:T(8,128)(2,1)S(1)} %collective-permute-done.2), channel_id=1, source_target_pairs={{0,2},{1,3},{2,4},{3,5},{4,6},{5,7},{6,0},{7,1},{8,10},{9,11},{10,... | collective-permute-start | bytes 1572872 | tf_op jit(solution)/shard_map/ppermute | solution.py:40
  35.2 12.2 %collective-permute-start.14 = (bf16[32,16,512]{2,1,0:T(8,128)(2,1)S(1)}, bf16[32,16,512]{2,1,0:T(8,128)(2,1)S(1)}, u32[]{:S(2)}, u32[]{:S(2)}) collective-permute-start(bf16[32,16,512]{2,1,0:T(8,128)(2,1)S(1)} %collective-permute-done.3), channel_id=1, source_target_pairs={{0,6},{1,7},{2,0},{3,1},{4,2},{5,3},{6,4},{7,5},{8,14},{9,15},{10,... | collective-permute-start | bytes 1572872 | tf_op jit(solution)/shard_map/ppermute | solution.py:40
  37.6 6.9 %collective-permute-start.11 = (bf16[2,64,576]{2,1,0:T(8,128)(2,1)S(1)}, bf16[2,64,576]{2,1,0:T(8,128)(2,1)S(1)}, u32[]{:S(2)}, u32[]{:S(2)}) collective-permute-start(bf16[2,64,576]{2,1,0:T(8,128)(2,1)S(1)} %pick.3.mine_ref), channel_id=1, source_target_pairs={{0,32},{16,48},{32,0},{48,16},{64,96},{80,112},{96,64},{112,80},{1... | collective-permute-start | bytes 442376 | tf_op jit(solution)/shard_map/ppermute | solution.py:484
  47.5 19.8 %collective-permute-start.15 = (bf16[3584,640]{1,0:T(8,128)(2,1)S(1)}, bf16[3584,640]{1,0:T(8,128)(2,1)S(1)}, u32[]{:S(2)}, u32[]{:S(2)}) collective-permute-start(bf16[3584,640]{1,0:T(8,128)(2,1)S(1)} %bitcast.5), channel_id=1, source_target_pairs={{0,1},{1,0},{2,3},{3,2},{4,5},{5,4},{6,7},{7,6},{8,9},{9,8},{10,11... | collective-permute-start | bytes 13762568 | tf_op jit(solution)/shard_map/ppermute | solution.py:44
  47.6 19.7 %collective-permute-start.16 = (bf16[640,3584]{1,0:T(8,128)(2,1)S(1)}, bf16[640,3584]{1,0:T(8,128)(2,1)}, u32[]{:S(2)}, u32[]{:S(2)}) collective-permute-start(bf16[640,3584]{1,0:T(8,128)(2,1)S(1)} %bitcast.7), channel_id=1, source_target_pairs={{0,1},{1,0},{2,3},{3,2},{4,5},{5,4},{6,7},{7,6},{8,9},{9,8},{10,11... | collective-permute-start | bytes 13762568 | tf_op jit(solution)/shard_map/ppermute | solution.py:44
  48.0 16.3 %collective-permute-start.13 = (bf16[32,16,512]{2,1,0:T(8,128)(2,1)S(1)}, bf16[32,16,512]{2,1,0:T(8,128)(2,1)S(1)}, u32[]{:S(2)}, u32[]{:S(2)}) collective-permute-start(bf16[32,16,512]{2,1,0:T(8,128)(2,1)S(1)} %collective-permute-done.8), channel_id=1, source_target_pairs={{0,4},{1,5},{2,6},{3,7},{4,0},{5,1},{6,2},{7,3},{8,12},{9,13},{10,... | collective-permute-start | bytes 1572872 | tf_op jit(solution)/shard_map/ppermute | solution.py:40
  50.7 7.4 %collective-permute-start.12 = (bf16[2,64,576]{2,1,0:T(8,128)(2,1)S(1)}, bf16[2,64,576]{2,1,0:T(8,128)(2,1)S(1)}, u32[]{:S(2)}, u32[]{:S(2)}) collective-permute-start(bf16[2,64,576]{2,1,0:T(8,128)(2,1)S(1)} %pick.4.mine_ref), channel_id=1, source_target_pairs={{0,64},{16,80},{32,96},{48,112},{64,0},{80,16},{96,32},{112,48},{1... | collective-permute-start | bytes 442376 | tf_op jit(solution)/shard_map/ppermute | solution.py:484
  51.8 23.5 %collective-permute-start.9 = (bf16[32,16,512]{2,1,0:T(8,128)(2,1)S(1)}, bf16[32,16,512]{2,1,0:T(8,128)(2,1)S(1)}, u32[]{:S(2)}, u32[]{:S(2)}) collective-permute-start(bf16[32,16,512]{2,1,0:T(8,128)(2,1)S(1)} %copy-done.5), channel_id=1, source_target_pairs={{0,2},{1,3},{2,4},{3,5},{4,6},{5,7},{6,0},{7,1},{8,10},{9,11},{10,... | collective-permute-start | bytes 1572872 | tf_op jit(solution)/shard_map/ppermute | solution.py:40
  58.1 17.3 %collective-permute-start.17 = (bf16[32,16,512]{2,1,0:T(8,128)(2,1)S(1)}, bf16[32,16,512]{2,1,0:T(8,128)(2,1)S(1)}, u32[]{:S(2)}, u32[]{:S(2)}) collective-permute-start(bf16[32,16,512]{2,1,0:T(8,128)(2,1)S(1)} %copy-done.4), channel_id=1, source_target_pairs={{0,6},{1,7},{2,0},{3,1},{4,2},{5,3},{6,4},{7,5},{8,14},{9,15},{10,... | collective-permute-start | bytes 1572872 | tf_op jit(solution)/shard_map/ppermute | solution.py:40
  70.5 11.7 %collective-permute-start.18 = (bf16[32,3584]{1,0:T(8,128)(2,1)S(1)}, bf16[32,3584]{1,0:T(8,128)(2,1)S(1)}, u32[]{:S(2)}, u32[]{:S(2)}) collective-permute-start(bf16[32,3584]{1,0:T(8,128)(2,1)S(1)} %get-tuple-element.93), channel_id=1, source_target_pairs={{0,72},{1,73},{2,74},{3,75},{4,76},{5,77},{6,78},{7,79},{8,0},{9,1... | collective-permute-start | bytes 688136 | tf_op jit(solution)/shard_map/ppermute | solution.py:40
  72.1 12.0 %collective-permute-start.19 = (bf16[32,3584]{1,0:T(8,128)(2,1)S(1)}, bf16[32,3584]{1,0:T(8,128)(2,1)S(1)}, u32[]{:S(2)}, u32[]{:S(2)}) collective-permute-start(bf16[32,3584]{1,0:T(8,128)(2,1)S(1)} %get-tuple-element.95), channel_id=1, source_target_pairs={{0,8},{1,9},{2,10},{3,11},{4,12},{5,13},{6,14},{7,15},{8,64},{9,65... | collective-permute-start | bytes 688136 | tf_op jit(solution)/shard_map/ppermute | solution.py:40
  72.7 14.3 %collective-permute-start.21 = (bf16[32,3584]{1,0:T(8,128)(2,1)S(1)}, bf16[32,3584]{1,0:T(8,128)(2,1)S(1)}, u32[]{:S(2)}, u32[]{:S(2)}) collective-permute-start(bf16[32,3584]{1,0:T(8,128)(2,1)S(1)} %get-tuple-element.97), channel_id=1, source_target_pairs={{0,4},{1,5},{2,6},{3,7},{4,0},{5,1},{6,2},{7,3},{8,12},{9,13},{10,... | collective-permute-start | bytes 688136 | tf_op jit(solution)/shard_map/ppermute | solution.py:40
  80.1 15.3 %collective-permute-start.24 = (bf16[32,3584]{1,0:T(8,128)(2,1)S(1)}, bf16[32,3584]{1,0:T(8,128)(2,1)S(1)}, u32[]{:S(2)}, u32[]{:S(2)}) collective-permute-start(bf16[32,3584]{1,0:T(8,128)(2,1)S(1)} %get-tuple-element.101), channel_id=1, source_target_pairs={{0,4},{1,5},{2,6},{3,7},{4,0},{5,1},{6,2},{7,3},{8,12},{9,13},{10,... | collective-permute-start | bytes 688136 | tf_op jit(solution)/shard_map/ppermute | solution.py:40
  82.3 13.2 %collective-permute-start.23 = (bf16[32,3584]{1,0:T(8,128)(2,1)S(1)}, bf16[32,3584]{1,0:T(8,128)(2,1)S(1)}, u32[]{:S(2)}, u32[]{:S(2)}) collective-permute-start(bf16[32,3584]{1,0:T(8,128)(2,1)S(1)} %fold.4), channel_id=1, source_target_pairs={{0,6},{1,7},{2,0},{3,1},{4,2},{5,3},{6,4},{7,5},{8,14},{9,15},{10,... | collective-permute-start | bytes 688136 | tf_op jit(solution)/shard_map/ppermute | solution.py:40
  84.2 11.3 %collective-permute-start.25 = (bf16[32,3584]{1,0:T(8,128)(2,1)S(1)}, bf16[32,3584]{1,0:T(8,128)(2,1)S(1)}, u32[]{:S(2)}, u32[]{:S(2)}) collective-permute-start(bf16[32,3584]{1,0:T(8,128)(2,1)S(1)} %fold.5), channel_id=1, source_target_pairs={{0,2},{1,3},{2,4},{3,5},{4,6},{5,7},{6,0},{7,1},{8,10},{9,11},{10,... | collective-permute-start | bytes 688136 | tf_op jit(solution)/shard_map/ppermute | solution.py:40
  84.5 10.9 %collective-permute-start.20 = (bf16[32,3584]{1,0:T(8,128)(2,1)S(1)}, bf16[32,3584]{1,0:T(8,128)(2,1)S(1)}, u32[]{:S(2)}, u32[]{:S(2)}) collective-permute-start(bf16[32,3584]{1,0:T(8,128)(2,1)S(1)} %get-tuple-element.96), channel_id=1, source_target_pairs={{0,72},{1,73},{2,74},{3,75},{4,76},{5,77},{6,78},{7,79},{8,0},{9,1... | collective-permute-start | bytes 688136 | tf_op jit(solution)/shard_map/ppermute | solution.py:40
  87.0 8.5 %collective-permute-start.22 = (bf16[32,3584]{1,0:T(8,128)(2,1)S(1)}, bf16[32,3584]{1,0:T(8,128)(2,1)S(1)}, u32[]{:S(2)}, u32[]{:S(2)}) collective-permute-start(bf16[32,3584]{1,0:T(8,128)(2,1)S(1)} %collective-permute-done.21), channel_id=1, source_target_pairs={{0,8},{1,9},{2,10},{3,11},{4,12},{5,13},{6,14},{7,15},{8,64},{9,65... | collective-permute-start | bytes 688136 | tf_op jit(solution)/shard_map/ppermute | solution.py:40
  95.9 7.9 %collective-permute-start.31 = (bf16[32,3584]{1,0:T(8,128)(2,1)S(1)}, bf16[32,3584]{1,0:T(8,128)(2,1)S(1)}, u32[]{:S(2)}, u32[]{:S(2)}) collective-permute-start(bf16[32,3584]{1,0:T(8,128)(2,1)S(1)} %get-tuple-element.103.refs_0_), channel_id=1, source_target_pairs={{0,72},{1,73},{2,74},{3,75},{4,76},{5,77},{6,78},{7,79},{8,0},{9,1... | collective-permute-start | bytes 688136 | tf_op jit(solution)/shard_map/ppermute | solution.py:40
  99.2 13.5 %collective-permute-start.28 = (bf16[32,3584]{1,0:T(8,128)(2,1)S(1)}, bf16[32,3584]{1,0:T(8,128)(2,1)S(1)}, u32[]{:S(2)}, u32[]{:S(2)}) collective-permute-start(bf16[32,3584]{1,0:T(8,128)(2,1)S(1)} %get-tuple-element.103.refs_0_), channel_id=1, source_target_pairs={{0,6},{1,7},{2,0},{3,1},{4,2},{5,3},{6,4},{7,5},{8,14},{9,15},{10,... | collective-permute-start | bytes 688136 | tf_op jit(solution)/shard_map/ppermute | solution.py:40
  102.4 12.6 %collective-permute-start.26 = (bf16[32,3584]{1,0:T(8,128)(2,1)S(1)}, bf16[32,3584]{1,0:T(8,128)(2,1)S(1)}, u32[]{:S(2)}, u32[]{:S(2)}) collective-permute-start(bf16[32,3584]{1,0:T(8,128)(2,1)S(1)} %get-tuple-element.103.refs_0_), channel_id=1, source_target_pairs={{0,2},{1,3},{2,4},{3,5},{4,6},{5,7},{6,0},{7,1},{8,10},{9,11},{10,... | collective-permute-start | bytes 688136 | tf_op jit(solution)/shard_map/ppermute | solution.py:40
  102.4 12.6 %collective-permute-start.27 = (bf16[32,3584]{1,0:T(8,128)(2,1)S(1)}, bf16[32,3584]{1,0:T(8,128)(2,1)S(1)}, u32[]{:S(2)}, u32[]{:S(2)}) collective-permute-start(bf16[32,3584]{1,0:T(8,128)(2,1)S(1)} %get-tuple-element.103.refs_0_), channel_id=1, source_target_pairs={{0,4},{1,5},{2,6},{3,7},{4,0},{5,1},{6,2},{7,3},{8,12},{9,13},{10,... | collective-permute-start | bytes 688136 | tf_op jit(solution)/shard_map/ppermute | solution.py:40
  103.8 17.9 %collective-permute-start.29 = (bf16[32,3584]{1,0:T(8,128)(2,1)S(1)}, bf16[32,3584]{1,0:T(8,128)(2,1)S(1)}, u32[]{:S(2)}, u32[]{:S(2)}) collective-permute-start(bf16[32,3584]{1,0:T(8,128)(2,1)S(1)} %get-tuple-element.103.refs_0_), channel_id=1, source_target_pairs={{0,8},{1,9},{2,10},{3,11},{4,12},{5,13},{6,14},{7,15},{8,64},{9,65... | collective-permute-start | bytes 688136 | tf_op jit(solution)/shard_map/ppermute | solution.py:40
  112.7 9.1 %collective-permute-start.32 = (bf16[32,3584]{1,0:T(8,128)(2,1)S(1)}, bf16[32,3584]{1,0:T(8,128)(2,1)S(1)}, u32[]{:S(2)}, u32[]{:S(2)}) collective-permute-start(bf16[32,3584]{1,0:T(8,128)(2,1)S(1)} %collective-permute-done.31), channel_id=1, source_target_pairs={{0,4},{1,5},{2,6},{3,7},{4,0},{5,1},{6,2},{7,3},{8,12},{9,13},{10,... | collective-permute-start | bytes 688136 | tf_op jit(solution)/shard_map/ppermute | solution.py:40
  112.7 9.1 %collective-permute-start.33 = (bf16[32,3584]{1,0:T(8,128)(2,1)S(1)}, bf16[32,3584]{1,0:T(8,128)(2,1)S(1)}, u32[]{:S(2)}, u32[]{:S(2)}) collective-permute-start(bf16[32,3584]{1,0:T(8,128)(2,1)S(1)} %collective-permute-done.28.refs_3_), channel_id=1, source_target_pairs={{0,72},{1,73},{2,74},{3,75},{4,76},{5,77},{6,78},{7,79},{8,0},{9,1... | collective-permute-start | bytes 688136 | tf_op jit(solution)/shard_map/ppermute | solution.py:40
  115.0 7.2 %collective-permute-start.30 = (bf16[32,3584]{1,0:T(8,128)(2,1)S(1)}, bf16[32,3584]{1,0:T(8,128)(2,1)S(1)}, u32[]{:S(2)}, u32[]{:S(2)}) collective-permute-start(bf16[32,3584]{1,0:T(8,128)(2,1)S(1)} %collective-permute-done.26.refs_1_), channel_id=1, source_target_pairs={{0,8},{1,9},{2,10},{3,11},{4,12},{5,13},{6,14},{7,15},{8,64},{9,65... | collective-permute-start | bytes 688136 | tf_op jit(solution)/shard_map/ppermute | solution.py:40
  129.0 9.7 %collective-permute-start.37 = (bf16[32,3584]{1,0:T(8,128)(2,1)S(1)}, bf16[32,3584]{1,0:T(8,128)(2,1)S(1)}, u32[]{:S(2)}, u32[]{:S(2)}) collective-permute-start(bf16[32,3584]{1,0:T(8,128)(2,1)S(1)} %get-tuple-element.112), channel_id=1, source_target_pairs={{0,72},{1,73},{2,74},{3,75},{4,76},{5,77},{6,78},{7,79},{8,0},{9,1... | collective-permute-start | bytes 688136 | tf_op jit(solution)/shard_map/ppermute | solution.py:40
  131.9 9.2 %collective-permute-start.35 = (bf16[32,3584]{1,0:T(8,128)(2,1)S(1)}, bf16[32,3584]{1,0:T(8,128)(2,1)S(1)}, u32[]{:S(2)}, u32[]{:S(2)}) collective-permute-start(bf16[32,3584]{1,0:T(8,128)(2,1)S(1)} %get-tuple-element.110), channel_id=1, source_target_pairs={{0,4},{1,5},{2,6},{3,7},{4,0},{5,1},{6,2},{7,3},{8,12},{9,13},{10,... | collective-permute-start | bytes 688136 | tf_op jit(solution)/shard_map/ppermute | solution.py:40
  133.3 7.7 %collective-permute-start.40 = (bf16[32,3584]{1,0:T(8,128)(2,1)S(1)}, bf16[32,3584]{1,0:T(8,128)(2,1)S(1)}, u32[]{:S(2)}, u32[]{:S(2)}) collective-permute-start(bf16[32,3584]{1,0:T(8,128)(2,1)S(1)} %get-tuple-element.115), channel_id=1, source_target_pairs={{0,8},{1,9},{2,10},{3,11},{4,12},{5,13},{6,14},{7,15},{8,64},{9,65... | collective-permute-start | bytes 688136 | tf_op jit(solution)/shard_map/ppermute | solution.py:40
  133.9 9.6 %collective-permute-start.39 = (bf16[32,3584]{1,0:T(8,128)(2,1)S(1)}, bf16[32,3584]{1,0:T(8,128)(2,1)S(1)}, u32[]{:S(2)}, u32[]{:S(2)}) collective-permute-start(bf16[32,3584]{1,0:T(8,128)(2,1)S(1)} %get-tuple-element.113), channel_id=1, source_target_pairs={{0,4},{1,5},{2,6},{3,7},{4,0},{5,1},{6,2},{7,3},{8,12},{9,13},{10,... | collective-permute-start | bytes 688136 | tf_op jit(solution)/shard_map/ppermute | solution.py:40
  135.4 8.1 %collective-permute-start.34 = (bf16[32,3584]{1,0:T(8,128)(2,1)S(1)}, bf16[32,3584]{1,0:T(8,128)(2,1)S(1)}, u32[]{:S(2)}, u32[]{:S(2)}) collective-permute-start(bf16[32,3584]{1,0:T(8,128)(2,1)S(1)} %get-tuple-element.109), channel_id=1, source_target_pairs={{0,72},{1,73},{2,74},{3,75},{4,76},{5,77},{6,78},{7,79},{8,0},{9,1... | collective-permute-start | bytes 688136 | tf_op jit(solution)/shard_map/ppermute | solution.py:40
  138.7 9.6 %collective-permute-start.38 = (bf16[32,3584]{1,0:T(8,128)(2,1)S(1)}, bf16[32,3584]{1,0:T(8,128)(2,1)S(1)}, u32[]{:S(2)}, u32[]{:S(2)}) collective-permute-start(bf16[32,3584]{1,0:T(8,128)(2,1)S(1)} %fold.6), channel_id=1, source_target_pairs={{0,6},{1,7},{2,0},{3,1},{4,2},{5,3},{6,4},{7,5},{8,14},{9,15},{10,... | collective-permute-start | bytes 688136 | tf_op jit(solution)/shard_map/ppermute | solution.py:40
  141.1 7.2 %collective-permute-start.36 = (bf16[32,3584]{1,0:T(8,128)(2,1)S(1)}, bf16[32,3584]{1,0:T(8,128)(2,1)S(1)}, u32[]{:S(2)}, u32[]{:S(2)}) collective-permute-start(bf16[32,3584]{1,0:T(8,128)(2,1)S(1)} %collective-permute-done.35), channel_id=1, source_target_pairs={{0,8},{1,9},{2,10},{3,11},{4,12},{5,13},{6,14},{7,15},{8,64},{9,65... | collective-permute-start | bytes 688136 | tf_op jit(solution)/shard_map/ppermute | solution.py:40
  141.2 7.3 %collective-permute-start.41 = (bf16[32,3584]{1,0:T(8,128)(2,1)S(1)}, bf16[32,3584]{1,0:T(8,128)(2,1)S(1)}, u32[]{:S(2)}, u32[]{:S(2)}) collective-permute-start(bf16[32,3584]{1,0:T(8,128)(2,1)S(1)} %fold.7), channel_id=1, source_target_pairs={{0,2},{1,3},{2,4},{3,5},{4,6},{5,7},{6,0},{7,1},{8,10},{9,11},{10,... | collective-permute-start | bytes 688136 | tf_op jit(solution)/shard_map/ppermute | solution.py:40
  (6 other events, 83.4 us)

commit v5 on v4

--- a/solution.py
+++ b/solution.py
@@ -549,12 +549,12 @@
     values_a = values_of([after(own0, far_in0), near2], up2)
     values_b = values_of([far_in0, far1], up2)
     values_c = values_of([far2, far3], up2)
-    block = page_pick(block, after(page_trade(block, 2), far2), offset, 2)
-    values_b = after(values_b, values_a, block, fup_other, down_other)
+    block = page_pick(block, page_trade(after(block, values_a), 2), offset, 2)
+    values_b = after(values_b, values_a, fup_other, down_other)
     far = project([(values_b, 0, 2 * n), (values_c, 0, 2 * n)], out2, far_shapes)
     back1, back3 = shift(far[1], dz=-1), shift(far[3], dz=1)
     aside = shift(far[2], dx=-2)
-    values_d = values_of([after(near1, far[0]), near3], up2)
+    values_d = values_of([after(near1, far[0], block), near3], up2)
     near = project(
         [(values_a, 0, n), (values_d, 0, n), (values_a, n, n), (values_d, n, n)], out2, near_shapes
     )

time: 150 us -> 150 us (level)
    ppermute x34, waiting for transfers between devices: 23 us -> 28.6 us  [shift(): return lax.ppermute(value, GRID, pairs)]
    ppermute x3, waiting for transfers between devices: 8.84 us -> 3.63 us  [page_trade(): return lax.ppermute(block, 'dp', [(d, d ^ 1 << bit) for d in range(8)])]
  transfers between devices with their start and end apart: 42 -> 42, of which waited for: 15 -> 14; matrix products, arithmetic and copies ran while one was open for 0% -> 0% of each run, Pallas kernels for 32% -> 32%
where the time goes in v5:
time: 150 us
  starting transfers between devices  58.6 us (39%)
  Pallas kernels  54.7 us (36%)
  waiting for transfers between devices  33.3 us (22%)
  between operations  2.41 us (2%)
    ppermute x34, starting transfers between devices, shift(): return lax.ppermute(value, GRID, pairs)  51.3 us
    ppermute x34, waiting for transfers between devices, shift(): return lax.ppermute(value, GRID, pairs)  28.6 us
    pallas_call x2, Pallas kernels, feed(): pl.pallas_call(functools.partial(feed_kernel, blocks=len(blocks)), in_spe...  13.5 us
    pallas_call x1, Pallas kernels, attend(): pl.pallas_call(functools.partial(attend_kernel, first_request=first), gri...  8.32 us
    pallas_call x1, Pallas kernels, hold_feed(): pl.pallas_call(hold_feed_kernel, in_specs=[HBM_SPEC, ANY_SPEC] * 3, out_s...  8.27 us
    pallas_call x2, Pallas kernels, project(): pl.pallas_call(functools.partial(project_kernel, parts=parts), in_specs=[...  6.41 us
    pallas_call x1, Pallas kernels, hold_projection(): pl.pallas_call(hold_projection_kernel, in_specs=[HBM_SPEC, ANY_SPEC] * 2,...  6.29 us
    pallas_call x4, Pallas kernels, values_of(): pl.pallas_call(functools.partial(values_kernel, blocks=len(blocks)), in_s...  6.11 us
  transfers between devices with their start and end apart: 42, of which 14 were waited for; matrix products, arithmetic and copies ran while one was open for 0% of the time, Pallas kernels for 32%

profile of v5, /device:TPU:0, one launch (start us, length us, event | category | flops | bytes accessed | tf_op | source)
XLA Modules:
  0.0 149.9 jit_solution(15990821969571146733)
XLA Ops:
  1.3 8.3 %attend.1 = (bf16[32,16,512]{2,1,0:T(8,128)(2,1)}, bf16[32,16,512]{2,1,0:T(8,128)(2,1)}, bf16[32,16,512]{2,1,0:T(8,128)(2,1)}, bf16[32,16,512]{2,1,0:T(8,128)(2,...) custom-call(s32[16]{0:T(128)} %lens_ref.1, ...), custom_call_target="tpu_custom_call" | custom-call | flops 2281701376 | bytes 12800000 | tf_op jit(solution)/shard_map/attend/pallas_call | solution.py:108
  9.6 1.1 collective-permute-done.up_other
  10.7 4.1 %collective-permute-start.3 = (bf16[32,16,512]{2,1,0:T(8,128)(2,1)}, bf16[32,16,512]{2,1,0:T(8,128)(2,1)S(1)}, u32[]{:S(2)}, u32[]{:S(2)}) collective-permute-start(bf16[32,16,512]{2,1,0:T(8,128)(2,1)} %get-tuple-element.64), channel_id=1, source_target_pairs={{0,72},{1,73},{2,74},{3,75},{4,76},{5,77},{6,78},{7,79},{8,0},{9,1... | collective-permute-start | bytes 1572872 | tf_op jit(solution)/shard_map/ppermute | solution.py:40
  14.8 3.0 %collective-permute-start.1 = (bf16[32,16,512]{2,1,0:T(8,128)(2,1)}, bf16[32,16,512]{2,1,0:T(8,128)(2,1)S(1)}, u32[]{:S(2)}, u32[]{:S(2)}) collective-permute-start(bf16[32,16,512]{2,1,0:T(8,128)(2,1)} %get-tuple-element.60), channel_id=1, source_target_pairs={{0,4},{1,5},{2,6},{3,7},{4,0},{5,1},{6,2},{7,3},{8,12},{9,13},{10,... | collective-permute-start | bytes 1572872 | tf_op jit(solution)/shard_map/ppermute | solution.py:40
  19.2 2.0 %pages.1 = (bf16[2,64,576]{2,1,0:T(8,128)(2,1)S(1)}, s32[1]{0:T(128)}) custom-call(s32[8]{0:T(128)S(1)} %bitcast.2, s32[1]{0:T(128)S(6)} %copy.16.request_ref, s32[1]{0:T(128)S(6)} %copy.17.count_ref, bf16[16,192,576]{2,1,0:T(8,128)(2,1)} %cache_ref.3), custom_call_target="tpu_custom_call" | custom-call | flops 1000 | bytes 400000 | tf_op jit(solution)/shard_map/pages/pallas_call | solution.py:450
  21.3 1.7 %collective-permute-start.6 = (bf16[2,64,576]{2,1,0:T(8,128)(2,1)S(1)}, bf16[2,64,576]{2,1,0:T(8,128)(2,1)S(1)}, u32[]{:S(2)}, u32[]{:S(2)}) collective-permute-start(bf16[2,64,576]{2,1,0:T(8,128)(2,1)S(1)} %get-tuple-element.67.mine_ref), channel_id=1, source_target_pairs={{0,16},{16,0},{32,48},{48,32},{64,80},{80,64},{96,112},{112,96},{1... | collective-permute-start | bytes 442376 | tf_op jit(solution)/shard_map/ppermute | solution.py:484
  23.0 6.3 %hold_projection.1 = (bf16[16,512,128]{2,1,0:T(8,128)(2,1)S(1)}, bf16[2048,3584]{1,0:T(8,128)(2,1)S(1)}) custom-call(bf16[8,512,128]{2,1,0:T(8,128)(2,1)} %up_own.1, bf16[8,512,128]{2,1,0:T(8,128)(2,1)S(1)} %collective-permute-done.up_other, bf16[1024,3584]{1,0:T(8,128)(2,1)} %out_own.1, bf16[1024,3584]{1,0:T(8,128)(2,1)} %collective-permute-done.4.out_other), custom_call_target="tpu_custom_call" | custom-call | bytes 17000000 | tf_op jit(solution)/shard_map/hold_projection/pallas_call | solution.py:167
  29.3 0.9 collective-permute-done.2
  30.5 3.2 %collective-permute-start.8 = (bf16[32,16,512]{2,1,0:T(8,128)(2,1)S(1)}, bf16[32,16,512]{2,1,0:T(8,128)(2,1)S(1)}, u32[]{:S(2)}, u32[]{:S(2)}) collective-permute-start(bf16[32,16,512]{2,1,0:T(8,128)(2,1)S(1)} %copy-done.6), channel_id=1, source_target_pairs={{0,72},{1,73},{2,74},{3,75},{4,76},{5,77},{6,78},{7,79},{8,0},{9,1... | collective-permute-start | bytes 1572872 | tf_op jit(solution)/shard_map/ppermute | solution.py:40
  33.7 1.5 collective-permute-start.10
  35.2 1.7 %collective-permute-start.11 = (bf16[32,16,512]{2,1,0:T(8,128)(2,1)S(1)}, bf16[32,16,512]{2,1,0:T(8,128)(2,1)S(1)}, u32[]{:S(2)}, u32[]{:S(2)}) collective-permute-start(bf16[32,16,512]{2,1,0:T(8,128)(2,1)S(1)} %collective-permute-done.3), channel_id=1, source_target_pairs={{0,6},{1,7},{2,0},{3,1},{4,2},{5,3},{6,4},{7,5},{8,14},{9,15},{10,... | collective-permute-start | bytes 1572872 | tf_op jit(solution)/shard_map/ppermute | solution.py:40
  37.6 3.3 %collective-permute-start.12 = (bf16[2,64,576]{2,1,0:T(8,128)(2,1)S(1)}, bf16[2,64,576]{2,1,0:T(8,128)(2,1)S(1)}, u32[]{:S(2)}, u32[]{:S(2)}) collective-permute-start(bf16[2,64,576]{2,1,0:T(8,128)(2,1)S(1)} %pick.3.mine_ref), channel_id=1, source_target_pairs={{0,32},{16,48},{32,0},{48,16},{64,96},{80,112},{96,64},{112,80},{1... | collective-permute-start | bytes 442376 | tf_op jit(solution)/shard_map/ppermute | solution.py:484
  40.9 3.6 %collective-permute-done.12.other_ref = bf16[2,64,576]{2,1,0:T(8,128)(2,1)S(1)} collective-permute-done((bf16[2,64,576]{2,1,0:T(8,128)(2,1)S(1)}, bf16[2,64,576]{2,1,0:T(8,128)(2,1)S(1)}, u32[]{:S(2)}, u32[]{:S(2)}) %collective-permute-start.12) | collective-permute-done | bytes 147488 | tf_op jit(solution)/shard_map/ppermute | solution.py:484
  45.4 2.0 %collective-permute-done.10.refs_1_ = bf16[32,16,512]{2,1,0:T(8,128)(2,1)S(1)} collective-permute-done((bf16[32,16,512]{2,1,0:T(8,128)(2,1)S(1)}, bf16[32,16,512]{2,1,0:T(8,128)(2,1)S(1)}, u32[]{:S(2)}, u32[]{:S(2)}) %collective-permute-start.10) | collective-permute-done | bytes 524320 | tf_op jit(solution)/shard_map/ppermute | solution.py:40
  48.0 2.6 %collective-permute-start.15 = (bf16[32,16,512]{2,1,0:T(8,128)(2,1)S(1)}, bf16[32,16,512]{2,1,0:T(8,128)(2,1)S(1)}, u32[]{:S(2)}, u32[]{:S(2)}) collective-permute-start(bf16[32,16,512]{2,1,0:T(8,128)(2,1)S(1)} %collective-permute-done.8), channel_id=1, source_target_pairs={{0,4},{1,5},{2,6},{3,7},{4,0},{5,1},{6,2},{7,3},{8,12},{9,13},{10,... | collective-permute-start | bytes 1572872 | tf_op jit(solution)/shard_map/ppermute | solution.py:40
  50.7 1.1 collective-permute-start.9
  51.8 2.2 %collective-permute-start.17 = (bf16[32,16,512]{2,1,0:T(8,128)(2,1)S(1)}, bf16[32,16,512]{2,1,0:T(8,128)(2,1)S(1)}, u32[]{:S(2)}, u32[]{:S(2)}) collective-permute-start(bf16[32,16,512]{2,1,0:T(8,128)(2,1)S(1)} %copy-done.4), channel_id=1, source_target_pairs={{0,6},{1,7},{2,0},{3,1},{4,2},{5,3},{6,4},{7,5},{8,14},{9,15},{10,... | collective-permute-start | bytes 1572872 | tf_op jit(solution)/shard_map/ppermute | solution.py:40
  53.9 1.5 %values.4.refs_0_.refs_2_ = bf16[64,2048]{1,0:T(8,128)(2,1)S(1)} custom-call(bf16[32,16,512]{2,1,0:T(8,128)(2,1)S(1)} %copy-done, bf16[32,16,512]{2,1,0:T(8,128)(2,1)S(1)} %collective-permute-done.1.refs_1_, bf16[16,512,128]{2,1,0:T(8,128)(2,1)S(1)} %get-tuple-element.73.refs_2_), custom_call_target="tpu_custom_call" | custom-call | flops 134217728 | bytes 4000000 | tf_op jit(solution)/shard_map/values/pallas_call | solution.py:236
  55.5 1.5 %values.5.refs_0_ = bf16[64,2048]{1,0:T(8,128)(2,1)S(1)} custom-call(bf16[32,16,512]{2,1,0:T(8,128)(2,1)S(1)} %collective-permute-done.7.refs_0_, bf16[32,16,512]{2,1,0:T(8,128)(2,1)S(1)} %collective-permute-done.10.refs_1_, bf16[16,512,128]{2,1,0:T(8,128)(2,1)S(1)} %get-tuple-element.73.refs_2_), custom_call_target="tpu_custom_call" | custom-call | flops 134217728 | bytes 4000000 | tf_op jit(solution)/shard_map/values/pallas_call | solution.py:236
  57.0 7.4 %collective-permute-done.15.refs_0_ = bf16[32,16,512]{2,1,0:T(8,128)(2,1)S(1)} collective-permute-done((bf16[32,16,512]{2,1,0:T(8,128)(2,1)S(1)}, bf16[32,16,512]{2,1,0:T(8,128)(2,1)S(1)}, u32[]{:S(2)}, u32[]{:S(2)}) %collective-permute-start.15) | collective-permute-done | bytes 524320 | tf_op jit(solution)/shard_map/ppermute | solution.py:40
  64.4 1.1 collective-permute-start.16
  65.5 1.5 %values.6.refs_1_ = bf16[64,2048]{1,0:T(8,128)(2,1)S(1)} custom-call(bf16[32,16,512]{2,1,0:T(8,128)(2,1)S(1)} %collective-permute-done.15.refs_0_, bf16[32,16,512]{2,1,0:T(8,128)(2,1)S(1)} %collective-permute-done.11.refs_1_, bf16[16,512,128]{2,1,0:T(8,128)(2,1)S(1)} %get-tuple-element.73.refs_2_), custom_call_target="tpu_custom_call" | custom-call | flops 134217728 | bytes 4000000 | tf_op jit(solution)/shard_map/values/pallas_call | solution.py:236
  67.1 3.2 %project.2 = (bf16[32,3584]{1,0:T(8,128)(2,1)S(1)}, bf16[32,3584]{1,0:T(8,128)(2,1)S(1)}, bf16[32,3584]{1,0:T(8,128)(2,1)S(1)}, bf16[32,3584]{1,0:T(8,128)(2,1)S(1)}) custom-call(bf16[64,2048]{1,0:T(8,128)(2,1)S(1)} %values.5.refs_0_, bf16[64,2048]{1,0:T(8,128)(2,1)S(1)} %values.6.refs_1_, bf16[2048,3584]{1,0:T(8,128)(2,1)S(1)} %get-tuple-element.65.refs_2_.refs_4_), custom_call_target="tpu_custom_call" | custom-call | flops 1879048192 | bytes 17000000 | tf_op jit(solution)/shard_map/project/pallas_call | solution.py:279
  70.3 0.9 collective-permute-start.18
  71.2 1.4 collective-permute-start.19
  72.6 2.6 %collective-permute-start.21 = (bf16[32,3584]{1,0:T(8,128)(2,1)S(1)}, bf16[32,3584]{1,0:T(8,128)(2,1)S(1)}, u32[]{:S(2)}, u32[]{:S(2)}) collective-permute-start(bf16[32,3584]{1,0:T(8,128)(2,1)S(1)} %get-tuple-element.97), channel_id=1, source_target_pairs={{0,4},{1,5},{2,6},{3,7},{4,0},{5,1},{6,2},{7,3},{8,12},{9,13},{10,... | collective-permute-start | bytes 688136 | tf_op jit(solution)/shard_map/ppermute | solution.py:40
  75.2 1.3 pick.5
  76.6 1.5 %values.7.refs_1_.refs_3_ = bf16[64,2048]{1,0:T(8,128)(2,1)S(1)} custom-call(bf16[32,16,512]{2,1,0:T(8,128)(2,1)S(1)} %collective-permute-done.9.refs_0_, bf16[32,16,512]{2,1,0:T(8,128)(2,1)S(1)} %collective-permute-done.17.refs_1_, bf16[16,512,128]{2,1,0:T(8,128)(2,1)S(1)} %get-tuple-element.73.refs_2_), custom_call_target="tpu_custom_call" | custom-call | flops 134217728 | bytes 4000000 | tf_op jit(solution)/shard_map/values/pallas_call | solution.py:236
  78.1 3.2 %project.3 = (f32[32,3584]{1,0:T(8,128)S(1)}, f32[32,3584]{1,0:T(8,128)S(1)}, bf16[32,3584]{1,0:T(8,128)(2,1)S(1)}, f32[32,3584]{1,0:T(8,128)S(1)}) custom-call(bf16[64,2048]{1,0:T(8,128)(2,1)S(1)} %values.4.refs_0_.refs_2_, bf16[64,2048]{1,0:T(8,128)(2,1)S(1)} %values.7.refs_1_.refs_3_, bf16[64,2048]{1,0:T(8,128)(2,1)S(1)} %values.4.refs_0_.refs_2_, ...), custom_call_target="tpu_custom_call" | custom-call | flops 1879048192 | bytes 17000000 | tf_op jit(solution)/shard_map/project/pallas_call | solution.py:279
  81.3 1.0 collective-permute-start.24
  82.4 2.9 %collective-permute-start.23 = (bf16[32,3584]{1,0:T(8,128)(2,1)S(1)}, bf16[32,3584]{1,0:T(8,128)(2,1)S(1)}, u32[]{:S(2)}, u32[]{:S(2)}) collective-permute-start(bf16[32,3584]{1,0:T(8,128)(2,1)S(1)} %fold.4), channel_id=1, source_target_pairs={{0,6},{1,7},{2,0},{3,1},{4,2},{5,3},{6,4},{7,5},{8,14},{9,15},{10,... | collective-permute-start | bytes 688136 | tf_op jit(solution)/shard_map/ppermute | solution.py:40
  85.5 2.0 %collective-permute-start.20 = (bf16[32,3584]{1,0:T(8,128)(2,1)S(1)}, bf16[32,3584]{1,0:T(8,128)(2,1)S(1)}, u32[]{:S(2)}, u32[]{:S(2)}) collective-permute-start(bf16[32,3584]{1,0:T(8,128)(2,1)S(1)} %get-tuple-element.96), channel_id=1, source_target_pairs={{0,72},{1,73},{2,74},{3,75},{4,76},{5,77},{6,78},{7,79},{8,0},{9,1... | collective-permute-start | bytes 688136 | tf_op jit(solution)/shard_map/ppermute | solution.py:40
  87.7 8.3 %hold_feed.1 = (bf16[5,3584,256]{2,1,0:T(8,128)(2,1)S(1)}, bf16[5,3584,256]{2,1,0:T(8,128)(2,1)S(1)}, bf16[1280,3584]{1,0:T(8,128)(2,1)S(1)}) custom-call(bf16[3584,640]{1,0:T(8,128)(2,1)} %g0, bf16[3584,640]{1,0:T(8,128)(2,1)} %collective-permute-done.5.g1, bf16[3584,640]{1,0:T(8,128)(2,1)} %u0.1, bf16[3584,640]{1,0:T(8,128)(2,1)S(1)} %collective-permute-done.13.u1, ...), custom_call_target="tpu_custom_call" | custom-call | bytes 27500000 | tf_op jit(solution)/shard_map/hold_feed/pallas_call | solution.py:198
  96.5 3.2 %collective-permute-start.31 = (bf16[32,3584]{1,0:T(8,128)(2,1)S(1)}, bf16[32,3584]{1,0:T(8,128)(2,1)S(1)}, u32[]{:S(2)}, u32[]{:S(2)}) collective-permute-start(bf16[32,3584]{1,0:T(8,128)(2,1)S(1)} %get-tuple-element.103.refs_0_), channel_id=1, source_target_pairs={{0,72},{1,73},{2,74},{3,75},{4,76},{5,77},{6,78},{7,79},{8,0},{9,1... | collective-permute-start | bytes 688136 | tf_op jit(solution)/shard_map/ppermute | solution.py:40
  99.6 3.2 %collective-permute-start.28 = (bf16[32,3584]{1,0:T(8,128)(2,1)S(1)}, bf16[32,3584]{1,0:T(8,128)(2,1)S(1)}, u32[]{:S(2)}, u32[]{:S(2)}) collective-permute-start(bf16[32,3584]{1,0:T(8,128)(2,1)S(1)} %get-tuple-element.103.refs_0_), channel_id=1, source_target_pairs={{0,6},{1,7},{2,0},{3,1},{4,2},{5,3},{6,4},{7,5},{8,14},{9,15},{10,... | collective-permute-start | bytes 688136 | tf_op jit(solution)/shard_map/ppermute | solution.py:40
  102.8 1.5 collective-permute-start.27
  104.3 8.6 %collective-permute-done.28.refs_3_ = bf16[32,3584]{1,0:T(8,128)(2,1)S(1)} collective-permute-done((bf16[32,3584]{1,0:T(8,128)(2,1)S(1)}, bf16[32,3584]{1,0:T(8,128)(2,1)S(1)}, u32[]{:S(2)}, u32[]{:S(2)}) %collective-permute-start.28) | collective-permute-done | bytes 229408 | tf_op jit(solution)/shard_map/ppermute | solution.py:40
  113.2 1.8 %collective-permute-done.26.refs_1_ = bf16[32,3584]{1,0:T(8,128)(2,1)S(1)} collective-permute-done((bf16[32,3584]{1,0:T(8,128)(2,1)S(1)}, bf16[32,3584]{1,0:T(8,128)(2,1)S(1)}, u32[]{:S(2)}, u32[]{:S(2)}) %collective-permute-start.26) | collective-permute-done | bytes 229408 | tf_op jit(solution)/shard_map/ppermute | solution.py:40
  115.0 6.8 %feed.2 = (f32[32,3584]{1,0:T(8,128)S(1)}, f32[32,3584]{1,0:T(8,128)S(1)}, bf16[32,3584]{1,0:T(8,128)(2,1)S(1)}, f32[32,3584]{1,0:T(8,128)S(1)}) custom-call(bf16[32,3584]{1,0:T(8,128)(2,1)S(1)} %get-tuple-element.103.refs_0_, bf16[32,3584]{1,0:T(8,128)(2,1)S(1)} %collective-permute-done.26.refs_1_, bf16[32,3584]{1,0:T(8,128)(2,1)S(1)} %collective-permute-done.27.refs_2_, ...), custom_call_target="tpu_custom_call" | custom-call | flops 3523215360 | bytes 28000000 | tf_op jit(solution)/shard_map/feed/pallas_call | solution.py:324
  122.2 6.8 %feed.3 = (bf16[32,3584]{1,0:T(8,128)(2,1)S(1)}, bf16[32,3584]{1,0:T(8,128)(2,1)S(1)}, bf16[32,3584]{1,0:T(8,128)(2,1)S(1)}, bf16[32,3584]{1,0:T(8,128)(2,1)S(1)}) custom-call(bf16[32,3584]{1,0:T(8,128)(2,1)S(1)} %collective-permute-done.29.refs_0_, bf16[32,3584]{1,0:T(8,128)(2,1)S(1)} %collective-permute-done.30.refs_1_, ...), custom_call_target="tpu_custom_call" | custom-call | flops 3523215360 | bytes 28000000 | tf_op jit(solution)/shard_map/feed/pallas_call | solution.py:324
  129.0 2.9 %collective-permute-start.37 = (bf16[32,3584]{1,0:T(8,128)(2,1)S(1)}, bf16[32,3584]{1,0:T(8,128)(2,1)S(1)}, u32[]{:S(2)}, u32[]{:S(2)}) collective-permute-start(bf16[32,3584]{1,0:T(8,128)(2,1)S(1)} %get-tuple-element.112), channel_id=1, source_target_pairs={{0,72},{1,73},{2,74},{3,75},{4,76},{5,77},{6,78},{7,79},{8,0},{9,1... | collective-permute-start | bytes 688136 | tf_op jit(solution)/shard_map/ppermute | solution.py:40
  131.9 1.7 %collective-permute-start.35 = (bf16[32,3584]{1,0:T(8,128)(2,1)S(1)}, bf16[32,3584]{1,0:T(8,128)(2,1)S(1)}, u32[]{:S(2)}, u32[]{:S(2)}) collective-permute-start(bf16[32,3584]{1,0:T(8,128)(2,1)S(1)} %get-tuple-element.110), channel_id=1, source_target_pairs={{0,4},{1,5},{2,6},{3,7},{4,0},{5,1},{6,2},{7,3},{8,12},{9,13},{10,... | collective-permute-start | bytes 688136 | tf_op jit(solution)/shard_map/ppermute | solution.py:40
  134.2 1.2 collective-permute-start.39
  135.4 3.2 %collective-permute-start.34 = (bf16[32,3584]{1,0:T(8,128)(2,1)S(1)}, bf16[32,3584]{1,0:T(8,128)(2,1)S(1)}, u32[]{:S(2)}, u32[]{:S(2)}) collective-permute-start(bf16[32,3584]{1,0:T(8,128)(2,1)S(1)} %get-tuple-element.109), channel_id=1, source_target_pairs={{0,72},{1,73},{2,74},{3,75},{4,76},{5,77},{6,78},{7,79},{8,0},{9,1... | collective-permute-start | bytes 688136 | tf_op jit(solution)/shard_map/ppermute | solution.py:40
  138.7 1.9 %collective-permute-start.38 = (bf16[32,3584]{1,0:T(8,128)(2,1)S(1)}, bf16[32,3584]{1,0:T(8,128)(2,1)S(1)}, u32[]{:S(2)}, u32[]{:S(2)}) collective-permute-start(bf16[32,3584]{1,0:T(8,128)(2,1)S(1)} %fold.6), channel_id=1, source_target_pairs={{0,6},{1,7},{2,0},{3,1},{4,2},{5,3},{6,4},{7,5},{8,14},{9,15},{10,... | collective-permute-start | bytes 688136 | tf_op jit(solution)/shard_map/ppermute | solution.py:40
  141.6 1.2 collective-permute-start.41
  142.8 1.1 collective-permute-done.39.refs_3_
  144.0 4.8 %collective-permute-done.36.refs_1_ = bf16[32,3584]{1,0:T(8,128)(2,1)S(1)} collective-permute-done((bf16[32,3584]{1,0:T(8,128)(2,1)S(1)}, bf16[32,3584]{1,0:T(8,128)(2,1)S(1)}, u32[]{:S(2)}, u32[]{:S(2)}) %collective-permute-start.36) | collective-permute-done | bytes 229408 | tf_op jit(solution)/shard_map/ppermute | solution.py:40
  (86 shorter events, 7.6 us)
Async XLA Ops:
  0.6 20.6 %collective-permute-start.4 = (bf16[1024,3584]{1,0:T(8,128)(2,1)}, bf16[1024,3584]{1,0:T(8,128)(2,1)}, u32[]{:S(2)}, u32[]{:S(2)}) collective-permute-start(bf16[1024,3584]{1,0:T(8,128)(2,1)} %out_own.1), channel_id=1, source_target_pairs={{0,1},{1,0},{2,3},{3,2},{4,5},{5,4},{6,7},{7,6},{8,9},{9,8},{10,11... | collective-permute-start | bytes 22020104 | tf_op jit(solution)/shard_map/ppermute | solution.py:44
  0.7 29.7 %collective-permute-start.5 = (bf16[3584,640]{1,0:T(8,128)(2,1)}, bf16[3584,640]{1,0:T(8,128)(2,1)}, u32[]{:S(2)}, u32[]{:S(2)}) collective-permute-start(bf16[3584,640]{1,0:T(8,128)(2,1)} %g0), channel_id=1, source_target_pairs={{0,1},{1,0},{2,3},{3,2},{4,5},{5,4},{6,7},{7,6},{8,9},{9,8},{10,11... | collective-permute-start | bytes 13762568 | tf_op jit(solution)/shard_map/ppermute | solution.py:44
  1.2 9.5 %collective-permute-start = (bf16[8,512,128]{2,1,0:T(8,128)(2,1)}, bf16[8,512,128]{2,1,0:T(8,128)(2,1)S(1)}, u32[]{:S(2)}, u32[]{:S(2)}) collective-permute-start(bf16[8,512,128]{2,1,0:T(8,128)(2,1)} %up_own.1), channel_id=1, source_target_pairs={{0,1},{1,0},{2,3},{3,2},{4,5},{5,4},{6,7},{7,6},{8,9},{9,8},{10,11... | collective-permute-start | bytes 3145736 | tf_op jit(solution)/shard_map/ppermute | solution.py:44
  10.7 18.6 %collective-permute-start.3 = (bf16[32,16,512]{2,1,0:T(8,128)(2,1)}, bf16[32,16,512]{2,1,0:T(8,128)(2,1)S(1)}, u32[]{:S(2)}, u32[]{:S(2)}) collective-permute-start(bf16[32,16,512]{2,1,0:T(8,128)(2,1)} %get-tuple-element.64), channel_id=1, source_target_pairs={{0,72},{1,73},{2,74},{3,75},{4,76},{5,77},{6,78},{7,79},{8,0},{9,1... | collective-permute-start | bytes 1572872 | tf_op jit(solution)/shard_map/ppermute | solution.py:40
  14.8 15.3 %collective-permute-start.2 = (bf16[32,16,512]{2,1,0:T(8,128)(2,1)}, bf16[32,16,512]{2,1,0:T(8,128)(2,1)S(1)}, u32[]{:S(2)}, u32[]{:S(2)}) collective-permute-start(bf16[32,16,512]{2,1,0:T(8,128)(2,1)} %get-tuple-element.62), channel_id=1, source_target_pairs={{0,8},{1,9},{2,10},{3,11},{4,12},{5,13},{6,14},{7,15},{8,64},{9,65... | collective-permute-start | bytes 1572872 | tf_op jit(solution)/shard_map/ppermute | solution.py:40
  14.8 15.6 %collective-permute-start.1 = (bf16[32,16,512]{2,1,0:T(8,128)(2,1)}, bf16[32,16,512]{2,1,0:T(8,128)(2,1)S(1)}, u32[]{:S(2)}, u32[]{:S(2)}) collective-permute-start(bf16[32,16,512]{2,1,0:T(8,128)(2,1)} %get-tuple-element.60), channel_id=1, source_target_pairs={{0,4},{1,5},{2,6},{3,7},{4,0},{5,1},{6,2},{7,3},{8,12},{9,13},{10,... | collective-permute-start | bytes 1572872 | tf_op jit(solution)/shard_map/ppermute | solution.py:40
  21.2 26.2 %slice-start = ((s8[4587520]{0:T(1024)(128)(4,1)}), s8[4194304]{0:T(1024)(128)(4,1)S(1)}, s32[]{:S(2)}) async-start(s8[4587520]{0:T(1024)(128)(4,1)} %bitcast.4), calls=%async_computation | async-start | bytes 8388608
  21.2 26.3 %slice-start.2 = ((s8[4587520]{0:T(1024)(128)(4,1)}), s8[4194304]{0:T(1024)(128)(4,1)S(1)}, s32[]{:S(2)}) async-start(s8[4587520]{0:T(1024)(128)(4,1)} %bitcast.6), calls=%async_computation.2 | async-start | bytes 8388608
  21.3 26.3 %slice-start.3 = ((s8[4587520]{0:T(1024)(128)(4,1)}), s8[393216]{0:T(1024)(128)(4,1)S(1)}, s32[]{:S(2)}) async-start(s8[4587520]{0:T(1024)(128)(4,1)} %bitcast.6), calls=%async_computation.3 | async-start | bytes 786432
  21.3 29.4 %copy-start.5 = (bf16[32,16,512]{2,1,0:T(8,128)(2,1)S(1)}, bf16[32,16,512]{2,1,0:T(8,128)(2,1)}, u32[]{:S(2)}) copy-start(bf16[32,16,512]{2,1,0:T(8,128)(2,1)} %get-tuple-element.77) | copy-start | bytes 1572868
  21.3 30.5 %copy-start.4 = (bf16[32,16,512]{2,1,0:T(8,128)(2,1)S(1)}, bf16[32,16,512]{2,1,0:T(8,128)(2,1)}, u32[]{:S(2)}) copy-start(bf16[32,16,512]{2,1,0:T(8,128)(2,1)} %get-tuple-element.90) | copy-start | bytes 1572868
  21.3 32.6 %copy-start = (bf16[32,16,512]{2,1,0:T(8,128)(2,1)S(1)}, bf16[32,16,512]{2,1,0:T(8,128)(2,1)}, u32[]{:S(2)}) copy-start(bf16[32,16,512]{2,1,0:T(8,128)(2,1)} %get-tuple-element.72.refs_0_) | copy-start | bytes 1572868
  21.3 8.0 %collective-permute-start.6 = (bf16[2,64,576]{2,1,0:T(8,128)(2,1)S(1)}, bf16[2,64,576]{2,1,0:T(8,128)(2,1)S(1)}, u32[]{:S(2)}, u32[]{:S(2)}) collective-permute-start(bf16[2,64,576]{2,1,0:T(8,128)(2,1)S(1)} %get-tuple-element.67.mine_ref), channel_id=1, source_target_pairs={{0,16},{16,0},{32,48},{48,32},{64,80},{80,64},{96,112},{112,96},{1... | collective-permute-start | bytes 442376 | tf_op jit(solution)/shard_map/ppermute | solution.py:484
  30.5 14.3 %collective-permute-start.7 = (bf16[32,16,512]{2,1,0:T(8,128)(2,1)S(1)}, bf16[32,16,512]{2,1,0:T(8,128)(2,1)S(1)}, u32[]{:S(2)}, u32[]{:S(2)}) collective-permute-start(bf16[32,16,512]{2,1,0:T(8,128)(2,1)S(1)} %copy-done.7), channel_id=1, source_target_pairs={{0,8},{1,9},{2,10},{3,11},{4,12},{5,13},{6,14},{7,15},{8,64},{9,65... | collective-permute-start | bytes 1572872 | tf_op jit(solution)/shard_map/ppermute | solution.py:40
  30.5 14.3 %collective-permute-start.8 = (bf16[32,16,512]{2,1,0:T(8,128)(2,1)S(1)}, bf16[32,16,512]{2,1,0:T(8,128)(2,1)S(1)}, u32[]{:S(2)}, u32[]{:S(2)}) collective-permute-start(bf16[32,16,512]{2,1,0:T(8,128)(2,1)S(1)} %copy-done.6), channel_id=1, source_target_pairs={{0,72},{1,73},{2,74},{3,75},{4,76},{5,77},{6,78},{7,79},{8,0},{9,1... | collective-permute-start | bytes 1572872 | tf_op jit(solution)/shard_map/ppermute | solution.py:40
  33.7 13.7 %collective-permute-start.10 = (bf16[32,16,512]{2,1,0:T(8,128)(2,1)S(1)}, bf16[32,16,512]{2,1,0:T(8,128)(2,1)S(1)}, u32[]{:S(2)}, u32[]{:S(2)}) collective-permute-start(bf16[32,16,512]{2,1,0:T(8,128)(2,1)S(1)} %collective-permute-done.2), channel_id=1, source_target_pairs={{0,2},{1,3},{2,4},{3,5},{4,6},{5,7},{6,0},{7,1},{8,10},{9,11},{10,... | collective-permute-start | bytes 1572872 | tf_op jit(solution)/shard_map/ppermute | solution.py:40
  35.2 12.2 %collective-permute-start.11 = (bf16[32,16,512]{2,1,0:T(8,128)(2,1)S(1)}, bf16[32,16,512]{2,1,0:T(8,128)(2,1)S(1)}, u32[]{:S(2)}, u32[]{:S(2)}) collective-permute-start(bf16[32,16,512]{2,1,0:T(8,128)(2,1)S(1)} %collective-permute-done.3), channel_id=1, source_target_pairs={{0,6},{1,7},{2,0},{3,1},{4,2},{5,3},{6,4},{7,5},{8,14},{9,15},{10,... | collective-permute-start | bytes 1572872 | tf_op jit(solution)/shard_map/ppermute | solution.py:40
  37.6 6.9 %collective-permute-start.12 = (bf16[2,64,576]{2,1,0:T(8,128)(2,1)S(1)}, bf16[2,64,576]{2,1,0:T(8,128)(2,1)S(1)}, u32[]{:S(2)}, u32[]{:S(2)}) collective-permute-start(bf16[2,64,576]{2,1,0:T(8,128)(2,1)S(1)} %pick.3.mine_ref), channel_id=1, source_target_pairs={{0,32},{16,48},{32,0},{48,16},{64,96},{80,112},{96,64},{112,80},{1... | collective-permute-start | bytes 442376 | tf_op jit(solution)/shard_map/ppermute | solution.py:484
  47.5 19.6 %collective-permute-start.13 = (bf16[3584,640]{1,0:T(8,128)(2,1)S(1)}, bf16[3584,640]{1,0:T(8,128)(2,1)S(1)}, u32[]{:S(2)}, u32[]{:S(2)}) collective-permute-start(bf16[3584,640]{1,0:T(8,128)(2,1)S(1)} %bitcast.5), channel_id=1, source_target_pairs={{0,1},{1,0},{2,3},{3,2},{4,5},{5,4},{6,7},{7,6},{8,9},{9,8},{10,11... | collective-permute-start | bytes 13762568 | tf_op jit(solution)/shard_map/ppermute | solution.py:44
  47.6 19.5 %collective-permute-start.14 = (bf16[640,3584]{1,0:T(8,128)(2,1)S(1)}, bf16[640,3584]{1,0:T(8,128)(2,1)}, u32[]{:S(2)}, u32[]{:S(2)}) collective-permute-start(bf16[640,3584]{1,0:T(8,128)(2,1)S(1)} %bitcast.7), channel_id=1, source_target_pairs={{0,1},{1,0},{2,3},{3,2},{4,5},{5,4},{6,7},{7,6},{8,9},{9,8},{10,11... | collective-permute-start | bytes 13762568 | tf_op jit(solution)/shard_map/ppermute | solution.py:44
  48.0 16.3 %collective-permute-start.15 = (bf16[32,16,512]{2,1,0:T(8,128)(2,1)S(1)}, bf16[32,16,512]{2,1,0:T(8,128)(2,1)S(1)}, u32[]{:S(2)}, u32[]{:S(2)}) collective-permute-start(bf16[32,16,512]{2,1,0:T(8,128)(2,1)S(1)} %collective-permute-done.8), channel_id=1, source_target_pairs={{0,4},{1,5},{2,6},{3,7},{4,0},{5,1},{6,2},{7,3},{8,12},{9,13},{10,... | collective-permute-start | bytes 1572872 | tf_op jit(solution)/shard_map/ppermute | solution.py:40
  50.7 25.9 %collective-permute-start.9 = (bf16[32,16,512]{2,1,0:T(8,128)(2,1)S(1)}, bf16[32,16,512]{2,1,0:T(8,128)(2,1)S(1)}, u32[]{:S(2)}, u32[]{:S(2)}) collective-permute-start(bf16[32,16,512]{2,1,0:T(8,128)(2,1)S(1)} %copy-done.5), channel_id=1, source_target_pairs={{0,2},{1,3},{2,4},{3,5},{4,6},{5,7},{6,0},{7,1},{8,10},{9,11},{10,... | collective-permute-start | bytes 1572872 | tf_op jit(solution)/shard_map/ppermute | solution.py:40
  51.8 24.8 %collective-permute-start.17 = (bf16[32,16,512]{2,1,0:T(8,128)(2,1)S(1)}, bf16[32,16,512]{2,1,0:T(8,128)(2,1)S(1)}, u32[]{:S(2)}, u32[]{:S(2)}) collective-permute-start(bf16[32,16,512]{2,1,0:T(8,128)(2,1)S(1)} %copy-done.4), channel_id=1, source_target_pairs={{0,6},{1,7},{2,0},{3,1},{4,2},{5,3},{6,4},{7,5},{8,14},{9,15},{10,... | collective-permute-start | bytes 1572872 | tf_op jit(solution)/shard_map/ppermute | solution.py:40
  64.4 8.2 %collective-permute-start.16 = (bf16[2,64,576]{2,1,0:T(8,128)(2,1)S(1)}, bf16[2,64,576]{2,1,0:T(8,128)(2,1)S(1)}, u32[]{:S(2)}, u32[]{:S(2)}) collective-permute-start(bf16[2,64,576]{2,1,0:T(8,128)(2,1)S(1)} %pick.4.mine_ref), channel_id=1, source_target_pairs={{0,64},{16,80},{32,96},{48,112},{64,0},{80,16},{96,32},{112,48},{1... | collective-permute-start | bytes 442376 | tf_op jit(solution)/shard_map/ppermute | solution.py:484
  70.3 12.0 %collective-permute-start.18 = (bf16[32,3584]{1,0:T(8,128)(2,1)S(1)}, bf16[32,3584]{1,0:T(8,128)(2,1)S(1)}, u32[]{:S(2)}, u32[]{:S(2)}) collective-permute-start(bf16[32,3584]{1,0:T(8,128)(2,1)S(1)} %get-tuple-element.93), channel_id=1, source_target_pairs={{0,72},{1,73},{2,74},{3,75},{4,76},{5,77},{6,78},{7,79},{8,0},{9,1... | collective-permute-start | bytes 688136 | tf_op jit(solution)/shard_map/ppermute | solution.py:40
  71.2 14.1 %collective-permute-start.19 = (bf16[32,3584]{1,0:T(8,128)(2,1)S(1)}, bf16[32,3584]{1,0:T(8,128)(2,1)S(1)}, u32[]{:S(2)}, u32[]{:S(2)}) collective-permute-start(bf16[32,3584]{1,0:T(8,128)(2,1)S(1)} %get-tuple-element.95), channel_id=1, source_target_pairs={{0,8},{1,9},{2,10},{3,11},{4,12},{5,13},{6,14},{7,15},{8,64},{9,65... | collective-permute-start | bytes 688136 | tf_op jit(solution)/shard_map/ppermute | solution.py:40
  72.6 14.9 %collective-permute-start.21 = (bf16[32,3584]{1,0:T(8,128)(2,1)S(1)}, bf16[32,3584]{1,0:T(8,128)(2,1)S(1)}, u32[]{:S(2)}, u32[]{:S(2)}) collective-permute-start(bf16[32,3584]{1,0:T(8,128)(2,1)S(1)} %get-tuple-element.97), channel_id=1, source_target_pairs={{0,4},{1,5},{2,6},{3,7},{4,0},{5,1},{6,2},{7,3},{8,12},{9,13},{10,... | collective-permute-start | bytes 688136 | tf_op jit(solution)/shard_map/ppermute | solution.py:40
  81.3 14.7 %collective-permute-start.24 = (bf16[32,3584]{1,0:T(8,128)(2,1)S(1)}, bf16[32,3584]{1,0:T(8,128)(2,1)S(1)}, u32[]{:S(2)}, u32[]{:S(2)}) collective-permute-start(bf16[32,3584]{1,0:T(8,128)(2,1)S(1)} %get-tuple-element.101), channel_id=1, source_target_pairs={{0,4},{1,5},{2,6},{3,7},{4,0},{5,1},{6,2},{7,3},{8,12},{9,13},{10,... | collective-permute-start | bytes 688136 | tf_op jit(solution)/shard_map/ppermute | solution.py:40
  82.4 13.6 %collective-permute-start.23 = (bf16[32,3584]{1,0:T(8,128)(2,1)S(1)}, bf16[32,3584]{1,0:T(8,128)(2,1)S(1)}, u32[]{:S(2)}, u32[]{:S(2)}) collective-permute-start(bf16[32,3584]{1,0:T(8,128)(2,1)S(1)} %fold.4), channel_id=1, source_target_pairs={{0,6},{1,7},{2,0},{3,1},{4,2},{5,3},{6,4},{7,5},{8,14},{9,15},{10,... | collective-permute-start | bytes 688136 | tf_op jit(solution)/shard_map/ppermute | solution.py:40
  85.4 10.7 %collective-permute-start.25 = (bf16[32,3584]{1,0:T(8,128)(2,1)S(1)}, bf16[32,3584]{1,0:T(8,128)(2,1)S(1)}, u32[]{:S(2)}, u32[]{:S(2)}) collective-permute-start(bf16[32,3584]{1,0:T(8,128)(2,1)S(1)} %fold.5), channel_id=1, source_target_pairs={{0,2},{1,3},{2,4},{3,5},{4,6},{5,7},{6,0},{7,1},{8,10},{9,11},{10,... | collective-permute-start | bytes 688136 | tf_op jit(solution)/shard_map/ppermute | solution.py:40
  85.5 10.6 %collective-permute-start.20 = (bf16[32,3584]{1,0:T(8,128)(2,1)S(1)}, bf16[32,3584]{1,0:T(8,128)(2,1)S(1)}, u32[]{:S(2)}, u32[]{:S(2)}) collective-permute-start(bf16[32,3584]{1,0:T(8,128)(2,1)S(1)} %get-tuple-element.96), channel_id=1, source_target_pairs={{0,72},{1,73},{2,74},{3,75},{4,76},{5,77},{6,78},{7,79},{8,0},{9,1... | collective-permute-start | bytes 688136 | tf_op jit(solution)/shard_map/ppermute | solution.py:40
  87.4 8.6 %collective-permute-start.22 = (bf16[32,3584]{1,0:T(8,128)(2,1)S(1)}, bf16[32,3584]{1,0:T(8,128)(2,1)S(1)}, u32[]{:S(2)}, u32[]{:S(2)}) collective-permute-start(bf16[32,3584]{1,0:T(8,128)(2,1)S(1)} %collective-permute-done.21), channel_id=1, source_target_pairs={{0,8},{1,9},{2,10},{3,11},{4,12},{5,13},{6,14},{7,15},{8,64},{9,65... | collective-permute-start | bytes 688136 | tf_op jit(solution)/shard_map/ppermute | solution.py:40
  96.5 7.8 %collective-permute-start.31 = (bf16[32,3584]{1,0:T(8,128)(2,1)S(1)}, bf16[32,3584]{1,0:T(8,128)(2,1)S(1)}, u32[]{:S(2)}, u32[]{:S(2)}) collective-permute-start(bf16[32,3584]{1,0:T(8,128)(2,1)S(1)} %get-tuple-element.103.refs_0_), channel_id=1, source_target_pairs={{0,72},{1,73},{2,74},{3,75},{4,76},{5,77},{6,78},{7,79},{8,0},{9,1... | collective-permute-start | bytes 688136 | tf_op jit(solution)/shard_map/ppermute | solution.py:40
  99.6 13.3 %collective-permute-start.28 = (bf16[32,3584]{1,0:T(8,128)(2,1)S(1)}, bf16[32,3584]{1,0:T(8,128)(2,1)S(1)}, u32[]{:S(2)}, u32[]{:S(2)}) collective-permute-start(bf16[32,3584]{1,0:T(8,128)(2,1)S(1)} %get-tuple-element.103.refs_0_), channel_id=1, source_target_pairs={{0,6},{1,7},{2,0},{3,1},{4,2},{5,3},{6,4},{7,5},{8,14},{9,15},{10,... | collective-permute-start | bytes 688136 | tf_op jit(solution)/shard_map/ppermute | solution.py:40
  102.8 12.2 %collective-permute-start.26 = (bf16[32,3584]{1,0:T(8,128)(2,1)S(1)}, bf16[32,3584]{1,0:T(8,128)(2,1)S(1)}, u32[]{:S(2)}, u32[]{:S(2)}) collective-permute-start(bf16[32,3584]{1,0:T(8,128)(2,1)S(1)} %get-tuple-element.103.refs_0_), channel_id=1, source_target_pairs={{0,2},{1,3},{2,4},{3,5},{4,6},{5,7},{6,0},{7,1},{8,10},{9,11},{10,... | collective-permute-start | bytes 688136 | tf_op jit(solution)/shard_map/ppermute | solution.py:40
  102.8 12.2 %collective-permute-start.27 = (bf16[32,3584]{1,0:T(8,128)(2,1)S(1)}, bf16[32,3584]{1,0:T(8,128)(2,1)S(1)}, u32[]{:S(2)}, u32[]{:S(2)}) collective-permute-start(bf16[32,3584]{1,0:T(8,128)(2,1)S(1)} %get-tuple-element.103.refs_0_), channel_id=1, source_target_pairs={{0,4},{1,5},{2,6},{3,7},{4,0},{5,1},{6,2},{7,3},{8,12},{9,13},{10,... | collective-permute-start | bytes 688136 | tf_op jit(solution)/shard_map/ppermute | solution.py:40
  104.3 17.5 %collective-permute-start.29 = (bf16[32,3584]{1,0:T(8,128)(2,1)S(1)}, bf16[32,3584]{1,0:T(8,128)(2,1)S(1)}, u32[]{:S(2)}, u32[]{:S(2)}) collective-permute-start(bf16[32,3584]{1,0:T(8,128)(2,1)S(1)} %get-tuple-element.103.refs_0_), channel_id=1, source_target_pairs={{0,8},{1,9},{2,10},{3,11},{4,12},{5,13},{6,14},{7,15},{8,64},{9,65... | collective-permute-start | bytes 688136 | tf_op jit(solution)/shard_map/ppermute | solution.py:40
  112.9 8.8 %collective-permute-start.32 = (bf16[32,3584]{1,0:T(8,128)(2,1)S(1)}, bf16[32,3584]{1,0:T(8,128)(2,1)S(1)}, u32[]{:S(2)}, u32[]{:S(2)}) collective-permute-start(bf16[32,3584]{1,0:T(8,128)(2,1)S(1)} %collective-permute-done.31), channel_id=1, source_target_pairs={{0,4},{1,5},{2,6},{3,7},{4,0},{5,1},{6,2},{7,3},{8,12},{9,13},{10,... | collective-permute-start | bytes 688136 | tf_op jit(solution)/shard_map/ppermute | solution.py:40
  112.9 8.8 %collective-permute-start.33 = (bf16[32,3584]{1,0:T(8,128)(2,1)S(1)}, bf16[32,3584]{1,0:T(8,128)(2,1)S(1)}, u32[]{:S(2)}, u32[]{:S(2)}) collective-permute-start(bf16[32,3584]{1,0:T(8,128)(2,1)S(1)} %collective-permute-done.28.refs_3_), channel_id=1, source_target_pairs={{0,72},{1,73},{2,74},{3,75},{4,76},{5,77},{6,78},{7,79},{8,0},{9,1... | collective-permute-start | bytes 688136 | tf_op jit(solution)/shard_map/ppermute | solution.py:40
  115.0 7.2 %collective-permute-start.30 = (bf16[32,3584]{1,0:T(8,128)(2,1)S(1)}, bf16[32,3584]{1,0:T(8,128)(2,1)S(1)}, u32[]{:S(2)}, u32[]{:S(2)}) collective-permute-start(bf16[32,3584]{1,0:T(8,128)(2,1)S(1)} %collective-permute-done.26.refs_1_), channel_id=1, source_target_pairs={{0,8},{1,9},{2,10},{3,11},{4,12},{5,13},{6,14},{7,15},{8,64},{9,65... | collective-permute-start | bytes 688136 | tf_op jit(solution)/shard_map/ppermute | solution.py:40
  129.0 9.7 %collective-permute-start.37 = (bf16[32,3584]{1,0:T(8,128)(2,1)S(1)}, bf16[32,3584]{1,0:T(8,128)(2,1)S(1)}, u32[]{:S(2)}, u32[]{:S(2)}) collective-permute-start(bf16[32,3584]{1,0:T(8,128)(2,1)S(1)} %get-tuple-element.112), channel_id=1, source_target_pairs={{0,72},{1,73},{2,74},{3,75},{4,76},{5,77},{6,78},{7,79},{8,0},{9,1... | collective-permute-start | bytes 688136 | tf_op jit(solution)/shard_map/ppermute | solution.py:40
  131.9 9.6 %collective-permute-start.35 = (bf16[32,3584]{1,0:T(8,128)(2,1)S(1)}, bf16[32,3584]{1,0:T(8,128)(2,1)S(1)}, u32[]{:S(2)}, u32[]{:S(2)}) collective-permute-start(bf16[32,3584]{1,0:T(8,128)(2,1)S(1)} %get-tuple-element.110), channel_id=1, source_target_pairs={{0,4},{1,5},{2,6},{3,7},{4,0},{5,1},{6,2},{7,3},{8,12},{9,13},{10,... | collective-permute-start | bytes 688136 | tf_op jit(solution)/shard_map/ppermute | solution.py:40
  133.6 7.9 %collective-permute-start.40 = (bf16[32,3584]{1,0:T(8,128)(2,1)S(1)}, bf16[32,3584]{1,0:T(8,128)(2,1)S(1)}, u32[]{:S(2)}, u32[]{:S(2)}) collective-permute-start(bf16[32,3584]{1,0:T(8,128)(2,1)S(1)} %get-tuple-element.115), channel_id=1, source_target_pairs={{0,8},{1,9},{2,10},{3,11},{4,12},{5,13},{6,14},{7,15},{8,64},{9,65... | collective-permute-start | bytes 688136 | tf_op jit(solution)/shard_map/ppermute | solution.py:40
  134.2 9.8 %collective-permute-start.39 = (bf16[32,3584]{1,0:T(8,128)(2,1)S(1)}, bf16[32,3584]{1,0:T(8,128)(2,1)S(1)}, u32[]{:S(2)}, u32[]{:S(2)}) collective-permute-start(bf16[32,3584]{1,0:T(8,128)(2,1)S(1)} %get-tuple-element.113), channel_id=1, source_target_pairs={{0,4},{1,5},{2,6},{3,7},{4,0},{5,1},{6,2},{7,3},{8,12},{9,13},{10,... | collective-permute-start | bytes 688136 | tf_op jit(solution)/shard_map/ppermute | solution.py:40
  135.4 8.6 %collective-permute-start.34 = (bf16[32,3584]{1,0:T(8,128)(2,1)S(1)}, bf16[32,3584]{1,0:T(8,128)(2,1)S(1)}, u32[]{:S(2)}, u32[]{:S(2)}) collective-permute-start(bf16[32,3584]{1,0:T(8,128)(2,1)S(1)} %get-tuple-element.109), channel_id=1, source_target_pairs={{0,72},{1,73},{2,74},{3,75},{4,76},{5,77},{6,78},{7,79},{8,0},{9,1... | collective-permute-start | bytes 688136 | tf_op jit(solution)/shard_map/ppermute | solution.py:40
  138.7 10.0 %collective-permute-start.38 = (bf16[32,3584]{1,0:T(8,128)(2,1)S(1)}, bf16[32,3584]{1,0:T(8,128)(2,1)S(1)}, u32[]{:S(2)}, u32[]{:S(2)}) collective-permute-start(bf16[32,3584]{1,0:T(8,128)(2,1)S(1)} %fold.6), channel_id=1, source_target_pairs={{0,6},{1,7},{2,0},{3,1},{4,2},{5,3},{6,4},{7,5},{8,14},{9,15},{10,... | collective-permute-start | bytes 688136 | tf_op jit(solution)/shard_map/ppermute | solution.py:40
  141.5 7.2 %collective-permute-start.36 = (bf16[32,3584]{1,0:T(8,128)(2,1)S(1)}, bf16[32,3584]{1,0:T(8,128)(2,1)S(1)}, u32[]{:S(2)}, u32[]{:S(2)}) collective-permute-start(bf16[32,3584]{1,0:T(8,128)(2,1)S(1)} %collective-permute-done.35), channel_id=1, source_target_pairs={{0,8},{1,9},{2,10},{3,11},{4,12},{5,13},{6,14},{7,15},{8,64},{9,65... | collective-permute-start | bytes 688136 | tf_op jit(solution)/shard_map/ppermute | solution.py:40
  141.6 7.3 %collective-permute-start.41 = (bf16[32,3584]{1,0:T(8,128)(2,1)S(1)}, bf16[32,3584]{1,0:T(8,128)(2,1)S(1)}, u32[]{:S(2)}, u32[]{:S(2)}) collective-permute-start(bf16[32,3584]{1,0:T(8,128)(2,1)S(1)} %fold.7), channel_id=1, source_target_pairs={{0,2},{1,3},{2,4},{3,5},{4,6},{5,7},{6,0},{7,1},{8,10},{9,11},{10,... | collective-permute-start | bytes 688136 | tf_op jit(solution)/shard_map/ppermute | solution.py:40
  (6 other events, 82.1 us)
